TPU v7x, 32 devices: a whole 2x2x4 slice. The times are simulated.
32 devices in a mesh: img: 4 (over y, x), ori: 8 (over z, core).
Axes of the slice: x: 2, y: 2, z: 4, core: 2. Of those that a mesh axis runs over, the one named last changes fastest.
Arguments:
- images: bfloat16 [8192, 2048], P(('img', 'ori')), may hold values from -128 to 128, as said below
- projections: bfloat16 [8192, 2048], P('ori'), may hold values from -1 to 1
- brick_dest: int32 [8192, 16, 1], P('ori'), may hold values from 0 to 31; in each aligned block of 4096 rows (0 to 4095, 4096 to 8191, ..., all dimensions but the last counted through in order) at most 256 rows name the same one
- brick_rows: int32 [8192, 16], P('ori'), may hold values from 0 to 255
- kernel: bfloat16 [32, 128, 128], P(('img', 'ori')), may hold values from -3 to 3
Outputs:
- data_volume: float32 [32, 256, 128], P(('img', 'ori'))
- weight_volume: float32 [32, 256], P(('img', 'ori'))
Inputs may be any that keep to these rules, and one draw needn't show every extreme that they name: `images`: images may be large where an image nearly equals reference projections. `brick_dest`: in each aligned block of 4096 segments (the slices one device owns, in order of orientation and segment) at most 256 segments name the same brick, and some block reaches 256.
All inputs are finite; a program needn't handle non-finite values.
Results may differ from a plain program's by a relative error of at most 0.0027.
Values may be sent and summed in bfloat16 or wider, within the bound.
No kernel may reach another device: no remote copies, remote signals or barrier semaphores. Data moves between devices by JAX's collectives and lax.ppermute only.
A program may use at most 128 MiB of HBM per device.

v0:
```python
import jax
import jax.numpy as jnp
from jax import lax
from jax.sharding import PartitionSpec as P

BRICK_ROWS = 256


temper_scale = 4.0


def body(images, projections, brick_dest, brick_rows, kernel):
    gathered = lax.all_gather(images, "ori", axis=0, tiled=True)
    image_count, fourier_width = gathered.shape
    orient_count = projections.shape[0]
    block_rows = min(512, image_count)
    blocks = gathered.reshape(image_count // block_rows, block_rows, fourier_width)
    squared_norm = jnp.sum(jnp.square(projections.astype(jnp.float32)), axis=1)

    def score_block(image_block):
        correlation = lax.dot_general(
            image_block, projections, (((1,), (1,)), ((), ())), preferred_element_type=jnp.float32
        )
        return temper_scale * (correlation - 0.5 * squared_norm[None, :])

    scores = lax.map(score_block, blocks)
    local_max = jnp.max(scores, axis=2)
    row_max = lax.pmax(local_max, "ori")
    row_total = lax.psum(jnp.sum(jnp.exp(scores - row_max[:, :, None]), axis=2), "ori")

    def weigh_block(running, inputs):
        slice_sums, weight_sums = running
        block_scores, image_block, block_max, block_total = inputs
        weights = jnp.exp(block_scores - block_max[:, None]) / block_total[:, None]
        rounded = weights.astype(jnp.bfloat16)
        slice_sums = slice_sums + lax.dot_general(
            rounded, image_block, (((0,), (0,)), ((), ())), preferred_element_type=jnp.float32
        )
        weight_sums = weight_sums + jnp.sum(weights, axis=0)
        return ((slice_sums, weight_sums), None)

    start = (
        jnp.zeros((orient_count, fourier_width), jnp.float32),
        jnp.zeros((orient_count,), jnp.float32),
    )
    (slice_sums, weight_sums), ignored = lax.scan(
        weigh_block, start, (scores, blocks, row_max, row_total)
    )
    image_groups = lax.axis_size("img")
    orient_groups = lax.axis_size("ori")
    devices = image_groups * orient_groups
    owned_rows = orient_count // image_groups
    first_row = lax.axis_index("img") * owned_rows
    own_slices, own_weights = (
        lax.psum_scatter(slice_sums, "img", scatter_dimension=0, tiled=True),
        lax.psum_scatter(weight_sums, "img", scatter_dimension=0, tiled=True),
    )
    segment_width = kernel.shape[1]
    segment_count = fourier_width // segment_width
    segments_here = owned_rows * segment_count
    capacity = max(2, 2 * segments_here // devices)
    segment_values = own_slices.astype(jnp.bfloat16).reshape(segments_here, segment_width)
    segment_weights = jnp.repeat(own_weights.astype(jnp.bfloat16), segment_count)
    segment_dest = lax.dynamic_slice_in_dim(brick_dest, first_row, owned_rows, 0).reshape(
        segments_here
    )
    segment_rows = lax.dynamic_slice_in_dim(brick_rows, first_row, owned_rows, 0).reshape(
        segments_here
    )
    member = (segment_dest[:, None] == jnp.arange(devices, dtype=jnp.int32)[None, :]).astype(
        jnp.int32
    )
    slot_index = jnp.sum(member * jnp.cumsum(member, axis=0), axis=1) - 1
    position = segment_dest * capacity + slot_index
    send_values = (
        jnp.zeros((devices * capacity, segment_width), jnp.bfloat16)
        .at[position]
        .set(segment_values)
    )
    send_weights = jnp.zeros((devices * capacity,), jnp.bfloat16).at[position].set(segment_weights)
    send_rows = (
        jnp.zeros((devices * capacity,), jnp.bfloat16)
        .at[position]
        .set(segment_rows.astype(jnp.bfloat16))
    )
    got_values, got_weights, got_rows = (
        lax.all_to_all(
            send_values.reshape(devices, capacity, segment_width),
            ("img", "ori"),
            split_axis=0,
            concat_axis=0,
            tiled=True,
        ),
        lax.all_to_all(
            send_weights.reshape(devices, capacity),
            ("img", "ori"),
            split_axis=0,
            concat_axis=0,
            tiled=True,
        ),
        lax.all_to_all(
            send_rows.reshape(devices, capacity),
            ("img", "ori"),
            split_axis=0,
            concat_axis=0,
            tiled=True,
        ),
    )
    got_values = got_values.reshape(-1, segment_width)
    got_weights = got_weights.reshape(-1)
    landing = got_rows.reshape(-1).astype(jnp.int32)
    placement = (landing[:, None] == jnp.arange(BRICK_ROWS, dtype=jnp.int32)[None, :]).astype(
        jnp.bfloat16
    )
    gridded = lax.dot_general(
        placement, got_values, (((0,), (0,)), ((), ())), preferred_element_type=jnp.float32
    )
    data_volume = jnp.dot(gridded, kernel[0].astype(jnp.float32), precision=lax.Precision.HIGHEST)
    weight_volume = jnp.dot(
        got_weights.astype(jnp.float32),
        placement.astype(jnp.float32),
        precision=lax.Precision.HIGHEST,
    )
    return (data_volume[None], weight_volume[None])


def solution(mesh):
    placed = (
        P(("img", "ori"), None),
        P("ori", None),
        P("ori", None, None),
        P("ori", None),
        P(("img", "ori"), None, None),
    )
    return jax.shard_map(
        body,
        mesh=mesh,
        in_specs=placed,
        out_specs=(P(("img", "ori"), None, None), P(("img", "ori"), None)),
        check_vma=False,
    )
```

profile of v0, /device:TPU:0, one launch (start us, length us, event | category | flops | bytes accessed | tf_op | source)
XLA Modules:
  0.0 379.1 jit_solution(9724128396634061463)
XLA Ops:
  11.1 83.3 %all-gather.2.cloned.1.call-done = bf16[2048,2048]{1,0:T(8,128)(2,1)} async-done(((bf16[256,2048]{1,0:T(8,128)(2,1)}), bf16[2048,2048]{1,0:T(8,128)(2,1)}) %all-gather.2.cloned.1.call-update) | async-done | bytes 8388624 | tf_op jit(solution)/shard_map/all_gather | solution.py:13
  94.4 26.1 %while.23 = (s32[]{:T(128)}, f32[4,512,1024]{2,1,0:T(8,128)}, bf16[4,512,2048]{2,1,0:T(8,128)(2,1)}, bf16[1024,2048]{1,0:T(8,128)(2,1)}, f32[1024]{0:T(1024)S(1)}, /*index=5*/s32[]{:T(128)}) while((s32[]{:T(128)}, f32[4,512,1024]{2,1,0:T(8,128)}, bf16[4,512,2048]{2,1,0:T(8,128)(2,1)}, bf16[1024,2048]{1,0:T(8,128)(2,1)}, f32[1024]{0:T(1024)S(1)}, ...), condition=%wide.region_6.7_spmd, body=%wide.region_5.6_spmd.sunk | while | flops 2148533248 | bytes 8401989 | solution.py:26
  94.4 6.5 %bitcast_dynamic-update-slice_fusion.2 = f32[4,512,1024]{2,1,0:T(8,128)} fusion(f32[4,512,1024]{2,1,0:T(8,128)} %get-tuple-element.207, s32[]{:T(128)} %get-tuple-element.206, bf16[1024,2048]{1,0:T(8,128)(2,1)} %get-tuple-element.215, bf16[4,512,2048]{2,1,0:T(8,128)(2,1)} %get-tuple-element.214, f32[1024]{0:T(1024)S(1)} %broadcast_multiply_fusion.3), kind=kOutput, calls=%fused_computation.3.clone.1 | convolution fusion | flops 2148532224 | bytes 8393728 | tf_op jit(solution)/shard_map/while/body/eval_jaxpr/dot_general | solution.py:21
  101.0 6.5 %bitcast_dynamic-update-slice_fusion.2 = f32[4,512,1024]{2,1,0:T(8,128)} fusion(f32[4,512,1024]{2,1,0:T(8,128)} %get-tuple-element.207, s32[]{:T(128)} %get-tuple-element.206, bf16[1024,2048]{1,0:T(8,128)(2,1)} %get-tuple-element.215, bf16[4,512,2048]{2,1,0:T(8,128)(2,1)} %get-tuple-element.214, f32[1024]{0:T(1024)S(1)} %broadcast_multiply_fusion.3), kind=kOutput, calls=%fused_computation.3.clone.1 | convolution fusion | flops 2148532224 | bytes 8393728 | tf_op jit(solution)/shard_map/while/body/eval_jaxpr/dot_general | solution.py:21
  107.4 6.5 %bitcast_dynamic-update-slice_fusion.2 = f32[4,512,1024]{2,1,0:T(8,128)} fusion(f32[4,512,1024]{2,1,0:T(8,128)} %get-tuple-element.207, s32[]{:T(128)} %get-tuple-element.206, bf16[1024,2048]{1,0:T(8,128)(2,1)} %get-tuple-element.215, bf16[4,512,2048]{2,1,0:T(8,128)(2,1)} %get-tuple-element.214, f32[1024]{0:T(1024)S(1)} %broadcast_multiply_fusion.3), kind=kOutput, calls=%fused_computation.3.clone.1 | convolution fusion | flops 2148532224 | bytes 8393728 | tf_op jit(solution)/shard_map/while/body/eval_jaxpr/dot_general | solution.py:21
  114.0 6.5 %bitcast_dynamic-update-slice_fusion.2 = f32[4,512,1024]{2,1,0:T(8,128)} fusion(f32[4,512,1024]{2,1,0:T(8,128)} %get-tuple-element.207, s32[]{:T(128)} %get-tuple-element.206, bf16[1024,2048]{1,0:T(8,128)(2,1)} %get-tuple-element.215, bf16[4,512,2048]{2,1,0:T(8,128)(2,1)} %get-tuple-element.214, f32[1024]{0:T(1024)S(1)} %broadcast_multiply_fusion.3), kind=kOutput, calls=%fused_computation.3.clone.1 | convolution fusion | flops 2148532224 | bytes 8393728 | tf_op jit(solution)/shard_map/while/body/eval_jaxpr/dot_general | solution.py:21
  120.5 3.8 %reduce_max.9 = f32[4,512]{1,0:T(4,128)S(1)} reduce(f32[4,512,1024]{2,1,0:T(8,128)} %get-tuple-element.221, f32[]{:T(128)} %constant.57.clone.1), dimensions={2}, to_apply=%region_7.8 | reduce | flops 2095104 | bytes 8396804 | tf_op jit(solution)/shard_map/reduce_max | solution.py:27
  124.3 14.3 %pmax.7 = f32[4,512]{1,0:T(4,128)S(1)} all-reduce(f32[4,512]{1,0:T(4,128)S(1)} %reduce_max.9), channel_id=1, replica_groups=mesh['img'=4,'ori'=8] {'ori'}, use_global_device_ids=true, to_apply=%region_8.9 | all-reduce | flops 2048 | bytes 16384 | tf_op jit(solution)/shard_map/pmax | solution.py:28
  138.6 4.3 %exponential_reduce_fusion = f32[4,512]{1,0:T(4,128)S(1)} fusion(f32[4,512,1024]{2,1,0:T(8,128)} %get-tuple-element.221, f32[4,512]{1,0:T(4,128)S(1)} %pmax.7), kind=kLoop, calls=%fused_computation.23 | loop fusion | flops 4192256 | bytes 8404992 | tf_op jit(solution)/shard_map/reduce_sum | solution.py:29
  143.0 14.1 %psum.7 = f32[4,512]{1,0:T(4,128)S(1)} all-reduce(f32[4,512]{1,0:T(4,128)S(1)} %exponential_reduce_fusion), channel_id=1, replica_groups=mesh['img'=4,'ori'=8] {'ori'}, use_global_device_ids=true, to_apply=%region_10.11 | all-reduce | flops 2048 | bytes 16384 | tf_op jit(solution)/shard_map/psum | solution.py:29
  157.1 47.9 %while.24 = (s32[]{:T(128)}, f32[1024,2048]{1,0:T(8,128)}, f32[1024]{0:T(1024)S(1)}, f32[4,512,1024]{2,1,0:T(8,128)}, f32[4,512]{1,0:T(4,128)S(1)}, /*index=5*/f...) while((s32[]{:T(128)}, f32[1024,2048]{1,0:T(8,128)}, ...), condition=%wide.region_13.14_spmd.clone, body=%wide.region_11.13_spmd.clone.sunk | while | flops 2154824704 | bytes 23102572 | solution.py:46
  157.1 8.0 %select_add_fusion.4 = f32[1024,2048]{1,0:T(8,128)} fusion(f32[1024,2048]{1,0:T(8,128)} %get-tuple-element.228, pred[]{:T(512)S(6)} %compare.3, bf16[4,512,2048]{2,1,0:T(8,128)(2,1)} %get-tuple-element.242, s32[]{:T(128)} %get-tuple-element.227, f32[4,512,1024]{2,1,0:T(8,128)} %get-tuple-element.239, f32[512]{0:T(512)S(1)} %bitcast.79, ...), kind=kOutput, calls=%fused_computation.9.clone.1 | convolution fusion | flops 2153250816 | bytes 20976640 | tf_op jit(solution)/shard_map/while/body/eval_jaxpr/dot_general | solution.py:36
  167.3 10.4 %select_add_fusion.4 = f32[1024,2048]{1,0:T(8,128)} fusion(f32[1024,2048]{1,0:T(8,128)} %get-tuple-element.228, pred[]{:T(512)S(6)} %compare.3, bf16[4,512,2048]{2,1,0:T(8,128)(2,1)} %get-tuple-element.242, s32[]{:T(128)} %get-tuple-element.227, f32[4,512,1024]{2,1,0:T(8,128)} %get-tuple-element.239, f32[512]{0:T(512)S(1)} %bitcast.79, ...), kind=kOutput, calls=%fused_computation.9.clone.1 | convolution fusion | flops 2153250816 | bytes 20976640 | tf_op jit(solution)/shard_map/while/body/eval_jaxpr/dot_general | solution.py:36
  179.8 10.4 %select_add_fusion.4 = f32[1024,2048]{1,0:T(8,128)} fusion(f32[1024,2048]{1,0:T(8,128)} %get-tuple-element.228, pred[]{:T(512)S(6)} %compare.3, bf16[4,512,2048]{2,1,0:T(8,128)(2,1)} %get-tuple-element.242, s32[]{:T(128)} %get-tuple-element.227, f32[4,512,1024]{2,1,0:T(8,128)} %get-tuple-element.239, f32[512]{0:T(512)S(1)} %bitcast.79, ...), kind=kOutput, calls=%fused_computation.9.clone.1 | convolution fusion | flops 2153250816 | bytes 20976640 | tf_op jit(solution)/shard_map/while/body/eval_jaxpr/dot_general | solution.py:36
  192.4 10.4 %select_add_fusion.4 = f32[1024,2048]{1,0:T(8,128)} fusion(f32[1024,2048]{1,0:T(8,128)} %get-tuple-element.228, pred[]{:T(512)S(6)} %compare.3, bf16[4,512,2048]{2,1,0:T(8,128)(2,1)} %get-tuple-element.242, s32[]{:T(128)} %get-tuple-element.227, f32[4,512,1024]{2,1,0:T(8,128)} %get-tuple-element.239, f32[512]{0:T(512)S(1)} %bitcast.79, ...), kind=kOutput, calls=%fused_computation.9.clone.1 | convolution fusion | flops 2153250816 | bytes 20976640 | tf_op jit(solution)/shard_map/while/body/eval_jaxpr/dot_general | solution.py:36
  206.1 9.2 %reduce-window.6 = s32[32,32,128]{2,1,0:T(8,128)S(1)} reduce-window(s32[32,32,128]{2,1,0:T(8,128)S(1)} %fusion.22, s32[]{:T(128)} %constant.30.clone.1), window={size=1x1x128 pad=0_0x0_0x127_0}, to_apply=%region_0.0 | reduce-window | flops 16646144 | bytes 1048580 | tf_op jit(solution)/shard_map/reduce-window
  218.1 28.6 %scatter_custom_fusion = bf16[8192]{0:T(1024)(128)(2,1)S(1)} fusion(s32[4096]{0:T(1024)S(1)} %bitcast.88, bf16[4096]{0:T(1024)(128)(2,1)S(1)} %reshape.127, bf16[]{:T(256)} %constant.21.clone.1), kind=kCustom, calls=%fused_computation.48 | custom fusion | bytes 16386 | tf_op jit(solution)/shard_map/scatter | solution.py:84
  252.8 10.4 %all-reduce = bf16[1024]{0:T(1024)(128)(2,1)S(1)} all-reduce(f32[1024]{0:T(1024)S(1)} %get-tuple-element.69), channel_id=3, replica_groups=mesh['img'=4,'ori'=8] {'img'}, use_global_device_ids=true, to_apply=%region_16.17.clone | all-reduce | flops 1024 | bytes 6144
  263.5 28.6 %scatter_custom_fusion.2 = bf16[8192]{0:T(1024)(128)(2,1)S(1)} fusion(s32[4096]{0:T(1024)S(1)} %bitcast.89, bf16[4096]{0:T(1024)(128)(2,1)S(1)} %reshape.143, bf16[]{:T(256)} %constant.21.clone.1), kind=kCustom, calls=%fused_computation.46 | custom fusion | bytes 16386 | tf_op jit(solution)/shard_map/scatter | solution.py:80
  293.4 3.7 all-to-all-start.2
  299.5 12.5 %scatter_custom_fusion.1 = bf16[8192,128]{1,0:T(8,128)(2,1)} fusion(s32[4096]{0:T(1024)S(1)} %bitcast.90, bf16[4096,128]{1,0:T(8,128)(2,1)S(1)} %reshape.135, bf16[]{:T(256)} %constant.21.clone.1), kind=kCustom, calls=%fused_computation.31 | custom fusion | bytes 2097154 | tf_op jit(solution)/shard_map/scatter | solution.py:78
  312.0 5.8 %all-to-all-start.1 = ((bf16[32,256,128]{2,1,0:T(8,128)(2,1)}), bf16[32,256,128]{2,1,0:T(8,128)(2,1)S(1)}, u32[]{:S(2)}, u32[]{:S(2)}) async-start(bf16[32,256,128]{2,1,0:T(8,128)(2,1)} %bitcast.7), calls=%async_computation.2 | async-start | bytes 4194304 | tf_op jit(solution)/shard_map/all_to_all | solution.py:87
  319.9 48.0 %all-to-all-done.1 = bf16[32,256,128]{2,1,0:T(8,128)(2,1)S(1)} async-done(((bf16[32,256,128]{2,1,0:T(8,128)(2,1)}), bf16[32,256,128]{2,1,0:T(8,128)(2,1)S(1)}, u32[]{:S(2)}, u32[]{:S(2)}) %all-to-all-start.1) | async-done | bytes 2097184 | tf_op jit(solution)/shard_map/all_to_all | solution.py:87
  367.9 3.5 fusion.15
  (66 shorter events, 28.4 us)
Async XLA Ops:
  7.2 364.2 %copy-start = (bf16[1,128,128]{2,1,0:T(8,128)(2,1)S(1)}, bf16[1,128,128]{2,1,0:T(8,128)(2,1)}, u32[]{:S(2)}) copy-start(bf16[1,128,128]{2,1,0:T(8,128)(2,1)} %param.13) | copy-start | bytes 98308
  7.2 87.2 %all-gather.2.cloned.1.call-start = ((), (), s32[]{:S(2)}) async-start(), calls=%async_computation.4 | async-start | bytes 9437184 | tf_op jit(solution)/shard_map/all_gather | solution.py:13
  7.9 289.3 %reduce-scatter.2.cloned.1.call-start = ((), (), s32[]{:S(2)}) async-start(), calls=%async_computation.5 | async-start | bytes 10485760 | tf_op jit(solution)/shard_map/reduce_scatter | solution.py:55
  205.0 46.6 %copy-start.1 = (u32[32]{0:T(128)S(1)}, u32[32]{0:T(128)}, u32[]{:S(2)}) copy-start(u32[32]{0:T(128)} %constant.61) | copy-start | bytes 388
  248.6 44.8 %all-to-all-start = ((bf16[32,2,128]{2,1,0:T(2,128)(2,1)}), bf16[32,2,128]{2,1,0:T(2,128)(2,1)S(1)}, u32[]{:S(2)}, u32[]{:S(2)}) async-start(bf16[32,2,128]{2,1,0:T(2,128)(2,1)} %reshape.158), calls=%async_computation | async-start | bytes 32768 | tf_op jit(solution)/shard_map/all_to_all | solution.py:101
  293.4 18.5 %all-to-all-start.2 = ((bf16[32,2,128]{2,1,0:T(2,128)(2,1)}), bf16[32,2,128]{2,1,0:T(2,128)(2,1)S(1)}, u32[]{:S(2)}, u32[]{:S(2)}) async-start(bf16[32,2,128]{2,1,0:T(2,128)(2,1)} %reshape.160), calls=%async_computation.3 | async-start | bytes 32768 | tf_op jit(solution)/shard_map/all_to_all | solution.py:94
  312.0 55.9 %all-to-all-start.1 = ((bf16[32,256,128]{2,1,0:T(8,128)(2,1)}), bf16[32,256,128]{2,1,0:T(8,128)(2,1)S(1)}, u32[]{:S(2)}, u32[]{:S(2)}) async-start(bf16[32,256,128]{2,1,0:T(8,128)(2,1)} %bitcast.7), calls=%async_computation.2 | async-start | bytes 4194304 | tf_op jit(solution)/shard_map/all_to_all | solution.py:87
Sparse Core Ops, SparseCore 0:
  9.6 84.7 all-gather.1
  205.1 84.9 reduce-scatter.1
where the time goes:
time: 380 us; the launch traced here: 379 us
  waiting for transfers between devices  132 us (35%)
  local copies, waits for them, and re-layouts  74.4 us (20%)
  matrix products  71.7 us (19%)
  blocking collectives  38.8 us (10%)
  other arithmetic  34.4 us (9%)
  between operations  14.9 us (4%)
  starting transfers between devices  12.6 us (3%)
    all_gather x1, waiting for transfers between devices, body(): gathered = lax.all_gather(images, 'ori', axis=0, tiled=True)  83.3 us
    all_to_all x1, waiting for transfers between devices, body(): lax.all_to_all(send_values.reshape(devices, capacity, segment_width), ('i...  48 us
    dot_general x4, matrix products, weigh_block(): lax.dot_general(rounded, image_block, (((0,), (0,)), ((), ())), preferred...  39.3 us
    scatter x1, local copies, waits for them, and re-layouts, body(): send_rows = jnp.zeros((devices * capacity,), jnp.bfloat16).at[position].s...  28.6 us
    scatter x1, local copies, waits for them, and re-layouts, body(): jnp.zeros((devices * capacity,), jnp.bfloat16).at[position]  28.6 us
    dot_general x4, matrix products, score_block(): lax.dot_general(image_block, projections, (((1,), (1,)), ((), ())), prefe...  26.1 us
    pmax x1, blocking collectives, body(): row_max = lax.pmax(local_max, 'ori')  14.3 us
    psum x1, blocking collectives, body(): lax.psum(jnp.sum(jnp.exp(scores - row_max[:, :, None]), axis=2), 'ori')  14.1 us
  transfers between devices with their start and end apart: 5, of which 2 were waited for; matrix products, arithmetic and copies ran while one was open for 25% of the time, Pallas kernels for 0%

commit v1 on v0

v1 whole, which is shorter than its diff:
```python
import functools

import jax
import jax.numpy as jnp
from jax import lax
from jax.experimental import pallas as pl
from jax.experimental.pallas import tpu as pltpu
from jax.sharding import PartitionSpec as P

BRICK_ROWS = 256
EXTRA_ROWS = 16
TILE = 256
temper_scale = 4.0

ANY = pl.BlockSpec(memory_space=pl.ANY)
VMEM = pl.BlockSpec(memory_space=pltpu.VMEM)
SMEM = pl.BlockSpec(memory_space=pltpu.SMEM)
NN = (((1,), (0,)), ((), ()))
NT = (((1,), (1,)), ((), ()))


def dot(a, b, dims=NN):
    return lax.dot_general(a, b, dims, preferred_element_type=jnp.float32)


def one_hot_rows(count, row):
    numbers = lax.broadcasted_iota(jnp.int32, (count, row.shape[1]), 0)
    return jnp.where(numbers == row, 1.0, 0.0).astype(jnp.bfloat16)


def place_kernel(bricks, groups, capacity, dest_ref, rows_ref, slot_ref, map_ref):
    width = dest_ref.shape[2]
    segments = dest_ref.shape[0] // groups
    room = map_ref.shape[2]
    upper = (
        lax.broadcasted_iota(jnp.int32, (width, width), 0)
        <= lax.broadcasted_iota(jnp.int32, (width, width), 1)
    )
    upper = jnp.where(upper, 1.0, 0.0).astype(jnp.bfloat16)
    ones = jnp.ones((width, width), jnp.bfloat16)

    def group(g, ignored):
        def segment(s, carry):
            taken, row_map = carry
            dest = dest_ref[g * segments + s]
            member = one_hot_rows(bricks, dest)
            count = dot(member, upper) + taken
            rank = jnp.sum(member.astype(jnp.float32) * count, axis=0, keepdims=True) - 1.0
            rank = rank.astype(jnp.int32)
            slot_ref[g * segments + s] = (dest * groups + g) * capacity + rank
            marked = member.astype(jnp.float32) * (rows_ref[g * segments + s] + 1).astype(
                jnp.float32
            )
            row_map += dot(marked.astype(jnp.bfloat16), one_hot_rows(room, rank), NT)
            return taken + dot(member, ones), row_map

        start = (jnp.zeros((bricks, width), jnp.float32), jnp.zeros((bricks, room), jnp.float32))
        taken, row_map = lax.fori_loop(0, segments, segment, start)
        map_ref[g] = row_map.astype(jnp.int32) - 1
        return ignored

    lax.fori_loop(0, groups, group, 0)


def score_kernel(chips, candidates, first, *refs):
    n = len(candidates)
    images, refs = refs[:n], refs[n:]
    proj_ref, refs = refs[0], refs[1:]
    if not first:
        norm_in, refs = refs[0], refs[4:]
    if first:
        norm_ref, refs = refs[0], refs[1:]
    else:
        norm_ref = norm_in
    p_hbm, x_hbm, stat_hbm, held, p_buf, stat_buf, sem_in, sem_p, sem_x, sem_s = refs
    block = held.shape[1]
    orients = proj_ref.shape[0]
    chunk = min(256, orients)
    me = lax.axis_index("ori")
    chip, core = me // 2, lax.rem(me, 2)
    plan = []
    for shift, other in candidates:
        source = chip + shift
        valid = jnp.logical_and(source >= 0, source < chips)
        plan.append((valid, jnp.clip(source, 0, chips - 1) * 2 + (1 - core if other else core)))

    def copies(i):
        slot = plan[i][1]
        rows = pl.ds(pl.multiple_of(slot * block, block), block)
        return (
            lambda: pltpu.make_async_copy(images[i], held.at[i], sem_in.at[i]),
            lambda: pltpu.make_async_copy(held.at[i], x_hbm.at[rows], sem_x.at[i]),
            lambda: pltpu.make_async_copy(p_buf.at[i], p_hbm.at[slot], sem_p.at[i]),
            lambda: pltpu.make_async_copy(stat_buf.at[i], stat_hbm.at[slot], sem_s.at[i]),
        )

    for i in range(n):

        @pl.when(plan[i][0])
        def _(i=i):
            copies(i)[0]().start()

    if first:

        def square(r, ignored):
            rows = pl.ds(pl.multiple_of(r * chunk, chunk), chunk)
            values = proj_ref[rows, :].astype(jnp.float32)
            total = jnp.sum(values * values, axis=1, keepdims=True)
            norm_ref[rows, :] = jnp.broadcast_to(total, (chunk, norm_ref.shape[1]))
            return ignored

        lax.fori_loop(0, orients // chunk, square, 0)

    for i in range(n):

        @pl.when(plan[i][0])
        def _(i=i):
            fetch, keep, out, stats = copies(i)
            fetch().wait()
            keep().start()

            def score(r, largest):
                rows = pl.ds(pl.multiple_of(r * chunk, chunk), chunk)
                found = dot(proj_ref[rows, :], held[i], NT)
                norm = norm_ref[rows, 0:1]
                found = temper_scale * (found - 0.5 * norm)
                p_buf[i, rows, :] = found
                return jnp.maximum(largest, jnp.max(found, axis=0, keepdims=True))

            largest = lax.fori_loop(
                0, orients // chunk, score, jnp.full((1, block), -jnp.inf, jnp.float32)
            )

            def exponential(r, total):
                rows = pl.ds(pl.multiple_of(r * chunk, chunk), chunk)
                value = jnp.exp(p_buf[i, rows, :] - largest)
                p_buf[i, rows, :] = value
                return total + jnp.sum(value, axis=0, keepdims=True)

            total = lax.fori_loop(
                0, orients // chunk, exponential, jnp.zeros((1, block), jnp.float32)
            )
            out().start()
            pick = lax.broadcasted_iota(jnp.int32, (8, block), 0) == 0
            stat_buf[i] = jnp.where(pick, largest, total)
            stats().start()

    for i in range(n):

        @pl.when(plan[i][0])
        def _(i=i):
            for copy in copies(i)[1:]:
                copy().wait()


def score_step(chips, candidates, images, projections, carry):
    block, width = images[0].shape
    orients = projections.shape[0]
    blocks = 2 * chips
    n = len(images)
    first = carry is None
    shapes = [
        jax.ShapeDtypeStruct((blocks, orients, block), jnp.float32),
        jax.ShapeDtypeStruct((blocks * block, width), jnp.bfloat16),
        jax.ShapeDtypeStruct((blocks, 8, block), jnp.float32),
    ]
    in_specs = [ANY] * n + [VMEM]
    args = list(images) + [projections]
    if first:
        out_shape = [jax.ShapeDtypeStruct((orients, 128), jnp.float32)] + shapes
        out_specs = [VMEM] + [ANY] * 3
        aliases = {}
    else:
        in_specs += [VMEM] + [ANY] * 3
        args += list(carry)
        out_shape, out_specs = shapes, [ANY] * 3
        aliases = {n + 2 + k: k for k in range(3)}
    out = pl.pallas_call(
        functools.partial(score_kernel, chips, candidates, first),
        out_shape=out_shape,
        in_specs=in_specs,
        out_specs=out_specs,
        scratch_shapes=[
            pltpu.VMEM((n, block, width), jnp.bfloat16),
            pltpu.VMEM((n, orients, block), jnp.float32),
            pltpu.VMEM((n, 8, block), jnp.float32),
            pltpu.SemaphoreType.DMA((n,)),
            pltpu.SemaphoreType.DMA((n,)),
            pltpu.SemaphoreType.DMA((n,)),
            pltpu.SemaphoreType.DMA((n,)),
        ],
        input_output_aliases=aliases,
        compiler_params=pltpu.CompilerParams(vmem_limit_bytes=40 << 20),
        cost_estimate=pl.CostEstimate(
            flops=2 * n * block * orients * width, bytes_accessed=n * (4 << 20), transcendentals=0
        ),
        name="score_blocks",
    )(*args)
    return tuple(out) if first else (carry[0],) + tuple(out)


def sum_kernel(
    bricks,
    capacity,
    slot_ref,
    p_ref,
    scale_ref,
    x_ref,
    dest_ref,
    rows_ref,
    map_ref,
    other_ref,
    mine_ref,
    weights,
    even,
    odd,
    slots,
    volume,
):
    g = pl.program_id(0)
    groups = pl.num_programs(0)
    blocks, owned, block = p_ref.shape
    segments = dest_ref.shape[0] // groups
    per_tile = TILE // 128
    tiles = segments // per_tile
    span = map_ref.shape[2]
    core = lax.rem(lax.axis_index("ori"), 2)

    @pl.when(g == 0)
    def _():
        zero = jnp.zeros((512, 128), jnp.float32)

        def clear(i, ignored):
            slots[pl.ds(pl.multiple_of(i * 512, 512), 512), :] = zero
            return ignored

        lax.fori_loop(0, slots.shape[0] // 512, clear, 0)
        volume[...] = jnp.zeros_like(volume)

    for k in range(blocks):
        weights[:, k * block : (k + 1) * block] = (p_ref[k] * scale_ref[k]).astype(jnp.bfloat16)

    def scatter(held, base):
        for s in range(per_tile):
            for r in range(owned // 8):
                values = held[r * 8 : r * 8 + 8, s * 128 : (s + 1) * 128]
                for k in range(8):
                    slot = slot_ref[base + s * owned + r * 8 + k]
                    slots[pl.ds(slot, 1), :] = values[k : k + 1, :]

    def product(t):
        columns = pl.ds(pl.multiple_of(t * TILE, TILE), TILE)
        return dot(weights[...], x_ref[:, columns])

    def pair(j, ignored):
        base = (g * segments + 2 * j * per_tile) * owned
        even[...] = product(2 * j)
        scatter(odd, base)
        odd[...] = product(2 * j + 1)
        scatter(even, base + per_tile * owned)
        return ignored

    lax.fori_loop(0, tiles // 2, pair, 0)

    ones = jnp.ones((8, blocks * block), jnp.bfloat16)
    sums = dot(ones, weights[...], NT)[0:1]
    high = sums.astype(jnp.bfloat16).astype(jnp.float32)
    low = sums - high

    def weigh(s, ignored):
        dest = dest_ref[g * segments + s]
        member = lax.broadcasted_iota(jnp.int32, (bricks, owned), 0) == dest
        parts = [jnp.where(member, part, 0.0).astype(jnp.bfloat16) for part in (high, low)]
        landed = one_hot_rows(BRICK_ROWS, rows_ref[g * segments + s])
        volume[...] += dot(parts[0], landed, NT) + dot(parts[1], landed, NT)
        return ignored

    lax.fori_loop(0, segments, weigh, 0)

    @pl.when(g == groups - 1)
    def _():
        scatter(odd, groups * segments * owned)
        sub = lax.broadcasted_iota(jnp.int32, (EXTRA_ROWS, 128), 0)

        def grid_brick(i, out_ref, parity):
            b = 2 * i + parity
            values = slots[pl.ds(pl.multiple_of(b * span, 8), span), :].astype(jnp.bfloat16)
            cells = dot(one_hot_rows(BRICK_ROWS, map_ref[b]), values)
            out_ref[i, 0:BRICK_ROWS, :] = cells.astype(jnp.bfloat16)
            total = volume[pl.ds(b, 1), :]
            top = total.astype(jnp.bfloat16).astype(jnp.float32)
            rest = total - top
            extra = jnp.where(sub == 0, top[:, :128], jnp.where(sub == 1, top[:, 128:], 0.0))
            extra += jnp.where(sub == 2, rest[:, :128], jnp.where(sub == 3, rest[:, 128:], 0.0))
            out_ref[i, BRICK_ROWS : BRICK_ROWS + EXTRA_ROWS, :] = extra.astype(jnp.bfloat16)

        def others(i, ignored):
            grid_brick(i, other_ref, 1 - core)
            return ignored

        def own(i, ignored):
            grid_brick(i, mine_ref, core)
            return ignored

        lax.fori_loop(0, bricks // 2, others, 0)
        lax.fori_loop(0, bricks // 2, own, 0)


def sum_step(bricks, groups, capacity, slot, p, scale, x, dest, rows, row_map):
    blocks, orients, block = p.shape
    width = x.shape[1]
    owned = orients // groups
    whole = lambda a: pl.BlockSpec(
        a.shape, lambda g: (0,) * a.ndim, pipeline_mode=pl.Buffered(1)
    )
    out = jax.ShapeDtypeStruct((bricks // 2, BRICK_ROWS + EXTRA_ROWS, 128), jnp.bfloat16)
    return pl.pallas_call(
        functools.partial(sum_kernel, bricks, capacity),
        grid=(groups,),
        out_shape=[out, out],
        in_specs=[
            SMEM,
            pl.BlockSpec((blocks, owned, block), lambda g: (0, g, 0)),
            whole(scale),
            whole(x),
            whole(dest),
            whole(rows),
            whole(row_map),
        ],
        out_specs=[whole(out), whole(out)],
        scratch_shapes=[
            pltpu.VMEM((owned, blocks * block), jnp.bfloat16),
            pltpu.VMEM((owned, TILE), jnp.float32),
            pltpu.VMEM((owned, TILE), jnp.float32),
            pltpu.VMEM((bricks * groups * capacity + 512, 128), jnp.float32),
            pltpu.VMEM((bricks, BRICK_ROWS), jnp.float32),
        ],
        compiler_params=pltpu.CompilerParams(vmem_limit_bytes=56 << 20),
        cost_estimate=pl.CostEstimate(
            flops=2 * blocks * block * orients * width, bytes_accessed=24 << 20, transcendentals=0
        ),
        name="sum_and_grid",
    )(slot, p, scale, x, dest, rows, row_map)


def body(images, projections, brick_dest, brick_rows, kernel):
    image_groups = lax.axis_size("img")
    orient_groups = lax.axis_size("ori")
    chips = orient_groups // 2
    bricks = image_groups * orient_groups
    orients, segments = brick_rows.shape
    owned = orients // image_groups
    capacity = max(2, 2 * owned * segments // bricks)
    me = lax.axis_index("ori")

    swap = [(i, i ^ 1) for i in range(orient_groups)]
    up = [(i, i + 2) for i in range(orient_groups - 2)]
    down = [(i + 2, i) for i in range(orient_groups - 2)]

    with jax.named_scope("place_segments"):

        def lanes(values):
            values = values.reshape(image_groups, owned, segments).transpose(0, 2, 1)
            return values.reshape(image_groups * segments, 1, owned)

        dest, rows = lanes(brick_dest), lanes(brick_rows)
        room = max(128, capacity)
        slot, row_map = pl.pallas_call(
            functools.partial(place_kernel, bricks, image_groups, capacity),
            out_shape=[
                jax.ShapeDtypeStruct(dest.shape, jnp.int32),
                jax.ShapeDtypeStruct((image_groups, bricks, room), jnp.int32),
            ],
            in_specs=[VMEM, VMEM],
            out_specs=[VMEM, VMEM],
            name="place_segments",
        )(dest, rows)
        row_map = row_map[:, :, :capacity].transpose(1, 0, 2).reshape(bricks, 1, image_groups * capacity)
        unused = jnp.full(((TILE // 128) * owned,), bricks * image_groups * capacity, jnp.int32)
        slot = jnp.concatenate([unused, slot.reshape(-1)])

    with jax.named_scope("score"):
        from_below = from_above = images
        carry = score_step(
            chips,
            ((0, False), (0, True)),
            (images, lax.ppermute(images, "ori", swap)),
            projections,
            None,
        )
        for distance in range(1, chips):
            from_below = lax.ppermute(from_below, "ori", up)
            from_above = lax.ppermute(from_above, "ori", down)
            arrived = (
                from_below,
                from_above,
                lax.ppermute(from_below, "ori", swap),
                lax.ppermute(from_above, "ori", swap),
            )
            candidates = (
                (-distance, False),
                (distance, False),
                (-distance, True),
                (distance, True),
            )
            carry = score_step(chips, candidates, arrived, projections, carry)
        _, p, x, stats = carry

    with jax.named_scope("softmax_total"):
        own_largest, own_total = stats[:, 0], stats[:, 1]
        pair = jnp.stack([own_largest, own_total])
        step = 1
        while step < orient_groups:
            partner = [(i, i ^ step) for i in range(orient_groups)]
            other = lax.ppermute(pair, "ori", partner)
            largest = jnp.maximum(pair[0], other[0])
            total = pair[1] * jnp.exp(pair[0] - largest) + other[1] * jnp.exp(other[0] - largest)
            pair = jnp.stack([largest, total])
            step *= 2
        scale = jnp.exp(own_largest - pair[0]) / pair[1]
        scale = scale[:, None, :]

    with jax.named_scope("sum_and_grid"):
        other_cells, cells = sum_step(
            bricks, image_groups, capacity, slot, p, scale, x, dest, rows, row_map
        )

    with jax.named_scope("brick_sums"):
        height = BRICK_ROWS + EXTRA_ROWS

        def add_up(cells, axis, ways, stride):
            own = lax.axis_index(axis) // stride
            total = lax.dynamic_index_in_dim(cells, own, 0, keepdims=False).astype(jnp.float32)
            for k in range(1, ways):
                perm = [(i, i ^ (k * stride)) for i in range(ways * stride)]
                part = lax.dynamic_index_in_dim(cells, own ^ k, 0, keepdims=False)
                total += lax.ppermute(part, axis, perm).astype(jnp.float32)
            return total

        other_cells = lax.ppermute(other_cells, "ori", swap)
        cells = cells.astype(jnp.float32) + other_cells.astype(jnp.float32)
        cells = cells.astype(jnp.bfloat16).reshape(image_groups, chips, height, 128)
        cells = add_up(cells, "img", image_groups, 1).astype(jnp.bfloat16)
        cells = add_up(cells, "ori", chips, 2)

    gridded = cells[:BRICK_ROWS]
    data_volume = jnp.dot(gridded, kernel[0].astype(jnp.float32), precision=lax.Precision.HIGHEST)
    extra = cells[BRICK_ROWS:]
    weight_volume = (extra[0:2] + extra[2:4]).reshape(1, BRICK_ROWS)
    return (data_volume[None], weight_volume)


def solution(mesh):
    placed = (
        P(("img", "ori"), None),
        P("ori", None),
        P("ori", None, None),
        P("ori", None),
        P(("img", "ori"), None, None),
    )
    return jax.shard_map(
        body,
        mesh=mesh,
        in_specs=placed,
        out_specs=(P(("img", "ori"), None, None), P(("img", "ori"), None)),
        check_vma=False,
    )
```

time: 380 us -> 229 us (0.60)
  Pallas kernels: 0 us -> 96.9 us
  matrix products: 71.7 us -> 0.86 us
  local copies, waits for them, and re-layouts: 74.4 us -> 10.4 us
  waiting for transfers between devices: 132 us -> 85.8 us
  blocking collectives: 38.8 us -> 0 us
  other arithmetic: 34.4 us -> 3.27 us
  starting transfers between devices: 12.6 us -> 29.9 us
  between operations: 14.9 us -> 0.93 us
    pallas_call x0 -> x6, Pallas kernels: none -> 96.9 us  [the longest x1 49 us: sum_step(): pl.pallas_call(functools.partial(sum_kernel, bricks, capacity), grid=(gro...]
    ppermute x0 -> x23, waiting for transfers between devices: none -> 85.8 us  [the longest x3 58.6 us: body(): from_below = lax.ppermute(from_below, 'ori', up)]
    all_gather x1 -> x0, waiting for transfers between devices: 83.3 us -> none  [body(): gathered = lax.all_gather(images, 'ori', axis=0, tiled=True)]
    dot_general x10 -> x0, matrix products: 70.9 us -> none  [the longest x4 39.3 us: weigh_block(): lax.dot_general(rounded, image_block, (((0,), (0,)), ((), ())), preferred...]
    scatter x3 -> x0, local copies, waits for them, and re-layouts: 69.6 us -> none  [the longest x1 28.6 us: body(): send_rows = jnp.zeros((devices * capacity,), jnp.bfloat16).at[position].s...]
    all_to_all x3 -> x0, waiting for transfers between devices: 48 us -> none  [the longest x1 48 us: body(): lax.all_to_all(send_values.reshape(devices, capacity, segment_width), ('i...]
    ppermute x0 -> x23, starting transfers between devices: none -> 29.9 us  [the longest x3 13.8 us: body(): from_below = lax.ppermute(from_below, 'ori', up)]
    reduce_sum x7 -> x0, other arithmetic: 16.1 us -> none  [the longest x4 8.36 us: weigh_block(): weight_sums = weight_sums + jnp.sum(weights, axis=0)]
  transfers between devices with their start and end apart: 5 -> 23, of which waited for: 2 -> 10; matrix products, arithmetic and copies ran while one was open for 25% -> 2% of each run, Pallas kernels for 0% -> 19%
where the time goes in v1:
time: 229 us; the launch traced here: 228 us
  Pallas kernels  96.9 us (42%)
  waiting for transfers between devices  85.8 us (37%)
  starting transfers between devices  29.9 us (13%)
  local copies, waits for them, and re-layouts  10.4 us (5%)
  other arithmetic  3.27 us (1%)
    ppermute x3, waiting for transfers between devices, body(): from_below = lax.ppermute(from_below, 'ori', up)  58.6 us
    pallas_call x1, Pallas kernels, sum_step(): pl.pallas_call(functools.partial(sum_kernel, bricks, capacity), grid=(gro...  49 us
    pallas_call x1, Pallas kernels, body(): pl.pallas_call(functools.partial(place_kernel, bricks, image_groups, capa...  24.3 us
    pallas_call x4, Pallas kernels, score_step(): pl.pallas_call(functools.partial(score_kernel, chips, candidates, first),...  23.6 us
    ppermute x6, waiting for transfers between devices, add_up(): total += lax.ppermute(part, axis, perm).astype(jnp.float32)  16.3 us
    ppermute x3, starting transfers between devices, body(): from_below = lax.ppermute(from_below, 'ori', up)  13.8 us
    ppermute x6, starting transfers between devices, add_up(): total += lax.ppermute(part, axis, perm).astype(jnp.float32)  8.01 us
    unnamed x16, local copies, waits for them, and re-layouts  5.64 us
  transfers between devices with their start and end apart: 23, of which 10 were waited for; matrix products, arithmetic and copies ran while one was open for 2% of the time, Pallas kernels for 19%

profile of v1, /device:TPU:0, one launch (start us, length us, event | category | flops | bytes accessed | tf_op | source)
XLA Modules:
  0.0 228.1 jit_solution(12694256915482820650)
XLA Ops:
  0.6 5.0 %collective-permute-start = (bf16[256,2048]{1,0:T(8,128)(2,1)}, bf16[256,2048]{1,0:T(8,128)(2,1)S(1)}, u32[]{:S(2)}, u32[]{:S(2)}) collective-permute-start(bf16[256,2048]{1,0:T(8,128)(2,1)} %refs_0_.1), channel_id=1, source_target_pairs={{0,2},{1,3},{2,4},{3,5},{4,6},{5,7},{8,10},{9,11},{10,12},{11,13},... | collective-permute-start | bytes 3145736 | tf_op jit(solution)/shard_map/score/ppermute | solution.py:392
  6.9 21.3 %collective-permute-done.refs_0_ = bf16[256,2048]{1,0:T(8,128)(2,1)S(1)} collective-permute-done((bf16[256,2048]{1,0:T(8,128)(2,1)}, bf16[256,2048]{1,0:T(8,128)(2,1)S(1)}, u32[]{:S(2)}, u32[]{:S(2)}) %collective-permute-start) | collective-permute-done | bytes 1048608 | tf_op jit(solution)/shard_map/score/ppermute | solution.py:392
  28.3 4.3 %collective-permute-start.1 = (bf16[256,2048]{1,0:T(8,128)(2,1)S(1)}, bf16[256,2048]{1,0:T(8,128)(2,1)S(1)}, u32[]{:S(2)}, u32[]{:S(2)}) collective-permute-start(bf16[256,2048]{1,0:T(8,128)(2,1)S(1)} %collective-permute-done.refs_0_), channel_id=1, source_target_pairs={{0,2},{1,3},{2,4},{3,5},{4,6},{5,7},{8,10},{9,11},{10,12},{11,13},... | collective-permute-start | bytes 3145736 | tf_op jit(solution)/shard_map/score/ppermute | solution.py:392
  34.5 19.6 %collective-permute-done.1.refs_0_ = bf16[256,2048]{1,0:T(8,128)(2,1)S(1)} collective-permute-done((bf16[256,2048]{1,0:T(8,128)(2,1)S(1)}, bf16[256,2048]{1,0:T(8,128)(2,1)S(1)}, u32[]{:S(2)}, u32[]{:S(2)}) %collective-permute-start.1) | collective-permute-done | bytes 1048608 | tf_op jit(solution)/shard_map/score/ppermute | solution.py:392
  54.1 4.4 %collective-permute-start.2 = (bf16[256,2048]{1,0:T(8,128)(2,1)S(1)}, bf16[256,2048]{1,0:T(8,128)(2,1)S(1)}, u32[]{:S(2)}, u32[]{:S(2)}) collective-permute-start(bf16[256,2048]{1,0:T(8,128)(2,1)S(1)} %collective-permute-done.1.refs_0_), channel_id=1, source_target_pairs={{0,2},{1,3},{2,4},{3,5},{4,6},{5,7},{8,10},{9,11},{10,12},{11,13},... | collective-permute-start | bytes 3145736 | tf_op jit(solution)/shard_map/score/ppermute | solution.py:392
  61.4 17.6 %collective-permute-done.2.refs_0_ = bf16[256,2048]{1,0:T(8,128)(2,1)S(1)} collective-permute-done((bf16[256,2048]{1,0:T(8,128)(2,1)S(1)}, bf16[256,2048]{1,0:T(8,128)(2,1)S(1)}, u32[]{:S(2)}, u32[]{:S(2)}) %collective-permute-start.2) | collective-permute-done | bytes 1048608 | tf_op jit(solution)/shard_map/score/ppermute | solution.py:392
  79.1 4.2 %collective-permute-done.5.refs_1_ = bf16[256,2048]{1,0:T(8,128)(2,1)S(1)} collective-permute-done((bf16[256,2048]{1,0:T(8,128)(2,1)S(1)}, bf16[256,2048]{1,0:T(8,128)(2,1)S(1)}, u32[]{:S(2)}, u32[]{:S(2)}) %collective-permute-start.5) | collective-permute-done | bytes 1048608 | tf_op jit(solution)/shard_map/score/ppermute | solution.py:393
  83.3 2.2 copy-done.1
  87.9 6.6 %score_blocks.4 = (f32[1024,128]{1,0:T(8,128)S(1)}, f32[8,1024,256]{2,1,0:T(8,128)}, bf16[2048,2048]{1,0:T(8,128)(2,1)}, f32[8,8,256]{2,1,0:T(8,128)S(1)}) custom-call(bf16[256,2048]{1,0:T(8,128)(2,1)S(1)} %copy-done.3, bf16[256,2048]{1,0:T(8,128)(2,1)S(1)} %copy-done.5, bf16[1024,2048]{1,0:T(8,128)(2,1)S(1)} %copy-done.1), custom_call_target="tpu_custom_call" | custom-call | flops 2147483648 | bytes 8388608 | tf_op jit(solution)/shard_map/score/score_blocks/pallas_call | solution.py:178
  94.6 5.6 %score_blocks.5 = (f32[8,1024,256]{2,1,0:T(8,128)}, bf16[2048,2048]{1,0:T(8,128)(2,1)}, f32[8,8,256]{2,1,0:T(8,128)S(1)}) custom-call(bf16[256,2048]{1,0:T(8,128)(2,1)S(1)} %collective-permute-done.refs_0_, bf16[256,2048]{1,0:T(8,128)(2,1)S(1)} %collective-permute-done.3.refs_1_, ...), custom_call_target="tpu_custom_call", output_to_operand_aliasing={{0}: (6, {}), {1}: (7, {}), {2}: (8, {})} | custom-call | flops 4294967296 | bytes 16777216 | tf_op jit(solution)/shard_map/score/score_blocks/pallas_call | solution.py:178
  100.2 5.7 %score_blocks.6 = (f32[8,1024,256]{2,1,0:T(8,128)}, bf16[2048,2048]{1,0:T(8,128)(2,1)}, f32[8,8,256]{2,1,0:T(8,128)S(1)}) custom-call(bf16[256,2048]{1,0:T(8,128)(2,1)S(1)} %collective-permute-done.1.refs_0_, bf16[256,2048]{1,0:T(8,128)(2,1)S(1)} %collective-permute-done.4.refs_1_, ...), custom_call_target="tpu_custom_call", output_to_operand_aliasing={{0}: (6, {}), {1}: (7, {}), {2}: (8, {})} | custom-call | flops 4294967296 | bytes 16777216 | tf_op jit(solution)/shard_map/score/score_blocks/pallas_call | solution.py:178
  106.0 5.7 %score_blocks.7 = (f32[8,1024,256]{2,1,0:T(8,128)}, bf16[2048,2048]{1,0:T(8,128)(2,1)}, f32[8,8,256]{2,1,0:T(8,128)S(1)}) custom-call(bf16[256,2048]{1,0:T(8,128)(2,1)S(1)} %collective-permute-done.2.refs_0_, bf16[256,2048]{1,0:T(8,128)(2,1)S(1)} %collective-permute-done.5.refs_1_, ...), custom_call_target="tpu_custom_call", output_to_operand_aliasing={{0}: (6, {}), {1}: (7, {}), {2}: (8, {})} | custom-call | flops 4294967296 | bytes 16777216 | tf_op jit(solution)/shard_map/score/score_blocks/pallas_call | solution.py:178
  113.9 3.0 %collective-permute-done.14 = f32[2,8,256]{2,0,1:T(2,128)S(1)} collective-permute-done((f32[2,8,256]{2,0,1:T(2,128)S(1)}, f32[2,8,256]{2,0,1:T(2,128)S(1)}, u32[]{:S(2)}, u32[]{:S(2)}) %collective-permute-start.14) | collective-permute-done | bytes 16416 | tf_op jit(solution)/shard_map/softmax_total/ppermute | solution.py:415
  117.0 1.8 collective-permute-start.15
  120.3 24.3 %place_segments.1 = (s32[64,1,256]{2,1,0:T(1,128)}, s32[4,32,256]{2,1,0:T(8,128)}) custom-call(s32[64,1,256]{2,1,0:T(1,128)} %reshape.45.dest_ref, s32[64,1,256]{2,1,0:T(1,128)} %reshape.47.rows_ref), custom_call_target="tpu_custom_call" | custom-call | tf_op jit(solution)/shard_map/place_segments/place_segments/pallas_call | solution.py:368
  148.6 49.0 %sum_and_grid.1 = (bf16[16,272,128]{2,1,0:T(8,128)(2,1)}, bf16[16,272,128]{2,1,0:T(8,128)(2,1)}) custom-call(s32[16896]{0:T(1024)} %concatenate.3.slot_ref, f32[8,1024,256]{2,1,0:T(8,128)} %get-tuple-element.30.p_ref, f32[8,1,256]{2,1,0:T(1,128)} %fusion.9.scale_ref, bf16[2048,2048]{1,0:T(8,128)(2,1)} %get-tuple-element.32.x_ref, ...), custom_call_target="tpu_custom_call" | custom-call | flops 8589934592 | bytes 25165824 | tf_op jit(solution)/shard_map/sum_and_grid/sum_and_grid/pallas_call | solution.py:317
  197.6 3.0 %collective-permute-done.16 = bf16[16,272,128]{2,1,0:T(8,128)(2,1)S(1)} collective-permute-done((bf16[16,272,128]{2,1,0:T(8,128)(2,1)}, bf16[16,272,128]{2,1,0:T(8,128)(2,1)S(1)}, u32[]{:S(2)}, u32[]{:S(2)}) %collective-permute-start.16) | collective-permute-done | bytes 1114144 | tf_op jit(solution)/shard_map/brick_sums/ppermute | solution.py:440
  200.6 1.5 add_convert_fusion
  202.2 1.5 collective-permute-start.17
  205.8 6.0 %collective-permute-done.17 = bf16[4,272,128]{2,1,0:T(8,128)(2,1)S(1)} collective-permute-done((bf16[4,272,128]{2,1,0:T(8,128)(2,1)S(1)}, bf16[4,272,128]{2,1,0:T(8,128)(2,1)S(1)}, u32[]{:S(2)}, u32[]{:S(2)}) %collective-permute-start.17) | collective-permute-done | bytes 278560 | tf_op jit(solution)/shard_map/brick_sums/ppermute | solution.py:437
  211.8 6.4 %collective-permute-done.18 = bf16[4,272,128]{2,1,0:T(8,128)(2,1)S(1)} collective-permute-done((bf16[4,272,128]{2,1,0:T(8,128)(2,1)S(1)}, bf16[4,272,128]{2,1,0:T(8,128)(2,1)S(1)}, u32[]{:S(2)}, u32[]{:S(2)}) %collective-permute-start.18) | collective-permute-done | bytes 278560 | tf_op jit(solution)/shard_map/brick_sums/ppermute | solution.py:437
  218.7 1.6 collective-permute-start.21
  220.3 2.4 %collective-permute-start.22 = (bf16[272,128]{1,0:T(8,128)(2,1)S(1)}, bf16[272,128]{1,0:T(8,128)(2,1)S(1)}, u32[]{:S(2)}, u32[]{:S(2)}) collective-permute-start(bf16[272,128]{1,0:T(8,128)(2,1)S(1)} %get-tuple-element.42), channel_id=1, source_target_pairs={{0,6},{1,7},{2,4},{3,5},{4,2},{5,3},{6,0},{7,1},{8,14},{9,15},{10,... | collective-permute-start | bytes 208904 | tf_op jit(solution)/shard_map/brick_sums/ppermute | solution.py:437
  222.8 3.9 %collective-permute-done.21 = bf16[272,128]{1,0:T(8,128)(2,1)S(1)} collective-permute-done((bf16[272,128]{1,0:T(8,128)(2,1)S(1)}, bf16[272,128]{1,0:T(8,128)(2,1)S(1)}, u32[]{:S(2)}, u32[]{:S(2)}) %collective-permute-start.21) | collective-permute-done | bytes 69664 | tf_op jit(solution)/shard_map/brick_sums/ppermute | solution.py:437
  (66 shorter events, 20.4 us)
Async XLA Ops:
  0.6 226.6 %copy-start = (bf16[1,128,128]{2,1,0:T(8,128)(2,1)S(1)}, bf16[1,128,128]{2,1,0:T(8,128)(2,1)}, u32[]{:S(2)}) copy-start(bf16[1,128,128]{2,1,0:T(8,128)(2,1)} %param.9) | copy-start | bytes 98308
  0.6 27.7 %collective-permute-start = (bf16[256,2048]{1,0:T(8,128)(2,1)}, bf16[256,2048]{1,0:T(8,128)(2,1)S(1)}, u32[]{:S(2)}, u32[]{:S(2)}) collective-permute-start(bf16[256,2048]{1,0:T(8,128)(2,1)} %refs_0_.1), channel_id=1, source_target_pairs={{0,2},{1,3},{2,4},{3,5},{4,6},{5,7},{8,10},{9,11},{10,12},{11,13},... | collective-permute-start | bytes 3145736 | tf_op jit(solution)/shard_map/score/ppermute | solution.py:392
  5.6 27.0 %collective-permute-start.3 = (bf16[256,2048]{1,0:T(8,128)(2,1)}, bf16[256,2048]{1,0:T(8,128)(2,1)S(1)}, u32[]{:S(2)}, u32[]{:S(2)}) collective-permute-start(bf16[256,2048]{1,0:T(8,128)(2,1)} %refs_0_.1), channel_id=1, source_target_pairs={{2,0},{3,1},{4,2},{5,3},{6,4},{7,5},{10,8},{11,9},{12,10},{13,11},... | collective-permute-start | bytes 3145736 | tf_op jit(solution)/shard_map/score/ppermute | solution.py:393
  28.3 25.8 %collective-permute-start.1 = (bf16[256,2048]{1,0:T(8,128)(2,1)S(1)}, bf16[256,2048]{1,0:T(8,128)(2,1)S(1)}, u32[]{:S(2)}, u32[]{:S(2)}) collective-permute-start(bf16[256,2048]{1,0:T(8,128)(2,1)S(1)} %collective-permute-done.refs_0_), channel_id=1, source_target_pairs={{0,2},{1,3},{2,4},{3,5},{4,6},{5,7},{8,10},{9,11},{10,12},{11,13},... | collective-permute-start | bytes 3145736 | tf_op jit(solution)/shard_map/score/ppermute | solution.py:392
  32.6 25.9 %collective-permute-start.4 = (bf16[256,2048]{1,0:T(8,128)(2,1)S(1)}, bf16[256,2048]{1,0:T(8,128)(2,1)S(1)}, u32[]{:S(2)}, u32[]{:S(2)}) collective-permute-start(bf16[256,2048]{1,0:T(8,128)(2,1)S(1)} %collective-permute-done.3.refs_1_), channel_id=1, source_target_pairs={{2,0},{3,1},{4,2},{5,3},{6,4},{7,5},{10,8},{11,9},{12,10},{13,11},... | collective-permute-start | bytes 3145736 | tf_op jit(solution)/shard_map/score/ppermute | solution.py:393
  33.9 26.0 %collective-permute-start.8 = (bf16[256,2048]{1,0:T(8,128)(2,1)}, bf16[256,2048]{1,0:T(8,128)(2,1)S(1)}, u32[]{:S(2)}, u32[]{:S(2)}) collective-permute-start(bf16[256,2048]{1,0:T(8,128)(2,1)} %refs_0_.1), channel_id=1, source_target_pairs={{0,1},{1,0},{2,3},{3,2},{4,5},{5,4},{6,7},{7,6},{8,9},{9,8},{10,11... | collective-permute-start | bytes 3145736 | tf_op jit(solution)/shard_map/score/ppermute | solution.py:387
  34.0 27.4 %collective-permute-start.11 = (bf16[256,2048]{1,0:T(8,128)(2,1)S(1)}, bf16[256,2048]{1,0:T(8,128)(2,1)S(1)}, u32[]{:S(2)}, u32[]{:S(2)}) collective-permute-start(bf16[256,2048]{1,0:T(8,128)(2,1)S(1)} %collective-permute-done.refs_0_), channel_id=1, source_target_pairs={{0,1},{1,0},{2,3},{3,2},{4,5},{5,4},{6,7},{7,6},{8,9},{9,8},{10,11... | collective-permute-start | bytes 3145736 | tf_op jit(solution)/shard_map/score/ppermute | solution.py:397
  54.1 25.0 %collective-permute-start.2 = (bf16[256,2048]{1,0:T(8,128)(2,1)S(1)}, bf16[256,2048]{1,0:T(8,128)(2,1)S(1)}, u32[]{:S(2)}, u32[]{:S(2)}) collective-permute-start(bf16[256,2048]{1,0:T(8,128)(2,1)S(1)} %collective-permute-done.1.refs_0_), channel_id=1, source_target_pairs={{0,2},{1,3},{2,4},{3,5},{4,6},{5,7},{8,10},{9,11},{10,12},{11,13},... | collective-permute-start | bytes 3145736 | tf_op jit(solution)/shard_map/score/ppermute | solution.py:392
  58.6 24.7 %collective-permute-start.5 = (bf16[256,2048]{1,0:T(8,128)(2,1)S(1)}, bf16[256,2048]{1,0:T(8,128)(2,1)S(1)}, u32[]{:S(2)}, u32[]{:S(2)}) collective-permute-start(bf16[256,2048]{1,0:T(8,128)(2,1)S(1)} %collective-permute-done.4.refs_1_), channel_id=1, source_target_pairs={{2,0},{3,1},{4,2},{5,3},{6,4},{7,5},{10,8},{11,9},{12,10},{13,11},... | collective-permute-start | bytes 3145736 | tf_op jit(solution)/shard_map/score/ppermute | solution.py:393
  59.9 34.7 %collective-permute-start.12 = (bf16[256,2048]{1,0:T(8,128)(2,1)S(1)}, bf16[256,2048]{1,0:T(8,128)(2,1)S(1)}, u32[]{:S(2)}, u32[]{:S(2)}) collective-permute-start(bf16[256,2048]{1,0:T(8,128)(2,1)S(1)} %collective-permute-done.3.refs_1_), channel_id=1, source_target_pairs={{0,1},{1,0},{2,3},{3,2},{4,5},{5,4},{6,7},{7,6},{8,9},{9,8},{10,11... | collective-permute-start | bytes 3145736 | tf_op jit(solution)/shard_map/score/ppermute | solution.py:398
  60.9 39.3 %collective-permute-start.10 = (bf16[256,2048]{1,0:T(8,128)(2,1)S(1)}, bf16[256,2048]{1,0:T(8,128)(2,1)S(1)}, u32[]{:S(2)}, u32[]{:S(2)}) collective-permute-start(bf16[256,2048]{1,0:T(8,128)(2,1)S(1)} %collective-permute-done.4.refs_1_), channel_id=1, source_target_pairs={{0,1},{1,0},{2,3},{3,2},{4,5},{5,4},{6,7},{7,6},{8,9},{9,8},{10,11... | collective-permute-start | bytes 3145736 | tf_op jit(solution)/shard_map/score/ppermute | solution.py:398
  61.4 38.8 %collective-permute-start.9 = (bf16[256,2048]{1,0:T(8,128)(2,1)S(1)}, bf16[256,2048]{1,0:T(8,128)(2,1)S(1)}, u32[]{:S(2)}, u32[]{:S(2)}) collective-permute-start(bf16[256,2048]{1,0:T(8,128)(2,1)S(1)} %collective-permute-done.1.refs_0_), channel_id=1, source_target_pairs={{0,1},{1,0},{2,3},{3,2},{4,5},{5,4},{6,7},{7,6},{8,9},{9,8},{10,11... | collective-permute-start | bytes 3145736 | tf_op jit(solution)/shard_map/score/ppermute | solution.py:397
  79.1 26.8 %collective-permute-start.6 = (bf16[256,2048]{1,0:T(8,128)(2,1)S(1)}, bf16[256,2048]{1,0:T(8,128)(2,1)S(1)}, u32[]{:S(2)}, u32[]{:S(2)}) collective-permute-start(bf16[256,2048]{1,0:T(8,128)(2,1)S(1)} %collective-permute-done.2.refs_0_), channel_id=1, source_target_pairs={{0,1},{1,0},{2,3},{3,2},{4,5},{5,4},{6,7},{7,6},{8,9},{9,8},{10,11... | collective-permute-start | bytes 3145736 | tf_op jit(solution)/shard_map/score/ppermute | solution.py:397
  83.3 22.6 %collective-permute-start.7 = (bf16[256,2048]{1,0:T(8,128)(2,1)S(1)}, bf16[256,2048]{1,0:T(8,128)(2,1)S(1)}, u32[]{:S(2)}, u32[]{:S(2)}) collective-permute-start(bf16[256,2048]{1,0:T(8,128)(2,1)S(1)} %collective-permute-done.5.refs_1_), channel_id=1, source_target_pairs={{0,1},{1,0},{2,3},{3,2},{4,5},{5,4},{6,7},{7,6},{8,9},{9,8},{10,11... | collective-permute-start | bytes 3145736 | tf_op jit(solution)/shard_map/score/ppermute | solution.py:398
  111.7 1.3 collective-permute-start.13
  113.1 3.8 %collective-permute-start.14 = (f32[2,8,256]{2,0,1:T(2,128)S(1)}, f32[2,8,256]{2,0,1:T(2,128)S(1)}, u32[]{:S(2)}, u32[]{:S(2)}) collective-permute-start(f32[2,8,256]{2,0,1:T(2,128)S(1)} %pad_maximum_fusion.1), channel_id=1, source_target_pairs={{0,2},{1,3},{2,0},{3,1},{4,6},{5,7},{6,4},{7,5},{8,10},{9,11},{10,... | collective-permute-start | bytes 49160 | tf_op jit(solution)/shard_map/softmax_total/ppermute | solution.py:415
  117.0 31.0 %collective-permute-start.15 = (f32[2,8,256]{2,0,1:T(2,128)S(1)}, f32[2,8,256]{2,0,1:T(2,128)S(1)}, u32[]{:S(2)}, u32[]{:S(2)}) collective-permute-start(f32[2,8,256]{2,0,1:T(2,128)S(1)} %pad_maximum_fusion.2), channel_id=1, source_target_pairs={{0,4},{1,5},{2,6},{3,7},{4,0},{5,1},{6,2},{7,3},{8,12},{9,13},{10,... | collective-permute-start | bytes 49160 | tf_op jit(solution)/shard_map/softmax_total/ppermute | solution.py:415
  197.6 3.0 %collective-permute-start.16 = (bf16[16,272,128]{2,1,0:T(8,128)(2,1)}, bf16[16,272,128]{2,1,0:T(8,128)(2,1)S(1)}, u32[]{:S(2)}, u32[]{:S(2)}) collective-permute-start(bf16[16,272,128]{2,1,0:T(8,128)(2,1)} %get-tuple-element.35), channel_id=1, source_target_pairs={{0,1},{1,0},{2,3},{3,2},{4,5},{5,4},{6,7},{7,6},{8,9},{9,8},{10,11... | collective-permute-start | bytes 3342344 | tf_op jit(solution)/shard_map/brick_sums/ppermute | solution.py:440
  202.2 9.6 %collective-permute-start.17 = (bf16[4,272,128]{2,1,0:T(8,128)(2,1)S(1)}, bf16[4,272,128]{2,1,0:T(8,128)(2,1)S(1)}, u32[]{:S(2)}, u32[]{:S(2)}) collective-permute-start(bf16[4,272,128]{2,1,0:T(8,128)(2,1)S(1)} %get-tuple-element.38), channel_id=1, source_target_pairs={{0,8},{8,0},{16,24},{24,16},{1,9},{9,1},{17,25},{25,17},{2,10},{10... | collective-permute-start | bytes 835592 | tf_op jit(solution)/shard_map/brick_sums/ppermute | solution.py:437
  203.7 14.4 %collective-permute-start.18 = (bf16[4,272,128]{2,1,0:T(8,128)(2,1)S(1)}, bf16[4,272,128]{2,1,0:T(8,128)(2,1)S(1)}, u32[]{:S(2)}, u32[]{:S(2)}) collective-permute-start(bf16[4,272,128]{2,1,0:T(8,128)(2,1)S(1)} %get-tuple-element.40), channel_id=1, source_target_pairs={{0,16},{8,24},{16,0},{24,8},{1,17},{9,25},{17,1},{25,9},{2,18},{10... | collective-permute-start | bytes 835592 | tf_op jit(solution)/shard_map/brick_sums/ppermute | solution.py:437
  205.3 12.9 %collective-permute-start.19 = (bf16[4,272,128]{2,1,0:T(8,128)(2,1)S(1)}, bf16[4,272,128]{2,1,0:T(8,128)(2,1)S(1)}, u32[]{:S(2)}, u32[]{:S(2)}) collective-permute-start(bf16[4,272,128]{2,1,0:T(8,128)(2,1)S(1)} %get-tuple-element.39), channel_id=1, source_target_pairs={{0,24},{8,16},{16,8},{24,0},{1,25},{9,17},{17,9},{25,1},{2,26},{10... | collective-permute-start | bytes 835592 | tf_op jit(solution)/shard_map/brick_sums/ppermute | solution.py:437
  218.3 4.5 %collective-permute-start.20 = (bf16[272,128]{1,0:T(8,128)(2,1)S(1)}, bf16[272,128]{1,0:T(8,128)(2,1)S(1)}, u32[]{:S(2)}, u32[]{:S(2)}) collective-permute-start(bf16[272,128]{1,0:T(8,128)(2,1)S(1)} %get-tuple-element.41), channel_id=1, source_target_pairs={{0,2},{1,3},{2,0},{3,1},{4,6},{5,7},{6,4},{7,5},{8,10},{9,11},{10,... | collective-permute-start | bytes 208904 | tf_op jit(solution)/shard_map/brick_sums/ppermute | solution.py:437
  218.7 7.9 %collective-permute-start.21 = (bf16[272,128]{1,0:T(8,128)(2,1)S(1)}, bf16[272,128]{1,0:T(8,128)(2,1)S(1)}, u32[]{:S(2)}, u32[]{:S(2)}) collective-permute-start(bf16[272,128]{1,0:T(8,128)(2,1)S(1)} %get-tuple-element.43), channel_id=1, source_target_pairs={{0,4},{1,5},{2,6},{3,7},{4,0},{5,1},{6,2},{7,3},{8,12},{9,13},{10,... | collective-permute-start | bytes 208904 | tf_op jit(solution)/shard_map/brick_sums/ppermute | solution.py:437
  220.3 6.3 %collective-permute-start.22 = (bf16[272,128]{1,0:T(8,128)(2,1)S(1)}, bf16[272,128]{1,0:T(8,128)(2,1)S(1)}, u32[]{:S(2)}, u32[]{:S(2)}) collective-permute-start(bf16[272,128]{1,0:T(8,128)(2,1)S(1)} %get-tuple-element.42), channel_id=1, source_target_pairs={{0,6},{1,7},{2,4},{3,5},{4,2},{5,3},{6,0},{7,1},{8,14},{9,15},{10,... | collective-permute-start | bytes 208904 | tf_op jit(solution)/shard_map/brick_sums/ppermute | solution.py:437
  (7 other events, 38.8 us)

commit v2 on v1

--- a/solution.py
+++ b/solution.py
@@ -40,22 +40,24 @@
     ones = jnp.ones((width, width), jnp.bfloat16)
 
     def group(g, ignored):
-        def segment(s, carry):
-            taken, row_map = carry
-            dest = dest_ref[g * segments + s]
-            member = one_hot_rows(bricks, dest)
-            count = dot(member, upper) + taken
-            rank = jnp.sum(member.astype(jnp.float32) * count, axis=0, keepdims=True) - 1.0
+        dests = [dest_ref[g * segments + s] for s in range(segments)]
+        members = [one_hot_rows(bricks, dest) for dest in dests]
+        stacked = jnp.concatenate(members, axis=0)
+        within = dot(stacked, upper)
+        totals = dot(stacked, ones)
+        taken = jnp.zeros((bricks, width), jnp.float32)
+        marked, ranks = [], []
+        for s in range(segments):
+            part = slice(s * bricks, (s + 1) * bricks)
+            member = members[s].astype(jnp.float32)
+            rank = jnp.sum(member * (within[part] + taken), axis=0, keepdims=True) - 1.0
             rank = rank.astype(jnp.int32)
-            slot_ref[g * segments + s] = (dest * groups + g) * capacity + rank
-            marked = member.astype(jnp.float32) * (rows_ref[g * segments + s] + 1).astype(
-                jnp.float32
-            )
-            row_map += dot(marked.astype(jnp.bfloat16), one_hot_rows(room, rank), NT)
-            return taken + dot(member, ones), row_map
-
-        start = (jnp.zeros((bricks, width), jnp.float32), jnp.zeros((bricks, room), jnp.float32))
-        taken, row_map = lax.fori_loop(0, segments, segment, start)
+            taken += totals[part]
+            slot_ref[g * segments + s] = (dests[s] * groups + g) * capacity + rank
+            row = (rows_ref[g * segments + s] + 1).astype(jnp.float32)
+            marked.append((member * row).astype(jnp.bfloat16))
+            ranks.append(one_hot_rows(room, rank))
+        row_map = dot(jnp.concatenate(marked, axis=1), jnp.concatenate(ranks, axis=1), NT)
         map_ref[g] = row_map.astype(jnp.int32) - 1
         return ignored
 
@@ -252,7 +254,22 @@
         columns = pl.ds(pl.multiple_of(t * TILE, TILE), TILE)
         return dot(weights[...], x_ref[:, columns])
 
+    ones = jnp.ones((8, blocks * block), jnp.bfloat16)
+    sums = dot(ones, weights[...], NT)[0:1]
+    high = sums.astype(jnp.bfloat16).astype(jnp.float32)
+    low = sums - high
+
+    def weigh(s):
+        dest = dest_ref[g * segments + s]
+        member = lax.broadcasted_iota(jnp.int32, (bricks, owned), 0) == dest
+        parts = [jnp.where(member, part, 0.0).astype(jnp.bfloat16) for part in (high, low)]
+        return jnp.concatenate(parts, axis=0), one_hot_rows(BRICK_ROWS, rows_ref[g * segments + s])
+
     def pair(j, ignored):
+        both = [weigh(2 * j * per_tile + k) for k in range(2 * per_tile)]
+        carried = jnp.concatenate([first for first, _ in both], axis=1)
+        landed = jnp.concatenate([second for _, second in both], axis=1)
+        volume[...] += dot(carried, landed, NT)
         base = (g * segments + 2 * j * per_tile) * owned
         even[...] = product(2 * j)
         scatter(odd, base)
@@ -262,32 +279,18 @@
 
     lax.fori_loop(0, tiles // 2, pair, 0)
 
-    ones = jnp.ones((8, blocks * block), jnp.bfloat16)
-    sums = dot(ones, weights[...], NT)[0:1]
-    high = sums.astype(jnp.bfloat16).astype(jnp.float32)
-    low = sums - high
-
-    def weigh(s, ignored):
-        dest = dest_ref[g * segments + s]
-        member = lax.broadcasted_iota(jnp.int32, (bricks, owned), 0) == dest
-        parts = [jnp.where(member, part, 0.0).astype(jnp.bfloat16) for part in (high, low)]
-        landed = one_hot_rows(BRICK_ROWS, rows_ref[g * segments + s])
-        volume[...] += dot(parts[0], landed, NT) + dot(parts[1], landed, NT)
-        return ignored
-
-    lax.fori_loop(0, segments, weigh, 0)
-
     @pl.when(g == groups - 1)
     def _():
         scatter(odd, groups * segments * owned)
         sub = lax.broadcasted_iota(jnp.int32, (EXTRA_ROWS, 128), 0)
+        unroll = 8
 
         def grid_brick(i, out_ref, parity):
             b = 2 * i + parity
             values = slots[pl.ds(pl.multiple_of(b * span, 8), span), :].astype(jnp.bfloat16)
             cells = dot(one_hot_rows(BRICK_ROWS, map_ref[b]), values)
             out_ref[i, 0:BRICK_ROWS, :] = cells.astype(jnp.bfloat16)
-            total = volume[pl.ds(b, 1), :]
+            total = volume[pl.ds(b, 1), :] + volume[pl.ds(bricks + b, 1), :]
             top = total.astype(jnp.bfloat16).astype(jnp.float32)
             rest = total - top
             extra = jnp.where(sub == 0, top[:, :128], jnp.where(sub == 1, top[:, 128:], 0.0))
@@ -295,15 +298,17 @@
             out_ref[i, BRICK_ROWS : BRICK_ROWS + EXTRA_ROWS, :] = extra.astype(jnp.bfloat16)
 
         def others(i, ignored):
-            grid_brick(i, other_ref, 1 - core)
+            for k in range(unroll):
+                grid_brick(i * unroll + k, other_ref, 1 - core)
             return ignored
 
         def own(i, ignored):
-            grid_brick(i, mine_ref, core)
+            for k in range(unroll):
+                grid_brick(i * unroll + k, mine_ref, core)
             return ignored
 
-        lax.fori_loop(0, bricks // 2, others, 0)
-        lax.fori_loop(0, bricks // 2, own, 0)
+        lax.fori_loop(0, bricks // 2 // unroll, others, 0)
+        lax.fori_loop(0, bricks // 2 // unroll, own, 0)
 
 
 def sum_step(bricks, groups, capacity, slot, p, scale, x, dest, rows, row_map):
@@ -333,7 +338,7 @@
             pltpu.VMEM((owned, TILE), jnp.float32),
             pltpu.VMEM((owned, TILE), jnp.float32),
             pltpu.VMEM((bricks * groups * capacity + 512, 128), jnp.float32),
-            pltpu.VMEM((bricks, BRICK_ROWS), jnp.float32),
+            pltpu.VMEM((2 * bricks, BRICK_ROWS), jnp.float32),
         ],
         compiler_params=pltpu.CompilerParams(vmem_limit_bytes=56 << 20),
         cost_estimate=pl.CostEstimate(
@@ -377,7 +382,7 @@
         )(dest, rows)
         row_map = row_map[:, :, :capacity].transpose(1, 0, 2).reshape(bricks, 1, image_groups * capacity)
         unused = jnp.full(((TILE // 128) * owned,), bricks * image_groups * capacity, jnp.int32)
-        slot = jnp.concatenate([unused, slot.reshape(-1)])
+        placed = (jnp.concatenate([unused, slot.reshape(-1)]), row_map, dest, rows)
 
     with jax.named_scope("score"):
         from_below = from_above = images
@@ -391,6 +396,9 @@
         for distance in range(1, chips):
             from_below = lax.ppermute(from_below, "ori", up)
             from_above = lax.ppermute(from_above, "ori", down)
+            from_below, from_above, carry, placed = lax.optimization_barrier(
+                (from_below, from_above, carry, placed)
+            )
             arrived = (
                 from_below,
                 from_above,
@@ -405,6 +413,7 @@
             )
             carry = score_step(chips, candidates, arrived, projections, carry)
         _, p, x, stats = carry
+        slot, row_map, dest, rows = placed
 
     with jax.named_scope("softmax_total"):
         own_largest, own_total = stats[:, 0], stats[:, 1]

time: 229 us -> 180 us (0.79)
  Pallas kernels: 96.9 us -> 64.7 us
  waiting for transfers between devices: 85.8 us -> 74.6 us
  starting transfers between devices: 29.9 us -> 25.7 us
    ppermute x3, waiting for transfers between devices: 58.6 us -> 31.1 us  [body(): from_below = lax.ppermute(from_below, 'ori', up)]
    pallas_call x1, Pallas kernels: 24.3 us -> 6.37 us  [body(): pl.pallas_call(functools.partial(place_kernel, bricks, image_groups, capa...]
    pallas_call x1, Pallas kernels: 49 us -> 34.8 us  [sum_step(): pl.pallas_call(functools.partial(sum_kernel, bricks, capacity), grid=(gro...]
    ppermute x3, waiting for transfers between devices: 4.19 us -> 11.5 us  [body(): from_above = lax.ppermute(from_above, 'ori', down)]
    ppermute x3, waiting for transfers between devices: 3.84 us -> 9.49 us  [body(): other = lax.ppermute(pair, 'ori', partner)]
    ppermute x3, starting transfers between devices: 3.07 us -> 0.25 us  [body(): other = lax.ppermute(pair, 'ori', partner)]
    unnamed x16 -> x8, local copies, waits for them, and re-layouts: 5.64 us -> 3.43 us
  transfers between devices with their start and end apart: 23 -> 23, of which waited for: 10 -> 14; matrix products, arithmetic and copies ran while one was open for 2% -> 4% of each run, Pallas kernels for 19% -> 13%
where the time goes in v2:
time: 180 us
  waiting for transfers between devices  74.6 us (41%)
  Pallas kernels  64.7 us (36%)
  starting transfers between devices  25.7 us (14%)
  local copies, waits for them, and re-layouts  9.04 us (5%)
  other arithmetic  4.11 us (2%)
    pallas_call x1, Pallas kernels, sum_step(): pl.pallas_call(functools.partial(sum_kernel, bricks, capacity), grid=(gro...  34.8 us
    ppermute x3, waiting for transfers between devices, body(): from_below = lax.ppermute(from_below, 'ori', up)  31.1 us
    pallas_call x4, Pallas kernels, score_step(): pl.pallas_call(functools.partial(score_kernel, chips, candidates, first),...  23.5 us
    ppermute x6, waiting for transfers between devices, add_up(): total += lax.ppermute(part, axis, perm).astype(jnp.float32)  15.9 us
    ppermute x3, starting transfers between devices, body(): from_below = lax.ppermute(from_below, 'ori', up)  11.5 us
    ppermute x3, waiting for transfers between devices, body(): from_above = lax.ppermute(from_above, 'ori', down)  11.5 us
    ppermute x3, waiting for transfers between devices, body(): other = lax.ppermute(pair, 'ori', partner)  9.49 us
    ppermute x6, starting transfers between devices, add_up(): total += lax.ppermute(part, axis, perm).astype(jnp.float32)  8 us
  transfers between devices with their start and end apart: 23, of which 14 were waited for; matrix products, arithmetic and copies ran while one was open for 4% of the time, Pallas kernels for 13%

profile of v2, /device:TPU:0, one launch (start us, length us, event | category | flops | bytes accessed | tf_op | source)
XLA Modules:
  0.0 179.9 jit_solution(9240499808139459342)
XLA Ops:
  1.2 4.6 %collective-permute-start = (bf16[256,2048]{1,0:T(8,128)(2,1)}, bf16[256,2048]{1,0:T(8,128)(2,1)S(1)}, u32[]{:S(2)}, u32[]{:S(2)}) collective-permute-start(bf16[256,2048]{1,0:T(8,128)(2,1)} %refs_0_.1), channel_id=1, source_target_pairs={{0,2},{1,3},{2,4},{3,5},{4,6},{5,7},{8,10},{9,11},{10,12},{11,13},... | collective-permute-start | bytes 3145736 | tf_op jit(solution)/shard_map/score/ppermute | solution.py:397
  10.3 6.4 %place_segments.1 = (s32[64,1,256]{2,1,0:T(1,128)}, s32[4,32,256]{2,1,0:T(8,128)}) custom-call(s32[64,1,256]{2,1,0:T(1,128)} %reshape.45.dest_ref, s32[64,1,256]{2,1,0:T(1,128)} %reshape.47.rows_ref), custom_call_target="tpu_custom_call" | custom-call | tf_op jit(solution)/shard_map/place_segments/place_segments/pallas_call | solution.py:373
  19.9 2.2 %copy-done.1 = bf16[1024,2048]{1,0:T(8,128)(2,1)S(1)} copy-done((bf16[1024,2048]{1,0:T(8,128)(2,1)S(1)}, bf16[1024,2048]{1,0:T(8,128)(2,1)}, u32[]{:S(2)}) %copy-start.1) | copy-done | bytes 4194328
  23.3 6.6 %score_blocks.4 = (f32[1024,128]{1,0:T(8,128)S(1)}, f32[8,1024,256]{2,1,0:T(8,128)}, bf16[2048,2048]{1,0:T(8,128)(2,1)}, f32[8,8,256]{2,1,0:T(8,128)S(1)}) custom-call(bf16[256,2048]{1,0:T(8,128)(2,1)S(1)} %copy-done.3, bf16[256,2048]{1,0:T(8,128)(2,1)S(1)} %collective-permute-done.2.refs_1_, bf16[1024,2048]{1,0:T(8,128)(2,1)S(1)} %copy-done.1), custom_call_target="tpu_custom_call" | custom-call | flops 2147483648 | bytes 8388608 | tf_op jit(solution)/shard_map/score/score_blocks/pallas_call | solution.py:180
  30.0 3.1 %collective-permute-done.1.refs_1_ = bf16[256,2048]{1,0:T(8,128)(2,1)S(1)} collective-permute-done((bf16[256,2048]{1,0:T(8,128)(2,1)}, bf16[256,2048]{1,0:T(8,128)(2,1)S(1)}, u32[]{:S(2)}, u32[]{:S(2)}) %collective-permute-start.1) | collective-permute-done | bytes 1048608 | tf_op jit(solution)/shard_map/score/ppermute | solution.py:398
  33.6 3.5 %collective-permute-start.3 = (bf16[256,2048]{1,0:T(8,128)(2,1)S(1)}, bf16[256,2048]{1,0:T(8,128)(2,1)S(1)}, u32[]{:S(2)}, u32[]{:S(2)}) collective-permute-start(bf16[256,2048]{1,0:T(8,128)(2,1)S(1)} %collective-permute-done.refs_0_), channel_id=1, source_target_pairs={{0,2},{1,3},{2,4},{3,5},{4,6},{5,7},{8,10},{9,11},{10,12},{11,13},... | collective-permute-start | bytes 3145736 | tf_op jit(solution)/shard_map/score/ppermute | solution.py:397
  38.4 5.6 %score_blocks.5 = (f32[8,1024,256]{2,1,0:T(8,128)}, bf16[2048,2048]{1,0:T(8,128)(2,1)}, f32[8,8,256]{2,1,0:T(8,128)S(1)}) custom-call(bf16[256,2048]{1,0:T(8,128)(2,1)S(1)} %collective-permute-done.refs_0_, bf16[256,2048]{1,0:T(8,128)(2,1)S(1)} %collective-permute-done.1.refs_1_, ...), custom_call_target="tpu_custom_call", output_to_operand_aliasing={{0}: (6, {}), {1}: (7, {}), {2}: (8, {})} | custom-call | flops 4294967296 | bytes 16777216 | tf_op jit(solution)/shard_map/score/score_blocks/pallas_call | solution.py:180
  44.1 15.5 %collective-permute-done.3.refs_0_ = bf16[256,2048]{1,0:T(8,128)(2,1)S(1)} collective-permute-done((bf16[256,2048]{1,0:T(8,128)(2,1)S(1)}, bf16[256,2048]{1,0:T(8,128)(2,1)S(1)}, u32[]{:S(2)}, u32[]{:S(2)}) %collective-permute-start.3) | collective-permute-done | bytes 1048608 | tf_op jit(solution)/shard_map/score/ppermute | solution.py:397
  59.6 4.2 %collective-permute-done.4.refs_1_ = bf16[256,2048]{1,0:T(8,128)(2,1)S(1)} collective-permute-done((bf16[256,2048]{1,0:T(8,128)(2,1)S(1)}, bf16[256,2048]{1,0:T(8,128)(2,1)S(1)}, u32[]{:S(2)}, u32[]{:S(2)}) %collective-permute-start.4) | collective-permute-done | bytes 1048608 | tf_op jit(solution)/shard_map/score/ppermute | solution.py:398
  64.3 3.5 %collective-permute-start.7 = (bf16[256,2048]{1,0:T(8,128)(2,1)S(1)}, bf16[256,2048]{1,0:T(8,128)(2,1)S(1)}, u32[]{:S(2)}, u32[]{:S(2)}) collective-permute-start(bf16[256,2048]{1,0:T(8,128)(2,1)S(1)} %collective-permute-done.3.refs_0_), channel_id=1, source_target_pairs={{0,2},{1,3},{2,4},{3,5},{4,6},{5,7},{8,10},{9,11},{10,12},{11,13},... | collective-permute-start | bytes 3145736 | tf_op jit(solution)/shard_map/score/ppermute | solution.py:397
  69.1 5.6 %score_blocks.6 = (f32[8,1024,256]{2,1,0:T(8,128)}, bf16[2048,2048]{1,0:T(8,128)(2,1)}, f32[8,8,256]{2,1,0:T(8,128)S(1)}) custom-call(bf16[256,2048]{1,0:T(8,128)(2,1)S(1)} %collective-permute-done.3.refs_0_, bf16[256,2048]{1,0:T(8,128)(2,1)S(1)} %collective-permute-done.4.refs_1_, ...), custom_call_target="tpu_custom_call", output_to_operand_aliasing={{0}: (6, {}), {1}: (7, {}), {2}: (8, {})} | custom-call | flops 4294967296 | bytes 16777216 | tf_op jit(solution)/shard_map/score/score_blocks/pallas_call | solution.py:180
  74.7 15.5 %collective-permute-done.7.refs_0_ = bf16[256,2048]{1,0:T(8,128)(2,1)S(1)} collective-permute-done((bf16[256,2048]{1,0:T(8,128)(2,1)S(1)}, bf16[256,2048]{1,0:T(8,128)(2,1)S(1)}, u32[]{:S(2)}, u32[]{:S(2)}) %collective-permute-start.7) | collective-permute-done | bytes 1048608 | tf_op jit(solution)/shard_map/score/ppermute | solution.py:397
  90.3 4.2 %collective-permute-done.8.refs_1_ = bf16[256,2048]{1,0:T(8,128)(2,1)S(1)} collective-permute-done((bf16[256,2048]{1,0:T(8,128)(2,1)S(1)}, bf16[256,2048]{1,0:T(8,128)(2,1)S(1)}, u32[]{:S(2)}, u32[]{:S(2)}) %collective-permute-start.8) | collective-permute-done | bytes 1048608 | tf_op jit(solution)/shard_map/score/ppermute | solution.py:398
  95.0 2.1 %collective-permute-done.11.refs_2_ = bf16[256,2048]{1,0:T(8,128)(2,1)S(1)} collective-permute-done((bf16[256,2048]{1,0:T(8,128)(2,1)S(1)}, bf16[256,2048]{1,0:T(8,128)(2,1)S(1)}, u32[]{:S(2)}, u32[]{:S(2)}) %collective-permute-start.11) | collective-permute-done | bytes 1048608 | tf_op jit(solution)/shard_map/score/ppermute | solution.py:405
  98.6 5.7 %score_blocks.7 = (f32[8,1024,256]{2,1,0:T(8,128)}, bf16[2048,2048]{1,0:T(8,128)(2,1)}, f32[8,8,256]{2,1,0:T(8,128)S(1)}) custom-call(bf16[256,2048]{1,0:T(8,128)(2,1)S(1)} %collective-permute-done.7.refs_0_, bf16[256,2048]{1,0:T(8,128)(2,1)S(1)} %collective-permute-done.8.refs_1_, ...), custom_call_target="tpu_custom_call", output_to_operand_aliasing={{0}: (6, {}), {1}: (7, {}), {2}: (8, {})} | custom-call | flops 4294967296 | bytes 16777216 | tf_op jit(solution)/shard_map/score/score_blocks/pallas_call | solution.py:180
  105.7 3.7 %collective-permute-done.14 = f32[2,8,256]{2,0,1:T(2,128)S(1)} collective-permute-done((f32[2,8,256]{2,0,1:T(2,128)S(1)}, f32[2,8,256]{2,0,1:T(2,128)S(1)}, u32[]{:S(2)}, u32[]{:S(2)}) %collective-permute-start.14) | collective-permute-done | bytes 16416 | tf_op jit(solution)/shard_map/softmax_total/ppermute | solution.py:424
  109.6 4.6 %collective-permute-done.15 = f32[2,8,256]{2,0,1:T(2,128)S(1)} collective-permute-done((f32[2,8,256]{2,0,1:T(2,128)S(1)}, f32[2,8,256]{2,0,1:T(2,128)S(1)}, u32[]{:S(2)}, u32[]{:S(2)}) %collective-permute-start.15) | collective-permute-done | bytes 16416 | tf_op jit(solution)/shard_map/softmax_total/ppermute | solution.py:424
  114.9 34.8 %sum_and_grid.1 = (bf16[16,272,128]{2,1,0:T(8,128)(2,1)}, bf16[16,272,128]{2,1,0:T(8,128)(2,1)}) custom-call(s32[16896]{0:T(1024)} %concatenate.3.slot_ref, f32[8,1024,256]{2,1,0:T(8,128)} %get-tuple-element.88.p_ref, f32[8,1,256]{2,1,0:T(1,128)} %fusion.9.scale_ref, bf16[2048,2048]{1,0:T(8,128)(2,1)} %get-tuple-element.90.x_ref, ...), custom_call_target="tpu_custom_call" | custom-call | flops 8589934592 | bytes 25165824 | tf_op jit(solution)/shard_map/sum_and_grid/sum_and_grid/pallas_call | solution.py:322
  149.7 3.0 %collective-permute-done.16 = bf16[16,272,128]{2,1,0:T(8,128)(2,1)S(1)} collective-permute-done((bf16[16,272,128]{2,1,0:T(8,128)(2,1)}, bf16[16,272,128]{2,1,0:T(8,128)(2,1)S(1)}, u32[]{:S(2)}, u32[]{:S(2)}) %collective-permute-start.16) | collective-permute-done | bytes 1114144 | tf_op jit(solution)/shard_map/brick_sums/ppermute | solution.py:449
  154.3 1.6 collective-permute-start.17
  157.9 6.0 %collective-permute-done.17 = bf16[4,272,128]{2,1,0:T(8,128)(2,1)S(1)} collective-permute-done((bf16[4,272,128]{2,1,0:T(8,128)(2,1)S(1)}, bf16[4,272,128]{2,1,0:T(8,128)(2,1)S(1)}, u32[]{:S(2)}, u32[]{:S(2)}) %collective-permute-start.17) | collective-permute-done | bytes 278560 | tf_op jit(solution)/shard_map/brick_sums/ppermute | solution.py:446
  163.9 6.4 %collective-permute-done.18 = bf16[4,272,128]{2,1,0:T(8,128)(2,1)S(1)} collective-permute-done((bf16[4,272,128]{2,1,0:T(8,128)(2,1)S(1)}, bf16[4,272,128]{2,1,0:T(8,128)(2,1)S(1)}, u32[]{:S(2)}, u32[]{:S(2)}) %collective-permute-start.18) | collective-permute-done | bytes 278560 | tf_op jit(solution)/shard_map/brick_sums/ppermute | solution.py:446
  170.6 4.3 %collective-permute-start.22 = (bf16[272,128]{1,0:T(8,128)(2,1)S(1)}, bf16[272,128]{1,0:T(8,128)(2,1)S(1)}, u32[]{:S(2)}, u32[]{:S(2)}) collective-permute-start(bf16[272,128]{1,0:T(8,128)(2,1)S(1)} %get-tuple-element.102), channel_id=1, source_target_pairs={{0,6},{1,7},{2,4},{3,5},{4,2},{5,3},{6,0},{7,1},{8,14},{9,15},{10,... | collective-permute-start | bytes 208904 | tf_op jit(solution)/shard_map/brick_sums/ppermute | solution.py:446
  174.9 3.5 %collective-permute-done.21 = bf16[272,128]{1,0:T(8,128)(2,1)S(1)} collective-permute-done((bf16[272,128]{1,0:T(8,128)(2,1)S(1)}, bf16[272,128]{1,0:T(8,128)(2,1)S(1)}, u32[]{:S(2)}, u32[]{:S(2)}) %collective-permute-start.21) | collective-permute-done | bytes 69664 | tf_op jit(solution)/shard_map/brick_sums/ppermute | solution.py:446
  (58 shorter events, 22.8 us)
Async XLA Ops:
  0.6 178.4 %copy-start = (bf16[1,128,128]{2,1,0:T(8,128)(2,1)S(1)}, bf16[1,128,128]{2,1,0:T(8,128)(2,1)}, u32[]{:S(2)}) copy-start(bf16[1,128,128]{2,1,0:T(8,128)(2,1)} %param.9) | copy-start | bytes 98308
  0.6 19.3 %collective-permute-start.2 = (bf16[256,2048]{1,0:T(8,128)(2,1)}, bf16[256,2048]{1,0:T(8,128)(2,1)S(1)}, u32[]{:S(2)}, u32[]{:S(2)}) collective-permute-start(bf16[256,2048]{1,0:T(8,128)(2,1)} %refs_0_.1), channel_id=1, source_target_pairs={{0,1},{1,0},{2,3},{3,2},{4,5},{5,4},{6,7},{7,6},{8,9},{9,8},{10,11... | collective-permute-start | bytes 3145736 | tf_op jit(solution)/shard_map/score/ppermute | solution.py:392
  1.2 28.8 %collective-permute-start = (bf16[256,2048]{1,0:T(8,128)(2,1)}, bf16[256,2048]{1,0:T(8,128)(2,1)S(1)}, u32[]{:S(2)}, u32[]{:S(2)}) collective-permute-start(bf16[256,2048]{1,0:T(8,128)(2,1)} %refs_0_.1), channel_id=1, source_target_pairs={{0,2},{1,3},{2,4},{3,5},{4,6},{5,7},{8,10},{9,11},{10,12},{11,13},... | collective-permute-start | bytes 3145736 | tf_op jit(solution)/shard_map/score/ppermute | solution.py:397
  5.7 27.4 %collective-permute-start.1 = (bf16[256,2048]{1,0:T(8,128)(2,1)}, bf16[256,2048]{1,0:T(8,128)(2,1)S(1)}, u32[]{:S(2)}, u32[]{:S(2)}) collective-permute-start(bf16[256,2048]{1,0:T(8,128)(2,1)} %refs_0_.1), channel_id=1, source_target_pairs={{2,0},{3,1},{4,2},{5,3},{6,4},{7,5},{10,8},{11,9},{12,10},{13,11},... | collective-permute-start | bytes 3145736 | tf_op jit(solution)/shard_map/score/ppermute | solution.py:398
  33.1 5.3 %collective-permute-start.5 = (bf16[256,2048]{1,0:T(8,128)(2,1)S(1)}, bf16[256,2048]{1,0:T(8,128)(2,1)S(1)}, u32[]{:S(2)}, u32[]{:S(2)}) collective-permute-start(bf16[256,2048]{1,0:T(8,128)(2,1)S(1)} %collective-permute-done.refs_0_), channel_id=1, source_target_pairs={{0,1},{1,0},{2,3},{3,2},{4,5},{5,4},{6,7},{7,6},{8,9},{9,8},{10,11... | collective-permute-start | bytes 3145736 | tf_op jit(solution)/shard_map/score/ppermute | solution.py:405
  33.1 5.3 %collective-permute-start.6 = (bf16[256,2048]{1,0:T(8,128)(2,1)S(1)}, bf16[256,2048]{1,0:T(8,128)(2,1)S(1)}, u32[]{:S(2)}, u32[]{:S(2)}) collective-permute-start(bf16[256,2048]{1,0:T(8,128)(2,1)S(1)} %collective-permute-done.1.refs_1_), channel_id=1, source_target_pairs={{0,1},{1,0},{2,3},{3,2},{4,5},{5,4},{6,7},{7,6},{8,9},{9,8},{10,11... | collective-permute-start | bytes 3145736 | tf_op jit(solution)/shard_map/score/ppermute | solution.py:406
  33.6 26.0 %collective-permute-start.3 = (bf16[256,2048]{1,0:T(8,128)(2,1)S(1)}, bf16[256,2048]{1,0:T(8,128)(2,1)S(1)}, u32[]{:S(2)}, u32[]{:S(2)}) collective-permute-start(bf16[256,2048]{1,0:T(8,128)(2,1)S(1)} %collective-permute-done.refs_0_), channel_id=1, source_target_pairs={{0,2},{1,3},{2,4},{3,5},{4,6},{5,7},{8,10},{9,11},{10,12},{11,13},... | collective-permute-start | bytes 3145736 | tf_op jit(solution)/shard_map/score/ppermute | solution.py:397
  37.1 26.7 %collective-permute-start.4 = (bf16[256,2048]{1,0:T(8,128)(2,1)S(1)}, bf16[256,2048]{1,0:T(8,128)(2,1)S(1)}, u32[]{:S(2)}, u32[]{:S(2)}) collective-permute-start(bf16[256,2048]{1,0:T(8,128)(2,1)S(1)} %collective-permute-done.1.refs_1_), channel_id=1, source_target_pairs={{2,0},{3,1},{4,2},{5,3},{6,4},{7,5},{10,8},{11,9},{12,10},{13,11},... | collective-permute-start | bytes 3145736 | tf_op jit(solution)/shard_map/score/ppermute | solution.py:398
  63.8 5.3 %collective-permute-start.10 = (bf16[256,2048]{1,0:T(8,128)(2,1)S(1)}, bf16[256,2048]{1,0:T(8,128)(2,1)S(1)}, u32[]{:S(2)}, u32[]{:S(2)}) collective-permute-start(bf16[256,2048]{1,0:T(8,128)(2,1)S(1)} %collective-permute-done.4.refs_1_), channel_id=1, source_target_pairs={{0,1},{1,0},{2,3},{3,2},{4,5},{5,4},{6,7},{7,6},{8,9},{9,8},{10,11... | collective-permute-start | bytes 3145736 | tf_op jit(solution)/shard_map/score/ppermute | solution.py:406
  63.8 5.3 %collective-permute-start.9 = (bf16[256,2048]{1,0:T(8,128)(2,1)S(1)}, bf16[256,2048]{1,0:T(8,128)(2,1)S(1)}, u32[]{:S(2)}, u32[]{:S(2)}) collective-permute-start(bf16[256,2048]{1,0:T(8,128)(2,1)S(1)} %collective-permute-done.3.refs_0_), channel_id=1, source_target_pairs={{0,1},{1,0},{2,3},{3,2},{4,5},{5,4},{6,7},{7,6},{8,9},{9,8},{10,11... | collective-permute-start | bytes 3145736 | tf_op jit(solution)/shard_map/score/ppermute | solution.py:405
  64.3 26.0 %collective-permute-start.7 = (bf16[256,2048]{1,0:T(8,128)(2,1)S(1)}, bf16[256,2048]{1,0:T(8,128)(2,1)S(1)}, u32[]{:S(2)}, u32[]{:S(2)}) collective-permute-start(bf16[256,2048]{1,0:T(8,128)(2,1)S(1)} %collective-permute-done.3.refs_0_), channel_id=1, source_target_pairs={{0,2},{1,3},{2,4},{3,5},{4,6},{5,7},{8,10},{9,11},{10,12},{11,13},... | collective-permute-start | bytes 3145736 | tf_op jit(solution)/shard_map/score/ppermute | solution.py:397
  67.8 26.7 %collective-permute-start.8 = (bf16[256,2048]{1,0:T(8,128)(2,1)S(1)}, bf16[256,2048]{1,0:T(8,128)(2,1)S(1)}, u32[]{:S(2)}, u32[]{:S(2)}) collective-permute-start(bf16[256,2048]{1,0:T(8,128)(2,1)S(1)} %collective-permute-done.4.refs_1_), channel_id=1, source_target_pairs={{2,0},{3,1},{4,2},{5,3},{6,4},{7,5},{10,8},{11,9},{12,10},{13,11},... | collective-permute-start | bytes 3145736 | tf_op jit(solution)/shard_map/score/ppermute | solution.py:398
  94.5 2.7 %collective-permute-start.11 = (bf16[256,2048]{1,0:T(8,128)(2,1)S(1)}, bf16[256,2048]{1,0:T(8,128)(2,1)S(1)}, u32[]{:S(2)}, u32[]{:S(2)}) collective-permute-start(bf16[256,2048]{1,0:T(8,128)(2,1)S(1)} %collective-permute-done.7.refs_0_), channel_id=1, source_target_pairs={{0,1},{1,0},{2,3},{3,2},{4,5},{5,4},{6,7},{7,6},{8,9},{9,8},{10,11... | collective-permute-start | bytes 3145736 | tf_op jit(solution)/shard_map/score/ppermute | solution.py:405
  94.5 4.2 %collective-permute-start.12 = (bf16[256,2048]{1,0:T(8,128)(2,1)S(1)}, bf16[256,2048]{1,0:T(8,128)(2,1)S(1)}, u32[]{:S(2)}, u32[]{:S(2)}) collective-permute-start(bf16[256,2048]{1,0:T(8,128)(2,1)S(1)} %collective-permute-done.8.refs_1_), channel_id=1, source_target_pairs={{0,1},{1,0},{2,3},{3,2},{4,5},{5,4},{6,7},{7,6},{8,9},{9,8},{10,11... | collective-permute-start | bytes 3145736 | tf_op jit(solution)/shard_map/score/ppermute | solution.py:406
  104.3 1.2 collective-permute-start.13
  105.7 3.8 %collective-permute-start.14 = (f32[2,8,256]{2,0,1:T(2,128)S(1)}, f32[2,8,256]{2,0,1:T(2,128)S(1)}, u32[]{:S(2)}, u32[]{:S(2)}) collective-permute-start(f32[2,8,256]{2,0,1:T(2,128)S(1)} %pad_maximum_fusion.1), channel_id=1, source_target_pairs={{0,2},{1,3},{2,0},{3,1},{4,6},{5,7},{6,4},{7,5},{8,10},{9,11},{10,... | collective-permute-start | bytes 49160 | tf_op jit(solution)/shard_map/softmax_total/ppermute | solution.py:424
  109.5 4.7 %collective-permute-start.15 = (f32[2,8,256]{2,0,1:T(2,128)S(1)}, f32[2,8,256]{2,0,1:T(2,128)S(1)}, u32[]{:S(2)}, u32[]{:S(2)}) collective-permute-start(f32[2,8,256]{2,0,1:T(2,128)S(1)} %pad_maximum_fusion.2), channel_id=1, source_target_pairs={{0,4},{1,5},{2,6},{3,7},{4,0},{5,1},{6,2},{7,3},{8,12},{9,13},{10,... | collective-permute-start | bytes 49160 | tf_op jit(solution)/shard_map/softmax_total/ppermute | solution.py:424
  149.7 3.0 %collective-permute-start.16 = (bf16[16,272,128]{2,1,0:T(8,128)(2,1)}, bf16[16,272,128]{2,1,0:T(8,128)(2,1)S(1)}, u32[]{:S(2)}, u32[]{:S(2)}) collective-permute-start(bf16[16,272,128]{2,1,0:T(8,128)(2,1)} %get-tuple-element.95), channel_id=1, source_target_pairs={{0,1},{1,0},{2,3},{3,2},{4,5},{5,4},{6,7},{7,6},{8,9},{9,8},{10,11... | collective-permute-start | bytes 3342344 | tf_op jit(solution)/shard_map/brick_sums/ppermute | solution.py:449
  154.3 9.6 %collective-permute-start.17 = (bf16[4,272,128]{2,1,0:T(8,128)(2,1)S(1)}, bf16[4,272,128]{2,1,0:T(8,128)(2,1)S(1)}, u32[]{:S(2)}, u32[]{:S(2)}) collective-permute-start(bf16[4,272,128]{2,1,0:T(8,128)(2,1)S(1)} %get-tuple-element.98), channel_id=1, source_target_pairs={{0,8},{8,0},{16,24},{24,16},{1,9},{9,1},{17,25},{25,17},{2,10},{10... | collective-permute-start | bytes 835592 | tf_op jit(solution)/shard_map/brick_sums/ppermute | solution.py:446
  155.9 14.4 %collective-permute-start.18 = (bf16[4,272,128]{2,1,0:T(8,128)(2,1)S(1)}, bf16[4,272,128]{2,1,0:T(8,128)(2,1)S(1)}, u32[]{:S(2)}, u32[]{:S(2)}) collective-permute-start(bf16[4,272,128]{2,1,0:T(8,128)(2,1)S(1)} %get-tuple-element.100), channel_id=1, source_target_pairs={{0,16},{8,24},{16,0},{24,8},{1,17},{9,25},{17,1},{25,9},{2,18},{10... | collective-permute-start | bytes 835592 | tf_op jit(solution)/shard_map/brick_sums/ppermute | solution.py:446
  157.4 12.9 %collective-permute-start.19 = (bf16[4,272,128]{2,1,0:T(8,128)(2,1)S(1)}, bf16[4,272,128]{2,1,0:T(8,128)(2,1)S(1)}, u32[]{:S(2)}, u32[]{:S(2)}) collective-permute-start(bf16[4,272,128]{2,1,0:T(8,128)(2,1)S(1)} %get-tuple-element.99), channel_id=1, source_target_pairs={{0,24},{8,16},{16,8},{24,0},{1,25},{9,17},{17,9},{25,1},{2,26},{10... | collective-permute-start | bytes 835592 | tf_op jit(solution)/shard_map/brick_sums/ppermute | solution.py:446
  170.4 4.5 %collective-permute-start.20 = (bf16[272,128]{1,0:T(8,128)(2,1)S(1)}, bf16[272,128]{1,0:T(8,128)(2,1)S(1)}, u32[]{:S(2)}, u32[]{:S(2)}) collective-permute-start(bf16[272,128]{1,0:T(8,128)(2,1)S(1)} %get-tuple-element.101), channel_id=1, source_target_pairs={{0,2},{1,3},{2,0},{3,1},{4,6},{5,7},{6,4},{7,5},{8,10},{9,11},{10,... | collective-permute-start | bytes 208904 | tf_op jit(solution)/shard_map/brick_sums/ppermute | solution.py:446
  170.5 7.9 %collective-permute-start.21 = (bf16[272,128]{1,0:T(8,128)(2,1)S(1)}, bf16[272,128]{1,0:T(8,128)(2,1)S(1)}, u32[]{:S(2)}, u32[]{:S(2)}) collective-permute-start(bf16[272,128]{1,0:T(8,128)(2,1)S(1)} %get-tuple-element.103), channel_id=1, source_target_pairs={{0,4},{1,5},{2,6},{3,7},{4,0},{5,1},{6,2},{7,3},{8,12},{9,13},{10,... | collective-permute-start | bytes 208904 | tf_op jit(solution)/shard_map/brick_sums/ppermute | solution.py:446
  170.6 7.8 %collective-permute-start.22 = (bf16[272,128]{1,0:T(8,128)(2,1)S(1)}, bf16[272,128]{1,0:T(8,128)(2,1)S(1)}, u32[]{:S(2)}, u32[]{:S(2)}) collective-permute-start(bf16[272,128]{1,0:T(8,128)(2,1)S(1)} %get-tuple-element.102), channel_id=1, source_target_pairs={{0,6},{1,7},{2,4},{3,5},{4,2},{5,3},{6,0},{7,1},{8,14},{9,15},{10,... | collective-permute-start | bytes 208904 | tf_op jit(solution)/shard_map/brick_sums/ppermute | solution.py:446
  (3 other events, 18.5 us)

commit v3 on v2

--- a/solution.py
+++ b/solution.py
@@ -24,8 +24,9 @@
 
 
 def one_hot_rows(count, row):
-    numbers = lax.broadcasted_iota(jnp.int32, (count, row.shape[1]), 0)
-    return jnp.where(numbers == row, 1.0, 0.0).astype(jnp.bfloat16)
+    numbers = lax.broadcasted_iota(jnp.int32, (count, row.shape[1]), 0).astype(jnp.bfloat16)
+    one, zero = jnp.ones((), jnp.bfloat16), jnp.zeros((), jnp.bfloat16)
+    return jnp.where(numbers == row.astype(jnp.bfloat16), one, zero)
 
 
 def place_kernel(bricks, groups, capacity, dest_ref, rows_ref, slot_ref, map_ref):
@@ -77,14 +78,15 @@
     p_hbm, x_hbm, stat_hbm, held, p_buf, stat_buf, sem_in, sem_p, sem_x, sem_s = refs
     block = held.shape[1]
     orients = proj_ref.shape[0]
-    chunk = min(256, orients)
+    chunk = min(512, orients)
     me = lax.axis_index("ori")
     chip, core = me // 2, lax.rem(me, 2)
     plan = []
-    for shift, other in candidates:
-        source = chip + shift
+    for distance, direct, own in candidates:
+        below = (core == 0) if direct else (core == 1)
+        source = chip + jnp.where(below, -distance, distance)
         valid = jnp.logical_and(source >= 0, source < chips)
-        plan.append((valid, jnp.clip(source, 0, chips - 1) * 2 + (1 - core if other else core)))
+        plan.append((valid, jnp.clip(source, 0, chips - 1) * 2 + (core if own else 1 - core)))
 
     def copies(i):
         slot = plan[i][1]
@@ -159,7 +161,7 @@
     block, width = images[0].shape
     orients = projections.shape[0]
     blocks = 2 * chips
-    n = len(images)
+    n = len(candidates)
     first = carry is None
     shapes = [
         jax.ShapeDtypeStruct((blocks, orients, block), jnp.float32),
@@ -192,13 +194,32 @@
             pltpu.SemaphoreType.DMA((n,)),
         ],
         input_output_aliases=aliases,
-        compiler_params=pltpu.CompilerParams(vmem_limit_bytes=40 << 20),
-        cost_estimate=pl.CostEstimate(
-            flops=2 * n * block * orients * width, bytes_accessed=n * (4 << 20), transcendentals=0
-        ),
+        compiler_params=pltpu.CompilerParams(vmem_limit_bytes=20 << 20),
+        cost_estimate=pl.CostEstimate(flops=1000, bytes_accessed=1000, transcendentals=0),
         name="score_blocks",
     )(*args)
     return tuple(out) if first else (carry[0],) + tuple(out)
+
+
+def merge_kernel(a_ref, b_ref, out_ref):
+    for k in range(a_ref.shape[0]):
+        a, b = a_ref[k], b_ref[k]
+        largest = jnp.maximum(a[0:1], b[0:1])
+        total = a[1:2] * jnp.exp(a[0:1] - largest) + b[1:2] * jnp.exp(b[0:1] - largest)
+        pick = lax.broadcasted_iota(jnp.int32, a.shape, 0) == 0
+        out_ref[k] = jnp.where(pick, largest, total)
+
+
+def merge_step(a, b):
+    return pl.pallas_call(
+        merge_kernel,
+        out_shape=jax.ShapeDtypeStruct(a.shape, a.dtype),
+        in_specs=[VMEM, VMEM],
+        out_specs=VMEM,
+        compiler_params=pltpu.CompilerParams(vmem_limit_bytes=4 << 20),
+        cost_estimate=pl.CostEstimate(flops=1000, bytes_accessed=1000, transcendentals=0),
+        name="merge_totals",
+    )(a, b)
 
 
 def sum_kernel(
@@ -206,7 +227,8 @@
     capacity,
     slot_ref,
     p_ref,
-    scale_ref,
+    stats_ref,
+    totals_ref,
     x_ref,
     dest_ref,
     rows_ref,
@@ -219,28 +241,22 @@
     slots,
     volume,
 ):
-    g = pl.program_id(0)
-    groups = pl.num_programs(0)
-    blocks, owned, block = p_ref.shape
+    blocks, orients, block = p_ref.shape
+    owned = dest_ref.shape[2]
+    groups = orients // owned
     segments = dest_ref.shape[0] // groups
     per_tile = TILE // 128
     tiles = segments // per_tile
     span = map_ref.shape[2]
     core = lax.rem(lax.axis_index("ori"), 2)
-
-    @pl.when(g == 0)
-    def _():
-        zero = jnp.zeros((512, 128), jnp.float32)
-
-        def clear(i, ignored):
-            slots[pl.ds(pl.multiple_of(i * 512, 512), 512), :] = zero
-            return ignored
-
-        lax.fori_loop(0, slots.shape[0] // 512, clear, 0)
-        volume[...] = jnp.zeros_like(volume)
-
-    for k in range(blocks):
-        weights[:, k * block : (k + 1) * block] = (p_ref[k] * scale_ref[k]).astype(jnp.bfloat16)
+    zero = jnp.zeros((512, 128), jnp.float32)
+
+    def clear(i, ignored):
+        slots[pl.ds(pl.multiple_of(i * 512, 512), 512), :] = zero
+        return ignored
+
+    lax.fori_loop(0, slots.shape[0] // 512, clear, 0)
+    volume[...] = jnp.zeros_like(volume)
 
     def scatter(held, base):
         for s in range(per_tile):
@@ -254,85 +270,83 @@
         columns = pl.ds(pl.multiple_of(t * TILE, TILE), TILE)
         return dot(weights[...], x_ref[:, columns])
 
-    ones = jnp.ones((8, blocks * block), jnp.bfloat16)
-    sums = dot(ones, weights[...], NT)[0:1]
-    high = sums.astype(jnp.bfloat16).astype(jnp.float32)
-    low = sums - high
-
-    def weigh(s):
-        dest = dest_ref[g * segments + s]
-        member = lax.broadcasted_iota(jnp.int32, (bricks, owned), 0) == dest
-        parts = [jnp.where(member, part, 0.0).astype(jnp.bfloat16) for part in (high, low)]
-        return jnp.concatenate(parts, axis=0), one_hot_rows(BRICK_ROWS, rows_ref[g * segments + s])
-
-    def pair(j, ignored):
-        both = [weigh(2 * j * per_tile + k) for k in range(2 * per_tile)]
-        carried = jnp.concatenate([first for first, _ in both], axis=1)
-        landed = jnp.concatenate([second for _, second in both], axis=1)
-        volume[...] += dot(carried, landed, NT)
-        base = (g * segments + 2 * j * per_tile) * owned
-        even[...] = product(2 * j)
-        scatter(odd, base)
-        odd[...] = product(2 * j + 1)
-        scatter(even, base + per_tile * owned)
+    def group(g, ignored):
+        rows = pl.ds(pl.multiple_of(g * owned, owned), owned)
+        for k in range(blocks):
+            scale = jnp.exp(stats_ref[k, 0:1] - totals_ref[k, 0:1]) / totals_ref[k, 1:2]
+            weights[:, k * block : (k + 1) * block] = (p_ref[k, rows, :] * scale).astype(
+                jnp.bfloat16
+            )
+        ones = jnp.ones((8, blocks * block), jnp.bfloat16)
+        sums = dot(ones, weights[...], NT)[0:1]
+        high = sums.astype(jnp.bfloat16).astype(jnp.float32)
+        low = sums - high
+
+        def weigh(s):
+            dest = dest_ref[g * segments + s]
+            member = lax.broadcasted_iota(jnp.int32, (bricks, owned), 0) == dest
+            parts = [jnp.where(member, part, 0.0).astype(jnp.bfloat16) for part in (high, low)]
+            landed = one_hot_rows(BRICK_ROWS, rows_ref[g * segments + s])
+            return jnp.concatenate(parts, axis=0), landed
+
+        def pair(j, ignored):
+            both = [weigh(2 * j * per_tile + k) for k in range(2 * per_tile)]
+            carried = jnp.concatenate([first for first, _ in both], axis=1)
+            landed = jnp.concatenate([second for _, second in both], axis=1)
+            volume[...] += dot(carried, landed, NT)
+            base = (g * segments + 2 * j * per_tile) * owned
+            even[...] = product(2 * j)
+            scatter(odd, base)
+            odd[...] = product(2 * j + 1)
+            scatter(even, base + per_tile * owned)
+            return ignored
+
+        return lax.fori_loop(0, tiles // 2, pair, ignored)
+
+    lax.fori_loop(0, groups, group, 0)
+    scatter(odd, groups * segments * owned)
+    sub = lax.broadcasted_iota(jnp.int32, (EXTRA_ROWS, 128), 0)
+    unroll = 8
+
+    def grid_brick(i, out_ref, parity):
+        b = 2 * i + parity
+        values = slots[pl.ds(pl.multiple_of(b * span, 8), span), :].astype(jnp.bfloat16)
+        cells = dot(one_hot_rows(BRICK_ROWS, map_ref[b]), values)
+        out_ref[i, 0:BRICK_ROWS, :] = cells.astype(out_ref.dtype)
+        total = volume[pl.ds(b, 1), :] + volume[pl.ds(bricks + b, 1), :]
+        top = total.astype(jnp.bfloat16).astype(jnp.float32)
+        rest = total - top
+        extra = jnp.where(sub == 0, top[:, :128], jnp.where(sub == 1, top[:, 128:], 0.0))
+        extra += jnp.where(sub == 2, rest[:, :128], jnp.where(sub == 3, rest[:, 128:], 0.0))
+        out_ref[i, BRICK_ROWS : BRICK_ROWS + EXTRA_ROWS, :] = extra.astype(out_ref.dtype)
+
+    def others(i, ignored):
+        for k in range(unroll):
+            grid_brick(i * unroll + k, other_ref, 1 - core)
         return ignored
 
-    lax.fori_loop(0, tiles // 2, pair, 0)
-
-    @pl.when(g == groups - 1)
-    def _():
-        scatter(odd, groups * segments * owned)
-        sub = lax.broadcasted_iota(jnp.int32, (EXTRA_ROWS, 128), 0)
-        unroll = 8
-
-        def grid_brick(i, out_ref, parity):
-            b = 2 * i + parity
-            values = slots[pl.ds(pl.multiple_of(b * span, 8), span), :].astype(jnp.bfloat16)
-            cells = dot(one_hot_rows(BRICK_ROWS, map_ref[b]), values)
-            out_ref[i, 0:BRICK_ROWS, :] = cells.astype(jnp.bfloat16)
-            total = volume[pl.ds(b, 1), :] + volume[pl.ds(bricks + b, 1), :]
-            top = total.astype(jnp.bfloat16).astype(jnp.float32)
-            rest = total - top
-            extra = jnp.where(sub == 0, top[:, :128], jnp.where(sub == 1, top[:, 128:], 0.0))
-            extra += jnp.where(sub == 2, rest[:, :128], jnp.where(sub == 3, rest[:, 128:], 0.0))
-            out_ref[i, BRICK_ROWS : BRICK_ROWS + EXTRA_ROWS, :] = extra.astype(jnp.bfloat16)
-
-        def others(i, ignored):
-            for k in range(unroll):
-                grid_brick(i * unroll + k, other_ref, 1 - core)
-            return ignored
-
-        def own(i, ignored):
-            for k in range(unroll):
-                grid_brick(i * unroll + k, mine_ref, core)
-            return ignored
-
-        lax.fori_loop(0, bricks // 2 // unroll, others, 0)
-        lax.fori_loop(0, bricks // 2 // unroll, own, 0)
-
-
-def sum_step(bricks, groups, capacity, slot, p, scale, x, dest, rows, row_map):
+    def own(i, ignored):
+        for k in range(unroll):
+            grid_brick(i * unroll + k, mine_ref, core)
+        return ignored
+
+    lax.fori_loop(0, bricks // 2 // unroll, others, 0)
+    lax.fori_loop(0, bricks // 2 // unroll, own, 0)
+
+
+def sum_step(bricks, groups, capacity, slot, p, stats, totals, x, dest, rows, row_map):
     blocks, orients, block = p.shape
     width = x.shape[1]
     owned = orients // groups
-    whole = lambda a: pl.BlockSpec(
-        a.shape, lambda g: (0,) * a.ndim, pipeline_mode=pl.Buffered(1)
-    )
-    out = jax.ShapeDtypeStruct((bricks // 2, BRICK_ROWS + EXTRA_ROWS, 128), jnp.bfloat16)
+    shape = (bricks // 2, BRICK_ROWS + EXTRA_ROWS, 128)
     return pl.pallas_call(
         functools.partial(sum_kernel, bricks, capacity),
-        grid=(groups,),
-        out_shape=[out, out],
-        in_specs=[
-            SMEM,
-            pl.BlockSpec((blocks, owned, block), lambda g: (0, g, 0)),
-            whole(scale),
-            whole(x),
-            whole(dest),
-            whole(rows),
-            whole(row_map),
+        out_shape=[
+            jax.ShapeDtypeStruct(shape, jnp.bfloat16),
+            jax.ShapeDtypeStruct(shape, jnp.float32),
         ],
-        out_specs=[whole(out), whole(out)],
+        in_specs=[SMEM] + [VMEM] * 7,
+        out_specs=[VMEM, VMEM],
         scratch_shapes=[
             pltpu.VMEM((owned, blocks * block), jnp.bfloat16),
             pltpu.VMEM((owned, TILE), jnp.float32),
@@ -340,12 +354,12 @@
             pltpu.VMEM((bricks * groups * capacity + 512, 128), jnp.float32),
             pltpu.VMEM((2 * bricks, BRICK_ROWS), jnp.float32),
         ],
-        compiler_params=pltpu.CompilerParams(vmem_limit_bytes=56 << 20),
+        compiler_params=pltpu.CompilerParams(vmem_limit_bytes=22 << 20),
         cost_estimate=pl.CostEstimate(
             flops=2 * blocks * block * orients * width, bytes_accessed=24 << 20, transcendentals=0
         ),
         name="sum_and_grid",
-    )(slot, p, scale, x, dest, rows, row_map)
+    )(slot, p, stats, totals, x, dest, rows, row_map)
 
 
 def body(images, projections, brick_dest, brick_rows, kernel):
@@ -359,8 +373,8 @@
     me = lax.axis_index("ori")
 
     swap = [(i, i ^ 1) for i in range(orient_groups)]
-    up = [(i, i + 2) for i in range(orient_groups - 2)]
-    down = [(i + 2, i) for i in range(orient_groups - 2)]
+    along = [(i, i + 2) for i in range(0, orient_groups - 2, 2)]
+    along += [(i + 2, i) for i in range(1, orient_groups - 2, 2)]
 
     with jax.named_scope("place_segments"):
 
@@ -378,6 +392,8 @@
             ],
             in_specs=[VMEM, VMEM],
             out_specs=[VMEM, VMEM],
+            compiler_params=pltpu.CompilerParams(vmem_limit_bytes=12 << 20),
+            cost_estimate=pl.CostEstimate(flops=1000, bytes_accessed=1000, transcendentals=0),
             name="place_segments",
         )(dest, rows)
         row_map = row_map[:, :, :capacity].transpose(1, 0, 2).reshape(bricks, 1, image_groups * capacity)
@@ -385,53 +401,50 @@
         placed = (jnp.concatenate([unused, slot.reshape(-1)]), row_map, dest, rows)
 
     with jax.named_scope("score"):
-        from_below = from_above = images
+        mate = lax.ppermute(images, "ori", swap)
+        moving = [images, mate]
+        mate, placed = lax.optimization_barrier((mate, placed))
         carry = score_step(
-            chips,
-            ((0, False), (0, True)),
-            (images, lax.ppermute(images, "ori", swap)),
-            projections,
-            None,
+            chips, ((0, True, True), (0, True, False)), (images, mate), projections, None
         )
+
+        def arrive(distance, q, part):
+            own = q == 0
+            both = (part, lax.ppermute(part, "ori", swap))
+            return ((distance, True, own), (distance, False, not own)), both
+
+        def score(waiting, carry):
+            return score_step(chips, waiting[0], waiting[1], projections, carry)
+
+        waiting = []
         for distance in range(1, chips):
-            from_below = lax.ppermute(from_below, "ori", up)
-            from_above = lax.ppermute(from_above, "ori", down)
-            from_below, from_above, carry, placed = lax.optimization_barrier(
-                (from_below, from_above, carry, placed)
-            )
-            arrived = (
-                from_below,
-                from_above,
-                lax.ppermute(from_below, "ori", swap),
-                lax.ppermute(from_above, "ori", swap),
-            )
-            candidates = (
-                (-distance, False),
-                (distance, False),
-                (-distance, True),
-                (distance, True),
-            )
-            carry = score_step(chips, candidates, arrived, projections, carry)
+            moving = [lax.ppermute(part, "ori", along) for part in moving]
+            for q in range(2):
+                if distance == 1:
+                    if q == 0:
+                        moving, carry = lax.optimization_barrier((moving, carry))
+                elif distance == 2 and q == 0:
+                    moving[q], carry = lax.optimization_barrier((moving[q], carry))
+                else:
+                    carry = score(waiting.pop(0), carry)
+                    moving[q], carry = lax.optimization_barrier((moving[q], carry))
+                waiting.append(arrive(distance, q, moving[q]))
+        late = [sum(parts, ()) for parts in zip(*waiting)]
+        carry = score(late, carry)
         _, p, x, stats = carry
         slot, row_map, dest, rows = placed
 
     with jax.named_scope("softmax_total"):
-        own_largest, own_total = stats[:, 0], stats[:, 1]
-        pair = jnp.stack([own_largest, own_total])
+        totals = stats
         step = 1
         while step < orient_groups:
             partner = [(i, i ^ step) for i in range(orient_groups)]
-            other = lax.ppermute(pair, "ori", partner)
-            largest = jnp.maximum(pair[0], other[0])
-            total = pair[1] * jnp.exp(pair[0] - largest) + other[1] * jnp.exp(other[0] - largest)
-            pair = jnp.stack([largest, total])
+            totals = merge_step(totals, lax.ppermute(totals, "ori", partner))
             step *= 2
-        scale = jnp.exp(own_largest - pair[0]) / pair[1]
-        scale = scale[:, None, :]
 
     with jax.named_scope("sum_and_grid"):
         other_cells, cells = sum_step(
-            bricks, image_groups, capacity, slot, p, scale, x, dest, rows, row_map
+            bricks, image_groups, capacity, slot, p, stats, totals, x, dest, rows, row_map
         )
 
     with jax.named_scope("brick_sums"):

time: 180 us -> 168 us (0.933)
  starting transfers between devices: 25.7 us -> 38.1 us
  waiting for transfers between devices: 74.6 us -> 63.3 us
  Pallas kernels: 64.7 us -> 53.6 us
    ppermute x16, waiting for transfers between devices: 55.7 us -> 41.9 us  [the longest x6 30.2 us: body(): moving = [lax.ppermute(part, 'ori', along) for part in moving]]
    ppermute x16, starting transfers between devices: 17.7 us -> 29.7 us  [the longest x6 24.8 us: body(): moving = [lax.ppermute(part, 'ori', along) for part in moving]]
    pallas_call x4 -> x5, Pallas kernels: 23.5 us -> 17.4 us  [score_step(): pl.pallas_call(functools.partial(score_kernel, chips, candidates, first),...]
    pallas_call x1 -> x4, Pallas kernels: 34.8 us -> 31.4 us  [the longest x1 31.3 us: sum_step(): pl.pallas_call(functools.partial(sum_kernel, bricks, capacity), out_shape...]
    ppermute x6, waiting for transfers between devices: 15.9 us -> 18.5 us  [add_up(): total += lax.ppermute(part, axis, perm).astype(jnp.float32)]
    unnamed x8 -> x10, local copies, waits for them, and re-layouts: 3.43 us -> 4.41 us
  transfers between devices with their start and end apart: 23 -> 23, of which waited for: 14 -> 15; matrix products, arithmetic and copies ran while one was open for 4% -> 2% of each run, Pallas kernels for 13% -> 9%
where the time goes in v3:
time: 168 us; the launch traced here: 167 us
  waiting for transfers between devices  63.3 us (38%)
  Pallas kernels  53.6 us (32%)
  starting transfers between devices  38.1 us (23%)
  local copies, waits for them, and re-layouts  7.3 us (4%)
  other arithmetic  3.21 us (2%)
    pallas_call x1, Pallas kernels, sum_step(): pl.pallas_call(functools.partial(sum_kernel, bricks, capacity), out_shape...  31.3 us
    ppermute x6, waiting for transfers between devices, body(): moving = [lax.ppermute(part, 'ori', along) for part in moving]  30.2 us
    ppermute x6, starting transfers between devices, body(): moving = [lax.ppermute(part, 'ori', along) for part in moving]  24.8 us
    ppermute x6, waiting for transfers between devices, add_up(): total += lax.ppermute(part, axis, perm).astype(jnp.float32)  18.5 us
    pallas_call x5, Pallas kernels, score_step(): pl.pallas_call(functools.partial(score_kernel, chips, candidates, first),...  17.4 us
    ppermute x6, starting transfers between devices, add_up(): total += lax.ppermute(part, axis, perm).astype(jnp.float32)  8.35 us
    ppermute x3, waiting for transfers between devices, body(): totals = merge_step(totals, lax.ppermute(totals, 'ori', partner))  7.98 us
    pallas_call x1, Pallas kernels, body(): pl.pallas_call(functools.partial(place_kernel, bricks, image_groups, capa...  4.74 us
  transfers between devices with their start and end apart: 23, of which 15 were waited for; matrix products, arithmetic and copies ran while one was open for 2% of the time, Pallas kernels for 9%

profile of v3, /device:TPU:0, one launch (start us, length us, event | category | flops | bytes accessed | tf_op | source)
XLA Modules:
  0.0 167.2 jit_solution(18071203267979905494)
XLA Ops:
  1.2 4.6 %collective-permute-start.1 = (bf16[256,2048]{1,0:T(8,128)(2,1)}, bf16[256,2048]{1,0:T(8,128)(2,1)S(1)}, u32[]{:S(2)}, u32[]{:S(2)}) collective-permute-start(bf16[256,2048]{1,0:T(8,128)(2,1)} %refs_0_.1), channel_id=1, source_target_pairs={{0,2},{2,4},{4,6},{3,1},{5,3},{7,5},{8,10},{10,12},{12,14},{11,9},... | collective-permute-start | bytes 3145736 | tf_op jit(solution)/shard_map/score/ppermute | solution.py:421
  5.7 3.5 %collective-permute-start.2 = (bf16[256,2048]{1,0:T(8,128)(2,1)S(1)}, bf16[256,2048]{1,0:T(8,128)(2,1)S(1)}, u32[]{:S(2)}, u32[]{:S(2)}) collective-permute-start(bf16[256,2048]{1,0:T(8,128)(2,1)S(1)} %collective-permute-done.refs_1_), channel_id=1, source_target_pairs={{0,2},{2,4},{4,6},{3,1},{5,3},{7,5},{8,10},{10,12},{12,14},{11,9},... | collective-permute-start | bytes 3145736 | tf_op jit(solution)/shard_map/score/ppermute | solution.py:421
  11.2 4.7 %place_segments.1 = (s32[64,1,256]{2,1,0:T(1,128)S(1)}, s32[4,32,256]{2,1,0:T(8,128)S(1)}) custom-call(s32[64,1,256]{2,1,0:T(1,128)S(1)} %reshape.33.dest_ref, s32[64,1,256]{2,1,0:T(1,128)S(1)} %reshape.35.rows_ref), custom_call_target="tpu_custom_call" | custom-call | flops 1000 | bytes 1000 | tf_op jit(solution)/shard_map/place_segments/place_segments/pallas_call | solution.py:387
  17.8 2.2 %copy-done.1 = bf16[1024,2048]{1,0:T(8,128)(2,1)S(1)} copy-done((bf16[1024,2048]{1,0:T(8,128)(2,1)S(1)}, bf16[1024,2048]{1,0:T(8,128)(2,1)}, u32[]{:S(2)}) %copy-start.1) | copy-done | bytes 4194328
  21.2 4.9 %score_blocks.5 = (f32[1024,128]{1,0:T(8,128)S(1)}, f32[8,1024,256]{2,1,0:T(8,128)S(1)}, bf16[2048,2048]{1,0:T(8,128)(2,1)S(1)}, f32[8,8,256]{2,1,0:T(8,128)S(1)}) custom-call(bf16[256,2048]{1,0:T(8,128)(2,1)S(1)} %copy-done.3, bf16[256,2048]{1,0:T(8,128)(2,1)S(1)} %collective-permute-done.refs_1_, bf16[1024,2048]{1,0:T(8,128)(2,1)S(1)} %copy-done.1), custom_call_target="tpu_custom_call" | custom-call | flops 1000 | bytes 1000 | tf_op jit(solution)/shard_map/score/score_blocks/pallas_call | solution.py:182
  26.2 3.2 %collective-permute-done.2.refs_0_ = bf16[256,2048]{1,0:T(8,128)(2,1)S(1)} collective-permute-done((bf16[256,2048]{1,0:T(8,128)(2,1)S(1)}, bf16[256,2048]{1,0:T(8,128)(2,1)S(1)}, u32[]{:S(2)}, u32[]{:S(2)}) %collective-permute-start.2) | collective-permute-done | bytes 1048608 | tf_op jit(solution)/shard_map/score/ppermute | solution.py:421
  29.4 4.4 %collective-permute-start.4 = (bf16[256,2048]{1,0:T(8,128)(2,1)S(1)}, bf16[256,2048]{1,0:T(8,128)(2,1)S(1)}, u32[]{:S(2)}, u32[]{:S(2)}) collective-permute-start(bf16[256,2048]{1,0:T(8,128)(2,1)S(1)} %collective-permute-done.1.refs_0_), channel_id=1, source_target_pairs={{0,2},{2,4},{4,6},{3,1},{5,3},{7,5},{8,10},{10,12},{12,14},{11,9},... | collective-permute-start | bytes 3145736 | tf_op jit(solution)/shard_map/score/ppermute | solution.py:421
  33.9 3.5 %collective-permute-start.3 = (bf16[256,2048]{1,0:T(8,128)(2,1)S(1)}, bf16[256,2048]{1,0:T(8,128)(2,1)S(1)}, u32[]{:S(2)}, u32[]{:S(2)}) collective-permute-start(bf16[256,2048]{1,0:T(8,128)(2,1)S(1)} %collective-permute-done.2.refs_0_), channel_id=1, source_target_pairs={{0,2},{2,4},{4,6},{3,1},{5,3},{7,5},{8,10},{10,12},{12,14},{11,9},... | collective-permute-start | bytes 3145736 | tf_op jit(solution)/shard_map/score/ppermute | solution.py:421
  37.5 8.6 %collective-permute-done.4.refs_0_ = bf16[256,2048]{1,0:T(8,128)(2,1)S(1)} collective-permute-done((bf16[256,2048]{1,0:T(8,128)(2,1)S(1)}, bf16[256,2048]{1,0:T(8,128)(2,1)S(1)}, u32[]{:S(2)}, u32[]{:S(2)}) %collective-permute-start.4) | collective-permute-done | bytes 1048608 | tf_op jit(solution)/shard_map/score/ppermute | solution.py:421
  46.1 4.4 %collective-permute-start.7 = (bf16[256,2048]{1,0:T(8,128)(2,1)S(1)}, bf16[256,2048]{1,0:T(8,128)(2,1)S(1)}, u32[]{:S(2)}, u32[]{:S(2)}) collective-permute-start(bf16[256,2048]{1,0:T(8,128)(2,1)S(1)} %collective-permute-done.4.refs_0_), channel_id=1, source_target_pairs={{0,2},{2,4},{4,6},{3,1},{5,3},{7,5},{8,10},{10,12},{12,14},{11,9},... | collective-permute-start | bytes 3145736 | tf_op jit(solution)/shard_map/score/ppermute | solution.py:421
  52.7 4.6 %collective-permute-done.3.refs_0_ = bf16[256,2048]{1,0:T(8,128)(2,1)S(1)} collective-permute-done((bf16[256,2048]{1,0:T(8,128)(2,1)S(1)}, bf16[256,2048]{1,0:T(8,128)(2,1)S(1)}, u32[]{:S(2)}, u32[]{:S(2)}) %collective-permute-start.3) | collective-permute-done | bytes 1048608 | tf_op jit(solution)/shard_map/score/ppermute | solution.py:421
  57.3 4.4 %collective-permute-start.10 = (bf16[256,2048]{1,0:T(8,128)(2,1)S(1)}, bf16[256,2048]{1,0:T(8,128)(2,1)S(1)}, u32[]{:S(2)}, u32[]{:S(2)}) collective-permute-start(bf16[256,2048]{1,0:T(8,128)(2,1)S(1)} %collective-permute-done.3.refs_0_), channel_id=1, source_target_pairs={{0,2},{2,4},{4,6},{3,1},{5,3},{7,5},{8,10},{10,12},{12,14},{11,9},... | collective-permute-start | bytes 3145736 | tf_op jit(solution)/shard_map/score/ppermute | solution.py:421
  63.9 4.6 %collective-permute-done.7.refs_2_ = bf16[256,2048]{1,0:T(8,128)(2,1)S(1)} collective-permute-done((bf16[256,2048]{1,0:T(8,128)(2,1)S(1)}, bf16[256,2048]{1,0:T(8,128)(2,1)S(1)}, u32[]{:S(2)}, u32[]{:S(2)}) %collective-permute-start.7) | collective-permute-done | bytes 1048608 | tf_op jit(solution)/shard_map/score/ppermute | solution.py:421
  70.6 9.2 %collective-permute-done.10.refs_4_ = bf16[256,2048]{1,0:T(8,128)(2,1)S(1)} collective-permute-done((bf16[256,2048]{1,0:T(8,128)(2,1)S(1)}, bf16[256,2048]{1,0:T(8,128)(2,1)S(1)}, u32[]{:S(2)}, u32[]{:S(2)}) %collective-permute-start.10) | collective-permute-done | bytes 1048608 | tf_op jit(solution)/shard_map/score/ppermute | solution.py:421
  84.0 6.3 %score_blocks.9 = (f32[8,1024,256]{2,1,0:T(8,128)S(1)}, bf16[2048,2048]{1,0:T(8,128)(2,1)S(1)}, f32[8,8,256]{2,1,0:T(8,128)S(1)}) custom-call(bf16[256,2048]{1,0:T(8,128)(2,1)S(1)} %collective-permute-done.3.refs_0_, bf16[256,2048]{1,0:T(8,128)(2,1)S(1)} %collective-permute-done.6.refs_1_, ...), custom_call_target="tpu_custom_call", output_to_operand_aliasing={{0}: (8, {}), {1}: (9, {}), {2}: (10, {})} | custom-call | flops 1000 | bytes 1000 | tf_op jit(solution)/shard_map/score/score_blocks/pallas_call | solution.py:182
  91.7 4.3 %collective-permute-done.14.b_ref = f32[8,8,256]{2,1,0:T(8,128)S(1)} collective-permute-done((f32[8,8,256]{2,1,0:T(8,128)S(1)}, f32[8,8,256]{2,1,0:T(8,128)S(1)}, u32[]{:S(2)}, u32[]{:S(2)}) %collective-permute-start.14) | collective-permute-done | bytes 65568 | tf_op jit(solution)/shard_map/softmax_total/ppermute | solution.py:442
  96.0 3.3 %collective-permute-start.15 = (f32[8,8,256]{2,1,0:T(8,128)S(1)}, f32[8,8,256]{2,1,0:T(8,128)S(1)}, u32[]{:S(2)}, u32[]{:S(2)}) collective-permute-start(f32[8,8,256]{2,1,0:T(8,128)S(1)} %merge_totals.4.a_ref), channel_id=1, source_target_pairs={{0,4},{1,5},{2,6},{3,7},{4,0},{5,1},{6,2},{7,3},{8,12},{9,13},{10,... | collective-permute-start | bytes 196616 | tf_op jit(solution)/shard_map/softmax_total/ppermute | solution.py:442
  99.3 2.6 %collective-permute-done.15.b_ref = f32[8,8,256]{2,1,0:T(8,128)S(1)} collective-permute-done((f32[8,8,256]{2,1,0:T(8,128)S(1)}, f32[8,8,256]{2,1,0:T(8,128)S(1)}, u32[]{:S(2)}, u32[]{:S(2)}) %collective-permute-start.15) | collective-permute-done | bytes 65568 | tf_op jit(solution)/shard_map/softmax_total/ppermute | solution.py:442
  101.9 31.3 %sum_and_grid.1 = (bf16[16,272,128]{2,1,0:T(8,128)(2,1)}, f32[16,272,128]{2,1,0:T(8,128)S(1)}) custom-call(s32[16896]{0:T(1024)S(1)} %concatenate.3.slot_ref, f32[8,1024,256]{2,1,0:T(8,128)S(1)} %get-tuple-element.96.p_ref, f32[8,8,256]{2,1,0:T(8,128)S(1)} %get-tuple-element.97.a_ref.stats_ref, f32[8,8,256]{2,1,0:T(8,128)S(1)} %merge_totals.5.totals_ref, ...), custom_call_target="tpu_custom_call" | custom-call | flops 8589934592 | bytes 25165824 | tf_op jit(solution)/shard_map/sum_and_grid/sum_and_grid/pallas_call | solution.py:342
  133.2 3.0 %collective-permute-done.16 = bf16[16,272,128]{2,1,0:T(8,128)(2,1)S(1)} collective-permute-done((bf16[16,272,128]{2,1,0:T(8,128)(2,1)}, bf16[16,272,128]{2,1,0:T(8,128)(2,1)S(1)}, u32[]{:S(2)}, u32[]{:S(2)}) %collective-permute-start.16) | collective-permute-done | bytes 1114144 | tf_op jit(solution)/shard_map/brick_sums/ppermute | solution.py:462
  142.3 6.0 %collective-permute-done.17 = bf16[4,272,128]{2,1,0:T(8,128)(2,1)S(1)} collective-permute-done((bf16[4,272,128]{2,1,0:T(8,128)(2,1)S(1)}, bf16[4,272,128]{2,1,0:T(8,128)(2,1)S(1)}, u32[]{:S(2)}, u32[]{:S(2)}) %collective-permute-start.17) | collective-permute-done | bytes 278560 | tf_op jit(solution)/shard_map/brick_sums/ppermute | solution.py:459
  148.3 6.4 %collective-permute-done.18 = bf16[4,272,128]{2,1,0:T(8,128)(2,1)S(1)} collective-permute-done((bf16[4,272,128]{2,1,0:T(8,128)(2,1)S(1)}, bf16[4,272,128]{2,1,0:T(8,128)(2,1)S(1)}, u32[]{:S(2)}, u32[]{:S(2)}) %collective-permute-start.18) | collective-permute-done | bytes 278560 | tf_op jit(solution)/shard_map/brick_sums/ppermute | solution.py:459
  156.4 3.2 %collective-permute-start.21 = (bf16[272,128]{1,0:T(8,128)(2,1)S(1)}, bf16[272,128]{1,0:T(8,128)(2,1)S(1)}, u32[]{:S(2)}, u32[]{:S(2)}) collective-permute-start(bf16[272,128]{1,0:T(8,128)(2,1)S(1)} %get-tuple-element.109), channel_id=1, source_target_pairs={{0,4},{1,5},{2,6},{3,7},{4,0},{5,1},{6,2},{7,3},{8,12},{9,13},{10,... | collective-permute-start | bytes 208904 | tf_op jit(solution)/shard_map/brick_sums/ppermute | solution.py:459
  159.7 4.1 %collective-permute-done.21 = bf16[272,128]{1,0:T(8,128)(2,1)S(1)} collective-permute-done((bf16[272,128]{1,0:T(8,128)(2,1)S(1)}, bf16[272,128]{1,0:T(8,128)(2,1)S(1)}, u32[]{:S(2)}, u32[]{:S(2)}) %collective-permute-start.21) | collective-permute-done | bytes 69664 | tf_op jit(solution)/shard_map/brick_sums/ppermute | solution.py:459
  (57 shorter events, 28.9 us)
Async XLA Ops:
  0.6 165.7 %copy-start = (bf16[1,128,128]{2,1,0:T(8,128)(2,1)S(1)}, bf16[1,128,128]{2,1,0:T(8,128)(2,1)}, u32[]{:S(2)}) copy-start(bf16[1,128,128]{2,1,0:T(8,128)(2,1)} %param.9) | copy-start | bytes 98308
  0.6 5.1 %collective-permute-start = (bf16[256,2048]{1,0:T(8,128)(2,1)}, bf16[256,2048]{1,0:T(8,128)(2,1)S(1)}, u32[]{:S(2)}, u32[]{:S(2)}) collective-permute-start(bf16[256,2048]{1,0:T(8,128)(2,1)} %refs_0_.1), channel_id=1, source_target_pairs={{0,1},{1,0},{2,3},{3,2},{4,5},{5,4},{6,7},{7,6},{8,9},{9,8},{10,11... | collective-permute-start | bytes 3145736 | tf_op jit(solution)/shard_map/score/ppermute | solution.py:404
  1.2 25.0 %collective-permute-start.1 = (bf16[256,2048]{1,0:T(8,128)(2,1)}, bf16[256,2048]{1,0:T(8,128)(2,1)S(1)}, u32[]{:S(2)}, u32[]{:S(2)}) collective-permute-start(bf16[256,2048]{1,0:T(8,128)(2,1)} %refs_0_.1), channel_id=1, source_target_pairs={{0,2},{2,4},{4,6},{3,1},{5,3},{7,5},{8,10},{10,12},{12,14},{11,9},... | collective-permute-start | bytes 3145736 | tf_op jit(solution)/shard_map/score/ppermute | solution.py:421
  5.7 23.7 %collective-permute-start.2 = (bf16[256,2048]{1,0:T(8,128)(2,1)S(1)}, bf16[256,2048]{1,0:T(8,128)(2,1)S(1)}, u32[]{:S(2)}, u32[]{:S(2)}) collective-permute-start(bf16[256,2048]{1,0:T(8,128)(2,1)S(1)} %collective-permute-done.refs_1_), channel_id=1, source_target_pairs={{0,2},{2,4},{4,6},{3,1},{5,3},{7,5},{8,10},{10,12},{12,14},{11,9},... | collective-permute-start | bytes 3145736 | tf_op jit(solution)/shard_map/score/ppermute | solution.py:421
  29.4 16.7 %collective-permute-start.4 = (bf16[256,2048]{1,0:T(8,128)(2,1)S(1)}, bf16[256,2048]{1,0:T(8,128)(2,1)S(1)}, u32[]{:S(2)}, u32[]{:S(2)}) collective-permute-start(bf16[256,2048]{1,0:T(8,128)(2,1)S(1)} %collective-permute-done.1.refs_0_), channel_id=1, source_target_pairs={{0,2},{2,4},{4,6},{3,1},{5,3},{7,5},{8,10},{10,12},{12,14},{11,9},... | collective-permute-start | bytes 3145736 | tf_op jit(solution)/shard_map/score/ppermute | solution.py:421
  33.9 16.8 %collective-permute-start.5 = (bf16[256,2048]{1,0:T(8,128)(2,1)S(1)}, bf16[256,2048]{1,0:T(8,128)(2,1)S(1)}, u32[]{:S(2)}, u32[]{:S(2)}) collective-permute-start(bf16[256,2048]{1,0:T(8,128)(2,1)S(1)} %collective-permute-done.1.refs_0_), channel_id=1, source_target_pairs={{0,1},{1,0},{2,3},{3,2},{4,5},{5,4},{6,7},{7,6},{8,9},{9,8},{10,11... | collective-permute-start | bytes 3145736 | tf_op jit(solution)/shard_map/score/ppermute | solution.py:413
  33.9 23.4 %collective-permute-start.3 = (bf16[256,2048]{1,0:T(8,128)(2,1)S(1)}, bf16[256,2048]{1,0:T(8,128)(2,1)S(1)}, u32[]{:S(2)}, u32[]{:S(2)}) collective-permute-start(bf16[256,2048]{1,0:T(8,128)(2,1)S(1)} %collective-permute-done.2.refs_0_), channel_id=1, source_target_pairs={{0,2},{2,4},{4,6},{3,1},{5,3},{7,5},{8,10},{10,12},{12,14},{11,9},... | collective-permute-start | bytes 3145736 | tf_op jit(solution)/shard_map/score/ppermute | solution.py:421
  37.4 24.4 %collective-permute-start.8 = (bf16[256,2048]{1,0:T(8,128)(2,1)S(1)}, bf16[256,2048]{1,0:T(8,128)(2,1)S(1)}, u32[]{:S(2)}, u32[]{:S(2)}) collective-permute-start(bf16[256,2048]{1,0:T(8,128)(2,1)S(1)} %collective-permute-done.2.refs_0_), channel_id=1, source_target_pairs={{0,1},{1,0},{2,3},{3,2},{4,5},{5,4},{6,7},{7,6},{8,9},{9,8},{10,11... | collective-permute-start | bytes 3145736 | tf_op jit(solution)/shard_map/score/ppermute | solution.py:413
  46.1 22.5 %collective-permute-start.7 = (bf16[256,2048]{1,0:T(8,128)(2,1)S(1)}, bf16[256,2048]{1,0:T(8,128)(2,1)S(1)}, u32[]{:S(2)}, u32[]{:S(2)}) collective-permute-start(bf16[256,2048]{1,0:T(8,128)(2,1)S(1)} %collective-permute-done.4.refs_0_), channel_id=1, source_target_pairs={{0,2},{2,4},{4,6},{3,1},{5,3},{7,5},{8,10},{10,12},{12,14},{11,9},... | collective-permute-start | bytes 3145736 | tf_op jit(solution)/shard_map/score/ppermute | solution.py:421
  50.5 18.0 %collective-permute-start.11 = (bf16[256,2048]{1,0:T(8,128)(2,1)S(1)}, bf16[256,2048]{1,0:T(8,128)(2,1)S(1)}, u32[]{:S(2)}, u32[]{:S(2)}) collective-permute-start(bf16[256,2048]{1,0:T(8,128)(2,1)S(1)} %collective-permute-done.4.refs_0_), channel_id=1, source_target_pairs={{0,1},{1,0},{2,3},{3,2},{4,5},{5,4},{6,7},{7,6},{8,9},{9,8},{10,11... | collective-permute-start | bytes 3145736 | tf_op jit(solution)/shard_map/score/ppermute | solution.py:413
  57.3 22.5 %collective-permute-start.10 = (bf16[256,2048]{1,0:T(8,128)(2,1)S(1)}, bf16[256,2048]{1,0:T(8,128)(2,1)S(1)}, u32[]{:S(2)}, u32[]{:S(2)}) collective-permute-start(bf16[256,2048]{1,0:T(8,128)(2,1)S(1)} %collective-permute-done.3.refs_0_), channel_id=1, source_target_pairs={{0,2},{2,4},{4,6},{3,1},{5,3},{7,5},{8,10},{10,12},{12,14},{11,9},... | collective-permute-start | bytes 3145736 | tf_op jit(solution)/shard_map/score/ppermute | solution.py:421
  61.8 18.5 %collective-permute-start.6 = (bf16[256,2048]{1,0:T(8,128)(2,1)S(1)}, bf16[256,2048]{1,0:T(8,128)(2,1)S(1)}, u32[]{:S(2)}, u32[]{:S(2)}) collective-permute-start(bf16[256,2048]{1,0:T(8,128)(2,1)S(1)} %collective-permute-done.3.refs_0_), channel_id=1, source_target_pairs={{0,1},{1,0},{2,3},{3,2},{4,5},{5,4},{6,7},{7,6},{8,9},{9,8},{10,11... | collective-permute-start | bytes 3145736 | tf_op jit(solution)/shard_map/score/ppermute | solution.py:413
  79.8 2.7 %collective-permute-start.12 = (bf16[256,2048]{1,0:T(8,128)(2,1)S(1)}, bf16[256,2048]{1,0:T(8,128)(2,1)S(1)}, u32[]{:S(2)}, u32[]{:S(2)}) collective-permute-start(bf16[256,2048]{1,0:T(8,128)(2,1)S(1)} %collective-permute-done.10.refs_4_), channel_id=1, source_target_pairs={{0,1},{1,0},{2,3},{3,2},{4,5},{5,4},{6,7},{7,6},{8,9},{9,8},{10,11... | collective-permute-start | bytes 3145736 | tf_op jit(solution)/shard_map/score/ppermute | solution.py:413
  79.8 4.2 %collective-permute-start.9 = (bf16[256,2048]{1,0:T(8,128)(2,1)S(1)}, bf16[256,2048]{1,0:T(8,128)(2,1)S(1)}, u32[]{:S(2)}, u32[]{:S(2)}) collective-permute-start(bf16[256,2048]{1,0:T(8,128)(2,1)S(1)} %collective-permute-done.7.refs_2_), channel_id=1, source_target_pairs={{0,1},{1,0},{2,3},{3,2},{4,5},{5,4},{6,7},{7,6},{8,9},{9,8},{10,11... | collective-permute-start | bytes 3145736 | tf_op jit(solution)/shard_map/score/ppermute | solution.py:413
  90.3 1.3 collective-permute-start.13
  91.6 4.3 %collective-permute-start.14 = (f32[8,8,256]{2,1,0:T(8,128)S(1)}, f32[8,8,256]{2,1,0:T(8,128)S(1)}, u32[]{:S(2)}, u32[]{:S(2)}) collective-permute-start(f32[8,8,256]{2,1,0:T(8,128)S(1)} %merge_totals.3.a_ref), channel_id=1, source_target_pairs={{0,2},{1,3},{2,0},{3,1},{4,6},{5,7},{6,4},{7,5},{8,10},{9,11},{10,... | collective-permute-start | bytes 196616 | tf_op jit(solution)/shard_map/softmax_total/ppermute | solution.py:442
  96.0 5.9 %collective-permute-start.15 = (f32[8,8,256]{2,1,0:T(8,128)S(1)}, f32[8,8,256]{2,1,0:T(8,128)S(1)}, u32[]{:S(2)}, u32[]{:S(2)}) collective-permute-start(f32[8,8,256]{2,1,0:T(8,128)S(1)} %merge_totals.4.a_ref), channel_id=1, source_target_pairs={{0,4},{1,5},{2,6},{3,7},{4,0},{5,1},{6,2},{7,3},{8,12},{9,13},{10,... | collective-permute-start | bytes 196616 | tf_op jit(solution)/shard_map/softmax_total/ppermute | solution.py:442
  133.2 3.0 %collective-permute-start.16 = (bf16[16,272,128]{2,1,0:T(8,128)(2,1)}, bf16[16,272,128]{2,1,0:T(8,128)(2,1)S(1)}, u32[]{:S(2)}, u32[]{:S(2)}) collective-permute-start(bf16[16,272,128]{2,1,0:T(8,128)(2,1)} %get-tuple-element.103), channel_id=1, source_target_pairs={{0,1},{1,0},{2,3},{3,2},{4,5},{5,4},{6,7},{7,6},{8,9},{9,8},{10,11... | collective-permute-start | bytes 3342344 | tf_op jit(solution)/shard_map/brick_sums/ppermute | solution.py:462
  138.7 9.6 %collective-permute-start.17 = (bf16[4,272,128]{2,1,0:T(8,128)(2,1)S(1)}, bf16[4,272,128]{2,1,0:T(8,128)(2,1)S(1)}, u32[]{:S(2)}, u32[]{:S(2)}) collective-permute-start(bf16[4,272,128]{2,1,0:T(8,128)(2,1)S(1)} %get-tuple-element.104), channel_id=1, source_target_pairs={{0,8},{8,0},{16,24},{24,16},{1,9},{9,1},{17,25},{25,17},{2,10},{10... | collective-permute-start | bytes 835592 | tf_op jit(solution)/shard_map/brick_sums/ppermute | solution.py:459
  140.3 14.4 %collective-permute-start.18 = (bf16[4,272,128]{2,1,0:T(8,128)(2,1)S(1)}, bf16[4,272,128]{2,1,0:T(8,128)(2,1)S(1)}, u32[]{:S(2)}, u32[]{:S(2)}) collective-permute-start(bf16[4,272,128]{2,1,0:T(8,128)(2,1)S(1)} %get-tuple-element.106), channel_id=1, source_target_pairs={{0,16},{8,24},{16,0},{24,8},{1,17},{9,25},{17,1},{25,9},{2,18},{10... | collective-permute-start | bytes 835592 | tf_op jit(solution)/shard_map/brick_sums/ppermute | solution.py:459
  141.8 12.9 %collective-permute-start.19 = (bf16[4,272,128]{2,1,0:T(8,128)(2,1)S(1)}, bf16[4,272,128]{2,1,0:T(8,128)(2,1)S(1)}, u32[]{:S(2)}, u32[]{:S(2)}) collective-permute-start(bf16[4,272,128]{2,1,0:T(8,128)(2,1)S(1)} %get-tuple-element.105), channel_id=1, source_target_pairs={{0,24},{8,16},{16,8},{24,0},{1,25},{9,17},{17,9},{25,1},{2,26},{10... | collective-permute-start | bytes 835592 | tf_op jit(solution)/shard_map/brick_sums/ppermute | solution.py:459
  154.9 4.8 %collective-permute-start.20 = (bf16[272,128]{1,0:T(8,128)(2,1)S(1)}, bf16[272,128]{1,0:T(8,128)(2,1)S(1)}, u32[]{:S(2)}, u32[]{:S(2)}) collective-permute-start(bf16[272,128]{1,0:T(8,128)(2,1)S(1)} %get-tuple-element.107), channel_id=1, source_target_pairs={{0,2},{1,3},{2,0},{3,1},{4,6},{5,7},{6,4},{7,5},{8,10},{9,11},{10,... | collective-permute-start | bytes 208904 | tf_op jit(solution)/shard_map/brick_sums/ppermute | solution.py:459
  156.4 7.4 %collective-permute-start.21 = (bf16[272,128]{1,0:T(8,128)(2,1)S(1)}, bf16[272,128]{1,0:T(8,128)(2,1)S(1)}, u32[]{:S(2)}, u32[]{:S(2)}) collective-permute-start(bf16[272,128]{1,0:T(8,128)(2,1)S(1)} %get-tuple-element.109), channel_id=1, source_target_pairs={{0,4},{1,5},{2,6},{3,7},{4,0},{5,1},{6,2},{7,3},{8,12},{9,13},{10,... | collective-permute-start | bytes 208904 | tf_op jit(solution)/shard_map/brick_sums/ppermute | solution.py:459
  159.6 6.1 %collective-permute-start.22 = (bf16[272,128]{1,0:T(8,128)(2,1)S(1)}, bf16[272,128]{1,0:T(8,128)(2,1)S(1)}, u32[]{:S(2)}, u32[]{:S(2)}) collective-permute-start(bf16[272,128]{1,0:T(8,128)(2,1)S(1)} %get-tuple-element.108), channel_id=1, source_target_pairs={{0,6},{1,7},{2,4},{3,5},{4,2},{5,3},{6,0},{7,1},{8,14},{9,15},{10,... | collective-permute-start | bytes 208904 | tf_op jit(solution)/shard_map/brick_sums/ppermute | solution.py:459
  (4 other events, 33.8 us)

commit v4 on v3

--- a/solution.py
+++ b/solution.py
@@ -194,32 +194,33 @@
             pltpu.SemaphoreType.DMA((n,)),
         ],
         input_output_aliases=aliases,
-        compiler_params=pltpu.CompilerParams(vmem_limit_bytes=20 << 20),
+        compiler_params=pltpu.CompilerParams(vmem_limit_bytes=14 << 20),
         cost_estimate=pl.CostEstimate(flops=1000, bytes_accessed=1000, transcendentals=0),
         name="score_blocks",
     )(*args)
     return tuple(out) if first else (carry[0],) + tuple(out)
 
 
-def merge_kernel(a_ref, b_ref, out_ref):
-    for k in range(a_ref.shape[0]):
-        a, b = a_ref[k], b_ref[k]
-        largest = jnp.maximum(a[0:1], b[0:1])
-        total = a[1:2] * jnp.exp(a[0:1] - largest) + b[1:2] * jnp.exp(b[0:1] - largest)
-        pick = lax.broadcasted_iota(jnp.int32, a.shape, 0) == 0
+def merge_kernel(*refs):
+    out_ref = refs[-1]
+    for k in range(out_ref.shape[0]):
+        sets = [ref[k] for ref in refs[:-1]]
+        largest = functools.reduce(jnp.maximum, [a[0:1] for a in sets])
+        total = sum(a[1:2] * jnp.exp(a[0:1] - largest) for a in sets)
+        pick = lax.broadcasted_iota(jnp.int32, sets[0].shape, 0) == 0
         out_ref[k] = jnp.where(pick, largest, total)
 
 
-def merge_step(a, b):
+def merge_step(*sets):
     return pl.pallas_call(
         merge_kernel,
-        out_shape=jax.ShapeDtypeStruct(a.shape, a.dtype),
-        in_specs=[VMEM, VMEM],
+        out_shape=jax.ShapeDtypeStruct(sets[0].shape, sets[0].dtype),
+        in_specs=[VMEM] * len(sets),
         out_specs=VMEM,
         compiler_params=pltpu.CompilerParams(vmem_limit_bytes=4 << 20),
         cost_estimate=pl.CostEstimate(flops=1000, bytes_accessed=1000, transcendentals=0),
         name="merge_totals",
-    )(a, b)
+    )(*sets)
 
 
 def sum_kernel(
@@ -235,11 +236,11 @@
     map_ref,
     other_ref,
     mine_ref,
+    volume,
     weights,
     even,
     odd,
     slots,
-    volume,
 ):
     blocks, orients, block = p_ref.shape
     owned = dest_ref.shape[2]
@@ -247,7 +248,6 @@
     segments = dest_ref.shape[0] // groups
     per_tile = TILE // 128
     tiles = segments // per_tile
-    span = map_ref.shape[2]
     core = lax.rem(lax.axis_index("ori"), 2)
     zero = jnp.zeros((512, 128), jnp.float32)
 
@@ -305,13 +305,35 @@
 
     lax.fori_loop(0, groups, group, 0)
     scatter(odd, groups * segments * owned)
+    span = map_ref.shape[2]
+
+    def slots_of(i, parity):
+        start = pl.multiple_of(brick_of(i, parity) * span, 8)
+        return slots[pl.ds(start, span), :].astype(jnp.bfloat16)
+
+    def keep(i, ignored):
+        mine_ref[i] = slots_of(i, core)
+        return ignored
+
+    lax.fori_loop(0, bricks // 2, keep, 0)
+    grid_bricks(1 - core, lambda i: slots_of(i, 1 - core), volume, map_ref, other_ref)
+
+
+def brick_of(i, parity):
+    chips = lax.axis_size("ori") // 2
+    group = lax.bitwise_xor(lax.axis_index("img"), i // chips)
+    chip = lax.bitwise_xor(lax.axis_index("ori") // 2, lax.rem(i, chips))
+    return (group * chips + chip) * 2 + parity
+
+
+def grid_bricks(parity, slots_of, volume, map_ref, out_ref):
+    bricks = map_ref.shape[0]
+    unroll = 8
     sub = lax.broadcasted_iota(jnp.int32, (EXTRA_ROWS, 128), 0)
-    unroll = 8
-
-    def grid_brick(i, out_ref, parity):
-        b = 2 * i + parity
-        values = slots[pl.ds(pl.multiple_of(b * span, 8), span), :].astype(jnp.bfloat16)
-        cells = dot(one_hot_rows(BRICK_ROWS, map_ref[b]), values)
+
+    def grid_brick(i):
+        b = brick_of(i, parity)
+        cells = dot(one_hot_rows(BRICK_ROWS, map_ref[b]), slots_of(i))
         out_ref[i, 0:BRICK_ROWS, :] = cells.astype(out_ref.dtype)
         total = volume[pl.ds(b, 1), :] + volume[pl.ds(bricks + b, 1), :]
         top = total.astype(jnp.bfloat16).astype(jnp.float32)
@@ -320,18 +342,31 @@
         extra += jnp.where(sub == 2, rest[:, :128], jnp.where(sub == 3, rest[:, 128:], 0.0))
         out_ref[i, BRICK_ROWS : BRICK_ROWS + EXTRA_ROWS, :] = extra.astype(out_ref.dtype)
 
-    def others(i, ignored):
+    def step(i, ignored):
         for k in range(unroll):
-            grid_brick(i * unroll + k, other_ref, 1 - core)
+            grid_brick(i * unroll + k)
         return ignored
 
-    def own(i, ignored):
-        for k in range(unroll):
-            grid_brick(i * unroll + k, mine_ref, core)
-        return ignored
-
-    lax.fori_loop(0, bricks // 2 // unroll, others, 0)
-    lax.fori_loop(0, bricks // 2 // unroll, own, 0)
+    lax.fori_loop(0, bricks // 2 // unroll, step, 0)
+
+
+def grid_kernel(slots, volume, map_ref, out_ref):
+    core = lax.rem(lax.axis_index("ori"), 2)
+    grid_bricks(core, lambda i: slots[i], volume, map_ref, out_ref)
+
+
+def grid_step(slots, volume, row_map):
+    bricks = row_map.shape[0]
+    shape = (bricks // 2, BRICK_ROWS + EXTRA_ROWS, 128)
+    return pl.pallas_call(
+        grid_kernel,
+        out_shape=jax.ShapeDtypeStruct(shape, jnp.float32),
+        in_specs=[VMEM] * 3,
+        out_specs=VMEM,
+        compiler_params=pltpu.CompilerParams(vmem_limit_bytes=8 << 20),
+        cost_estimate=pl.CostEstimate(flops=1000, bytes_accessed=1000, transcendentals=0),
+        name="grid_own_bricks",
+    )(slots, volume, row_map)
 
 
 def sum_step(bricks, groups, capacity, slot, p, stats, totals, x, dest, rows, row_map):
@@ -343,18 +378,18 @@
         functools.partial(sum_kernel, bricks, capacity),
         out_shape=[
             jax.ShapeDtypeStruct(shape, jnp.bfloat16),
-            jax.ShapeDtypeStruct(shape, jnp.float32),
+            jax.ShapeDtypeStruct((bricks // 2, groups * capacity, 128), jnp.bfloat16),
+            jax.ShapeDtypeStruct((2 * bricks, BRICK_ROWS), jnp.float32),
         ],
         in_specs=[SMEM] + [VMEM] * 7,
-        out_specs=[VMEM, VMEM],
+        out_specs=[VMEM] * 3,
         scratch_shapes=[
             pltpu.VMEM((owned, blocks * block), jnp.bfloat16),
             pltpu.VMEM((owned, TILE), jnp.float32),
             pltpu.VMEM((owned, TILE), jnp.float32),
             pltpu.VMEM((bricks * groups * capacity + 512, 128), jnp.float32),
-            pltpu.VMEM((2 * bricks, BRICK_ROWS), jnp.float32),
         ],
-        compiler_params=pltpu.CompilerParams(vmem_limit_bytes=22 << 20),
+        compiler_params=pltpu.CompilerParams(vmem_limit_bytes=19 << 20),
         cost_estimate=pl.CostEstimate(
             flops=2 * blocks * block * orients * width, bytes_accessed=24 << 20, transcendentals=0
         ),
@@ -392,7 +427,7 @@
             ],
             in_specs=[VMEM, VMEM],
             out_specs=[VMEM, VMEM],
-            compiler_params=pltpu.CompilerParams(vmem_limit_bytes=12 << 20),
+            compiler_params=pltpu.CompilerParams(vmem_limit_bytes=8 << 20),
             cost_estimate=pl.CostEstimate(flops=1000, bytes_accessed=1000, transcendentals=0),
             name="place_segments",
         )(dest, rows)
@@ -427,6 +462,8 @@
                     moving[q], carry = lax.optimization_barrier((moving[q], carry))
                 else:
                     carry = score(waiting.pop(0), carry)
+                    if distance == chips - 1 and q == 1:
+                        carry = score(waiting.pop(0), carry)
                     moving[q], carry = lax.optimization_barrier((moving[q], carry))
                 waiting.append(arrive(distance, q, moving[q]))
         late = [sum(parts, ()) for parts in zip(*waiting)]
@@ -435,15 +472,15 @@
         slot, row_map, dest, rows = placed
 
     with jax.named_scope("softmax_total"):
-        totals = stats
-        step = 1
-        while step < orient_groups:
-            partner = [(i, i ^ step) for i in range(orient_groups)]
-            totals = merge_step(totals, lax.ppermute(totals, "ori", partner))
-            step *= 2
+        totals = merge_step(stats, lax.ppermute(stats, "ori", swap))
+        others = [
+            lax.ppermute(totals, "ori", [(i, i ^ (2 * k)) for i in range(orient_groups)])
+            for k in range(1, chips)
+        ]
+        totals = merge_step(totals, *others)
 
     with jax.named_scope("sum_and_grid"):
-        other_cells, cells = sum_step(
+        other_cells, slots, volume = sum_step(
             bricks, image_groups, capacity, slot, p, stats, totals, x, dest, rows, row_map
         )
 
@@ -451,18 +488,18 @@
         height = BRICK_ROWS + EXTRA_ROWS
 
         def add_up(cells, axis, ways, stride):
-            own = lax.axis_index(axis) // stride
-            total = lax.dynamic_index_in_dim(cells, own, 0, keepdims=False).astype(jnp.float32)
+            total = cells[0].astype(jnp.float32)
             for k in range(1, ways):
                 perm = [(i, i ^ (k * stride)) for i in range(ways * stride)]
-                part = lax.dynamic_index_in_dim(cells, own ^ k, 0, keepdims=False)
+                part = cells[k].astype(jnp.bfloat16)
                 total += lax.ppermute(part, axis, perm).astype(jnp.float32)
             return total
 
         other_cells = lax.ppermute(other_cells, "ori", swap)
-        cells = cells.astype(jnp.float32) + other_cells.astype(jnp.float32)
-        cells = cells.astype(jnp.bfloat16).reshape(image_groups, chips, height, 128)
-        cells = add_up(cells, "img", image_groups, 1).astype(jnp.bfloat16)
+        cells = grid_step(slots, volume, row_map)
+        cells = cells + other_cells.astype(jnp.float32)
+        cells = cells.reshape(image_groups, chips, height, 128)
+        cells = add_up(cells, "img", image_groups, 1)
         cells = add_up(cells, "ori", chips, 2)
 
     gridded = cells[:BRICK_ROWS]

time: 168 us -> 160 us (0.952)
  waiting for transfers between devices: 63.3 us -> 56.4 us
    ppermute x1, waiting for transfers between devices: 2.96 us -> 0.23 us  [body(): other_cells = lax.ppermute(other_cells, 'ori', swap)]
    pallas_call x1, Pallas kernels: 31.3 us -> 28.7 us  [sum_step(): pl.pallas_call(functools.partial(sum_kernel, bricks, capacity), out_shape...]
    pallas_call x3, Pallas kernels: 0.12 us -> 2.62 us  [the longest x1 2.5 us: grid_step(): pl.pallas_call(grid_kernel, out_shape=jax.ShapeDtypeStruct(shape, jnp.flo...]
    ppermute x6, waiting for transfers between devices: 30.2 us -> 28.4 us  [body(): moving = [lax.ppermute(part, 'ori', along) for part in moving]]
    ppermute x3 -> x4, starting transfers between devices: 3.55 us -> 5.34 us  [the longest x3 5.14 us: body(): lax.ppermute(totals, 'ori', [(i, i ^ 2 * k) for i in range(orient_groups)])]
    unnamed x10 -> x8, local copies, waits for them, and re-layouts: 4.41 us -> 3.42 us
    ppermute x3 -> x4, waiting for transfers between devices: 7.98 us -> 7.28 us  [the longest x3 6.16 us: body(): lax.ppermute(totals, 'ori', [(i, i ^ 2 * k) for i in range(orient_groups)])]
    pallas_call x5 -> x6, Pallas kernels: 17.4 us -> 17.1 us  [score_step(): pl.pallas_call(functools.partial(score_kernel, chips, candidates, first),...]
  transfers between devices with their start and end apart: 23 -> 24, of which waited for: 15 -> 16; matrix products, arithmetic and copies ran while one was open for 2% -> 2% of each run, Pallas kernels for 9% -> 13%
where the time goes in v4:
time: 160 us; the launch traced here: 159 us
  waiting for transfers between devices  56.4 us (35%)
  Pallas kernels  53.2 us (33%)
  starting transfers between devices  39.5 us (25%)
  local copies, waits for them, and re-layouts  6.29 us (4%)
  other arithmetic  2.04 us (1%)
    pallas_call x1, Pallas kernels, sum_step(): pl.pallas_call(functools.partial(sum_kernel, bricks, capacity), out_shape...  28.7 us
    ppermute x6, waiting for transfers between devices, body(): moving = [lax.ppermute(part, 'ori', along) for part in moving]  28.4 us
    ppermute x6, starting transfers between devices, body(): moving = [lax.ppermute(part, 'ori', along) for part in moving]  24.8 us
    pallas_call x6, Pallas kernels, score_step(): pl.pallas_call(functools.partial(score_kernel, chips, candidates, first),...  17.1 us
    ppermute x6, waiting for transfers between devices, add_up(): total += lax.ppermute(part, axis, perm).astype(jnp.float32)  16.8 us
    ppermute x6, starting transfers between devices, add_up(): total += lax.ppermute(part, axis, perm).astype(jnp.float32)  8.01 us
    ppermute x3, waiting for transfers between devices, body(): lax.ppermute(totals, 'ori', [(i, i ^ 2 * k) for i in range(orient_groups)])  6.16 us
    ppermute x3, starting transfers between devices, body(): lax.ppermute(totals, 'ori', [(i, i ^ 2 * k) for i in range(orient_groups)])  5.14 us
  transfers between devices with their start and end apart: 24, of which 16 were waited for; matrix products, arithmetic and copies ran while one was open for 2% of the time, Pallas kernels for 13%

profile of v4, /device:TPU:0, one launch (start us, length us, event | category | flops | bytes accessed | tf_op | source)
XLA Modules:
  0.0 159.2 jit_solution(5969135701174545460)
XLA Ops:
  1.2 4.6 %collective-permute-start.1 = (bf16[256,2048]{1,0:T(8,128)(2,1)}, bf16[256,2048]{1,0:T(8,128)(2,1)S(1)}, u32[]{:S(2)}, u32[]{:S(2)}) collective-permute-start(bf16[256,2048]{1,0:T(8,128)(2,1)} %refs_0_.1), channel_id=1, source_target_pairs={{0,2},{2,4},{4,6},{3,1},{5,3},{7,5},{8,10},{10,12},{12,14},{11,9},... | collective-permute-start | bytes 3145736 | tf_op jit(solution)/shard_map/score/ppermute | solution.py:456
  5.7 3.5 %collective-permute-start.2 = (bf16[256,2048]{1,0:T(8,128)(2,1)S(1)}, bf16[256,2048]{1,0:T(8,128)(2,1)S(1)}, u32[]{:S(2)}, u32[]{:S(2)}) collective-permute-start(bf16[256,2048]{1,0:T(8,128)(2,1)S(1)} %collective-permute-done.refs_1_), channel_id=1, source_target_pairs={{0,2},{2,4},{4,6},{3,1},{5,3},{7,5},{8,10},{10,12},{12,14},{11,9},... | collective-permute-start | bytes 3145736 | tf_op jit(solution)/shard_map/score/ppermute | solution.py:456
  11.2 4.7 %place_segments.1 = (s32[64,1,256]{2,1,0:T(1,128)S(1)}, s32[4,32,256]{2,1,0:T(8,128)S(1)}) custom-call(s32[64,1,256]{2,1,0:T(1,128)S(1)} %reshape.38.dest_ref, s32[64,1,256]{2,1,0:T(1,128)S(1)} %reshape.40.rows_ref), custom_call_target="tpu_custom_call" | custom-call | flops 1000 | bytes 1000 | tf_op jit(solution)/shard_map/place_segments/place_segments/pallas_call | solution.py:422
  17.8 2.2 %copy-done.1 = bf16[1024,2048]{1,0:T(8,128)(2,1)S(1)} copy-done((bf16[1024,2048]{1,0:T(8,128)(2,1)S(1)}, bf16[1024,2048]{1,0:T(8,128)(2,1)}, u32[]{:S(2)}) %copy-start.1) | copy-done | bytes 4194328
  21.2 4.9 %score_blocks.6 = (f32[1024,128]{1,0:T(8,128)S(1)}, f32[8,1024,256]{2,1,0:T(8,128)S(1)}, bf16[2048,2048]{1,0:T(8,128)(2,1)S(1)}, f32[8,8,256]{2,1,0:T(8,128)S(1)}) custom-call(bf16[256,2048]{1,0:T(8,128)(2,1)S(1)} %copy-done.3, bf16[256,2048]{1,0:T(8,128)(2,1)S(1)} %collective-permute-done.refs_1_, bf16[1024,2048]{1,0:T(8,128)(2,1)S(1)} %copy-done.1), custom_call_target="tpu_custom_call" | custom-call | flops 1000 | bytes 1000 | tf_op jit(solution)/shard_map/score/score_blocks/pallas_call | solution.py:182
  26.2 3.2 %collective-permute-done.2.refs_0_ = bf16[256,2048]{1,0:T(8,128)(2,1)S(1)} collective-permute-done((bf16[256,2048]{1,0:T(8,128)(2,1)S(1)}, bf16[256,2048]{1,0:T(8,128)(2,1)S(1)}, u32[]{:S(2)}, u32[]{:S(2)}) %collective-permute-start.2) | collective-permute-done | bytes 1048608 | tf_op jit(solution)/shard_map/score/ppermute | solution.py:456
  29.4 4.4 %collective-permute-start.3 = (bf16[256,2048]{1,0:T(8,128)(2,1)S(1)}, bf16[256,2048]{1,0:T(8,128)(2,1)S(1)}, u32[]{:S(2)}, u32[]{:S(2)}) collective-permute-start(bf16[256,2048]{1,0:T(8,128)(2,1)S(1)} %collective-permute-done.1.refs_0_), channel_id=1, source_target_pairs={{0,2},{2,4},{4,6},{3,1},{5,3},{7,5},{8,10},{10,12},{12,14},{11,9},... | collective-permute-start | bytes 3145736 | tf_op jit(solution)/shard_map/score/ppermute | solution.py:456
  33.9 3.5 %collective-permute-start.5 = (bf16[256,2048]{1,0:T(8,128)(2,1)S(1)}, bf16[256,2048]{1,0:T(8,128)(2,1)S(1)}, u32[]{:S(2)}, u32[]{:S(2)}) collective-permute-start(bf16[256,2048]{1,0:T(8,128)(2,1)S(1)} %collective-permute-done.2.refs_0_), channel_id=1, source_target_pairs={{0,2},{2,4},{4,6},{3,1},{5,3},{7,5},{8,10},{10,12},{12,14},{11,9},... | collective-permute-start | bytes 3145736 | tf_op jit(solution)/shard_map/score/ppermute | solution.py:456
  37.5 8.6 %collective-permute-done.3.refs_0_ = bf16[256,2048]{1,0:T(8,128)(2,1)S(1)} collective-permute-done((bf16[256,2048]{1,0:T(8,128)(2,1)S(1)}, bf16[256,2048]{1,0:T(8,128)(2,1)S(1)}, u32[]{:S(2)}, u32[]{:S(2)}) %collective-permute-start.3) | collective-permute-done | bytes 1048608 | tf_op jit(solution)/shard_map/score/ppermute | solution.py:456
  46.1 4.4 %collective-permute-start.4 = (bf16[256,2048]{1,0:T(8,128)(2,1)S(1)}, bf16[256,2048]{1,0:T(8,128)(2,1)S(1)}, u32[]{:S(2)}, u32[]{:S(2)}) collective-permute-start(bf16[256,2048]{1,0:T(8,128)(2,1)S(1)} %collective-permute-done.3.refs_0_), channel_id=1, source_target_pairs={{0,2},{2,4},{4,6},{3,1},{5,3},{7,5},{8,10},{10,12},{12,14},{11,9},... | collective-permute-start | bytes 3145736 | tf_op jit(solution)/shard_map/score/ppermute | solution.py:456
  52.7 4.7 %collective-permute-done.5.refs_0_ = bf16[256,2048]{1,0:T(8,128)(2,1)S(1)} collective-permute-done((bf16[256,2048]{1,0:T(8,128)(2,1)S(1)}, bf16[256,2048]{1,0:T(8,128)(2,1)S(1)}, u32[]{:S(2)}, u32[]{:S(2)}) %collective-permute-start.5) | collective-permute-done | bytes 1048608 | tf_op jit(solution)/shard_map/score/ppermute | solution.py:456
  57.3 4.4 %collective-permute-start.9 = (bf16[256,2048]{1,0:T(8,128)(2,1)S(1)}, bf16[256,2048]{1,0:T(8,128)(2,1)S(1)}, u32[]{:S(2)}, u32[]{:S(2)}) collective-permute-start(bf16[256,2048]{1,0:T(8,128)(2,1)S(1)} %collective-permute-done.5.refs_0_), channel_id=1, source_target_pairs={{0,2},{2,4},{4,6},{3,1},{5,3},{7,5},{8,10},{10,12},{12,14},{11,9},... | collective-permute-start | bytes 3145736 | tf_op jit(solution)/shard_map/score/ppermute | solution.py:456
  63.8 4.8 %collective-permute-done.4.refs_0_ = bf16[256,2048]{1,0:T(8,128)(2,1)S(1)} collective-permute-done((bf16[256,2048]{1,0:T(8,128)(2,1)S(1)}, bf16[256,2048]{1,0:T(8,128)(2,1)S(1)}, u32[]{:S(2)}, u32[]{:S(2)}) %collective-permute-start.4) | collective-permute-done | bytes 1048608 | tf_op jit(solution)/shard_map/score/ppermute | solution.py:456
  72.6 7.2 %collective-permute-done.9.refs_2_ = bf16[256,2048]{1,0:T(8,128)(2,1)S(1)} collective-permute-done((bf16[256,2048]{1,0:T(8,128)(2,1)S(1)}, bf16[256,2048]{1,0:T(8,128)(2,1)S(1)}, u32[]{:S(2)}, u32[]{:S(2)}) %collective-permute-start.9) | collective-permute-done | bytes 1048608 | tf_op jit(solution)/shard_map/score/ppermute | solution.py:456
  80.3 2.1 %collective-permute-done.12.refs_3_ = bf16[256,2048]{1,0:T(8,128)(2,1)S(1)} collective-permute-done((bf16[256,2048]{1,0:T(8,128)(2,1)S(1)}, bf16[256,2048]{1,0:T(8,128)(2,1)S(1)}, u32[]{:S(2)}, u32[]{:S(2)}) %collective-permute-start.12) | collective-permute-done | bytes 1048608 | tf_op jit(solution)/shard_map/score/ppermute | solution.py:448
  84.0 4.2 %score_blocks.11 = (f32[8,1024,256]{2,1,0:T(8,128)S(1)}, bf16[2048,2048]{1,0:T(8,128)(2,1)S(1)}, f32[8,8,256]{2,1,0:T(8,128)S(1)}) custom-call(bf16[256,2048]{1,0:T(8,128)(2,1)S(1)} %collective-permute-done.4.refs_0_, bf16[256,2048]{1,0:T(8,128)(2,1)S(1)} %collective-permute-done.8.refs_1_, ...), custom_call_target="tpu_custom_call", output_to_operand_aliasing={{0}: (6, {}), {1}: (7, {}), {2}: (8, {})} | custom-call | flops 1000 | bytes 1000 | tf_op jit(solution)/shard_map/score/score_blocks/pallas_call | solution.py:182
  89.6 5.1 %collective-permute-start.15 = (f32[8,8,256]{2,1,0:T(8,128)S(1)}, f32[8,8,256]{2,1,0:T(8,128)S(1)}, u32[]{:S(2)}, u32[]{:S(2)}) collective-permute-start(f32[8,8,256]{2,1,0:T(8,128)S(1)} %merge_totals.2.refs_0_), channel_id=1, source_target_pairs={{0,4},{1,5},{2,6},{3,7},{4,0},{5,1},{6,2},{7,3},{8,12},{9,13},{10,... | collective-permute-start | bytes 196616 | tf_op jit(solution)/shard_map/softmax_total/ppermute | solution.py:477
  94.6 4.0 %collective-permute-done.15.refs_2_ = f32[8,8,256]{2,1,0:T(8,128)S(1)} collective-permute-done((f32[8,8,256]{2,1,0:T(8,128)S(1)}, f32[8,8,256]{2,1,0:T(8,128)S(1)}, u32[]{:S(2)}, u32[]{:S(2)}) %collective-permute-start.15) | collective-permute-done | bytes 65568 | tf_op jit(solution)/shard_map/softmax_total/ppermute | solution.py:477
  98.7 2.1 %collective-permute-done.16.refs_3_ = f32[8,8,256]{2,1,0:T(8,128)S(1)} collective-permute-done((f32[8,8,256]{2,1,0:T(8,128)S(1)}, f32[8,8,256]{2,1,0:T(8,128)S(1)}, u32[]{:S(2)}, u32[]{:S(2)}) %collective-permute-start.16) | collective-permute-done | bytes 65568 | tf_op jit(solution)/shard_map/softmax_total/ppermute | solution.py:477
  100.9 28.7 %sum_and_grid.1 = (bf16[16,272,128]{2,1,0:T(8,128)(2,1)S(1)}, bf16[16,1024,128]{2,1,0:T(8,128)(2,1)S(1)}, f32[64,256]{1,0:T(8,128)S(1)}) custom-call(s32[16896]{0:T(1024)S(1)} %concatenate.3.slot_ref, f32[8,1024,256]{2,1,0:T(8,128)S(1)} %get-tuple-element.103.p_ref, f32[8,8,256]{2,1,0:T(8,128)S(1)} %get-tuple-element.104.refs_0_.stats_ref, ...), custom_call_target="tpu_custom_call" | custom-call | flops 8589934592 | bytes 25165824 | tf_op jit(solution)/shard_map/sum_and_grid/sum_and_grid/pallas_call | solution.py:377
  129.6 2.5 %grid_own_bricks.1 = f32[16,272,128]{2,1,0:T(8,128)S(1)} custom-call(bf16[16,1024,128]{2,1,0:T(8,128)(2,1)S(1)} %get-tuple-element.109.slots, f32[64,256]{1,0:T(8,128)S(1)} %get-tuple-element.110.volume, s32[32,1,1024]{2,1,0:T(1,128)S(1)} %reshape.42.map_ref), custom_call_target="tpu_custom_call" | custom-call | flops 1000 | bytes 1000 | tf_op jit(solution)/shard_map/brick_sums/grid_own_bricks/pallas_call | solution.py:361
  136.3 6.0 %collective-permute-done.18 = bf16[4,272,128]{2,1,0:T(8,128)(2,1)S(1)} collective-permute-done((bf16[4,272,128]{2,1,0:T(8,128)(2,1)S(1)}, bf16[4,272,128]{2,1,0:T(8,128)(2,1)S(1)}, u32[]{:S(2)}, u32[]{:S(2)}) %collective-permute-start.18) | collective-permute-done | bytes 278560 | tf_op jit(solution)/shard_map/brick_sums/ppermute | solution.py:495
  142.3 6.5 %collective-permute-done.19 = bf16[4,272,128]{2,1,0:T(8,128)(2,1)S(1)} collective-permute-done((bf16[4,272,128]{2,1,0:T(8,128)(2,1)S(1)}, bf16[4,272,128]{2,1,0:T(8,128)(2,1)S(1)}, u32[]{:S(2)}, u32[]{:S(2)}) %collective-permute-start.19) | collective-permute-done | bytes 278560 | tf_op jit(solution)/shard_map/brick_sums/ppermute | solution.py:495
  153.8 3.0 %collective-permute-done.22 = bf16[272,128]{1,0:T(8,128)(2,1)S(1)} collective-permute-done((bf16[272,128]{1,0:T(8,128)(2,1)S(1)}, bf16[272,128]{1,0:T(8,128)(2,1)S(1)}, u32[]{:S(2)}, u32[]{:S(2)}) %collective-permute-start.22) | collective-permute-done | bytes 69664 | tf_op jit(solution)/shard_map/brick_sums/ppermute | solution.py:495
  (58 shorter events, 28.9 us)
Async XLA Ops:
  0.6 5.1 %collective-permute-start = (bf16[256,2048]{1,0:T(8,128)(2,1)}, bf16[256,2048]{1,0:T(8,128)(2,1)S(1)}, u32[]{:S(2)}, u32[]{:S(2)}) collective-permute-start(bf16[256,2048]{1,0:T(8,128)(2,1)} %refs_0_.1), channel_id=1, source_target_pairs={{0,1},{1,0},{2,3},{3,2},{4,5},{5,4},{6,7},{7,6},{8,9},{9,8},{10,11... | collective-permute-start | bytes 3145736 | tf_op jit(solution)/shard_map/score/ppermute | solution.py:439
  1.2 25.0 %collective-permute-start.1 = (bf16[256,2048]{1,0:T(8,128)(2,1)}, bf16[256,2048]{1,0:T(8,128)(2,1)S(1)}, u32[]{:S(2)}, u32[]{:S(2)}) collective-permute-start(bf16[256,2048]{1,0:T(8,128)(2,1)} %refs_0_.1), channel_id=1, source_target_pairs={{0,2},{2,4},{4,6},{3,1},{5,3},{7,5},{8,10},{10,12},{12,14},{11,9},... | collective-permute-start | bytes 3145736 | tf_op jit(solution)/shard_map/score/ppermute | solution.py:456
  5.7 23.7 %collective-permute-start.2 = (bf16[256,2048]{1,0:T(8,128)(2,1)S(1)}, bf16[256,2048]{1,0:T(8,128)(2,1)S(1)}, u32[]{:S(2)}, u32[]{:S(2)}) collective-permute-start(bf16[256,2048]{1,0:T(8,128)(2,1)S(1)} %collective-permute-done.refs_1_), channel_id=1, source_target_pairs={{0,2},{2,4},{4,6},{3,1},{5,3},{7,5},{8,10},{10,12},{12,14},{11,9},... | collective-permute-start | bytes 3145736 | tf_op jit(solution)/shard_map/score/ppermute | solution.py:456
  29.4 16.7 %collective-permute-start.3 = (bf16[256,2048]{1,0:T(8,128)(2,1)S(1)}, bf16[256,2048]{1,0:T(8,128)(2,1)S(1)}, u32[]{:S(2)}, u32[]{:S(2)}) collective-permute-start(bf16[256,2048]{1,0:T(8,128)(2,1)S(1)} %collective-permute-done.1.refs_0_), channel_id=1, source_target_pairs={{0,2},{2,4},{4,6},{3,1},{5,3},{7,5},{8,10},{10,12},{12,14},{11,9},... | collective-permute-start | bytes 3145736 | tf_op jit(solution)/shard_map/score/ppermute | solution.py:456
  33.9 16.8 %collective-permute-start.6 = (bf16[256,2048]{1,0:T(8,128)(2,1)S(1)}, bf16[256,2048]{1,0:T(8,128)(2,1)S(1)}, u32[]{:S(2)}, u32[]{:S(2)}) collective-permute-start(bf16[256,2048]{1,0:T(8,128)(2,1)S(1)} %collective-permute-done.1.refs_0_), channel_id=1, source_target_pairs={{0,1},{1,0},{2,3},{3,2},{4,5},{5,4},{6,7},{7,6},{8,9},{9,8},{10,11... | collective-permute-start | bytes 3145736 | tf_op jit(solution)/shard_map/score/ppermute | solution.py:448
  33.9 23.4 %collective-permute-start.5 = (bf16[256,2048]{1,0:T(8,128)(2,1)S(1)}, bf16[256,2048]{1,0:T(8,128)(2,1)S(1)}, u32[]{:S(2)}, u32[]{:S(2)}) collective-permute-start(bf16[256,2048]{1,0:T(8,128)(2,1)S(1)} %collective-permute-done.2.refs_0_), channel_id=1, source_target_pairs={{0,2},{2,4},{4,6},{3,1},{5,3},{7,5},{8,10},{10,12},{12,14},{11,9},... | collective-permute-start | bytes 3145736 | tf_op jit(solution)/shard_map/score/ppermute | solution.py:456
  37.4 24.4 %collective-permute-start.7 = (bf16[256,2048]{1,0:T(8,128)(2,1)S(1)}, bf16[256,2048]{1,0:T(8,128)(2,1)S(1)}, u32[]{:S(2)}, u32[]{:S(2)}) collective-permute-start(bf16[256,2048]{1,0:T(8,128)(2,1)S(1)} %collective-permute-done.2.refs_0_), channel_id=1, source_target_pairs={{0,1},{1,0},{2,3},{3,2},{4,5},{5,4},{6,7},{7,6},{8,9},{9,8},{10,11... | collective-permute-start | bytes 3145736 | tf_op jit(solution)/shard_map/score/ppermute | solution.py:448
  46.1 22.5 %collective-permute-start.4 = (bf16[256,2048]{1,0:T(8,128)(2,1)S(1)}, bf16[256,2048]{1,0:T(8,128)(2,1)S(1)}, u32[]{:S(2)}, u32[]{:S(2)}) collective-permute-start(bf16[256,2048]{1,0:T(8,128)(2,1)S(1)} %collective-permute-done.3.refs_0_), channel_id=1, source_target_pairs={{0,2},{2,4},{4,6},{3,1},{5,3},{7,5},{8,10},{10,12},{12,14},{11,9},... | collective-permute-start | bytes 3145736 | tf_op jit(solution)/shard_map/score/ppermute | solution.py:456
  50.5 18.0 %collective-permute-start.11 = (bf16[256,2048]{1,0:T(8,128)(2,1)S(1)}, bf16[256,2048]{1,0:T(8,128)(2,1)S(1)}, u32[]{:S(2)}, u32[]{:S(2)}) collective-permute-start(bf16[256,2048]{1,0:T(8,128)(2,1)S(1)} %collective-permute-done.3.refs_0_), channel_id=1, source_target_pairs={{0,1},{1,0},{2,3},{3,2},{4,5},{5,4},{6,7},{7,6},{8,9},{9,8},{10,11... | collective-permute-start | bytes 3145736 | tf_op jit(solution)/shard_map/score/ppermute | solution.py:448
  57.3 13.2 %collective-permute-start.10 = (bf16[256,2048]{1,0:T(8,128)(2,1)S(1)}, bf16[256,2048]{1,0:T(8,128)(2,1)S(1)}, u32[]{:S(2)}, u32[]{:S(2)}) collective-permute-start(bf16[256,2048]{1,0:T(8,128)(2,1)S(1)} %collective-permute-done.5.refs_0_), channel_id=1, source_target_pairs={{0,1},{1,0},{2,3},{3,2},{4,5},{5,4},{6,7},{7,6},{8,9},{9,8},{10,11... | collective-permute-start | bytes 3145736 | tf_op jit(solution)/shard_map/score/ppermute | solution.py:448
  57.3 22.5 %collective-permute-start.9 = (bf16[256,2048]{1,0:T(8,128)(2,1)S(1)}, bf16[256,2048]{1,0:T(8,128)(2,1)S(1)}, u32[]{:S(2)}, u32[]{:S(2)}) collective-permute-start(bf16[256,2048]{1,0:T(8,128)(2,1)S(1)} %collective-permute-done.5.refs_0_), channel_id=1, source_target_pairs={{0,2},{2,4},{4,6},{3,1},{5,3},{7,5},{8,10},{10,12},{12,14},{11,9},... | collective-permute-start | bytes 3145736 | tf_op jit(solution)/shard_map/score/ppermute | solution.py:456
  79.8 2.7 %collective-permute-start.12 = (bf16[256,2048]{1,0:T(8,128)(2,1)S(1)}, bf16[256,2048]{1,0:T(8,128)(2,1)S(1)}, u32[]{:S(2)}, u32[]{:S(2)}) collective-permute-start(bf16[256,2048]{1,0:T(8,128)(2,1)S(1)} %collective-permute-done.9.refs_2_), channel_id=1, source_target_pairs={{0,1},{1,0},{2,3},{3,2},{4,5},{5,4},{6,7},{7,6},{8,9},{9,8},{10,11... | collective-permute-start | bytes 3145736 | tf_op jit(solution)/shard_map/score/ppermute | solution.py:448
  79.8 4.2 %collective-permute-start.8 = (bf16[256,2048]{1,0:T(8,128)(2,1)S(1)}, bf16[256,2048]{1,0:T(8,128)(2,1)S(1)}, u32[]{:S(2)}, u32[]{:S(2)}) collective-permute-start(bf16[256,2048]{1,0:T(8,128)(2,1)S(1)} %collective-permute-done.4.refs_0_), channel_id=1, source_target_pairs={{0,1},{1,0},{2,3},{3,2},{4,5},{5,4},{6,7},{7,6},{8,9},{9,8},{10,11... | collective-permute-start | bytes 3145736 | tf_op jit(solution)/shard_map/score/ppermute | solution.py:448
  88.1 1.3 collective-permute-start.13
  89.5 5.1 %collective-permute-start.14 = (f32[8,8,256]{2,1,0:T(8,128)S(1)}, f32[8,8,256]{2,1,0:T(8,128)S(1)}, u32[]{:S(2)}, u32[]{:S(2)}) collective-permute-start(f32[8,8,256]{2,1,0:T(8,128)S(1)} %merge_totals.2.refs_0_), channel_id=1, source_target_pairs={{0,2},{1,3},{2,0},{3,1},{4,6},{5,7},{6,4},{7,5},{8,10},{9,11},{10,... | collective-permute-start | bytes 196616 | tf_op jit(solution)/shard_map/softmax_total/ppermute | solution.py:477
  89.6 9.1 %collective-permute-start.15 = (f32[8,8,256]{2,1,0:T(8,128)S(1)}, f32[8,8,256]{2,1,0:T(8,128)S(1)}, u32[]{:S(2)}, u32[]{:S(2)}) collective-permute-start(f32[8,8,256]{2,1,0:T(8,128)S(1)} %merge_totals.2.refs_0_), channel_id=1, source_target_pairs={{0,4},{1,5},{2,6},{3,7},{4,0},{5,1},{6,2},{7,3},{8,12},{9,13},{10,... | collective-permute-start | bytes 196616 | tf_op jit(solution)/shard_map/softmax_total/ppermute | solution.py:477
  94.6 6.2 %collective-permute-start.16 = (f32[8,8,256]{2,1,0:T(8,128)S(1)}, f32[8,8,256]{2,1,0:T(8,128)S(1)}, u32[]{:S(2)}, u32[]{:S(2)}) collective-permute-start(f32[8,8,256]{2,1,0:T(8,128)S(1)} %merge_totals.2.refs_0_), channel_id=1, source_target_pairs={{0,6},{1,7},{2,4},{3,5},{4,2},{5,3},{6,0},{7,1},{8,14},{9,15},{10,... | collective-permute-start | bytes 196616 | tf_op jit(solution)/shard_map/softmax_total/ppermute | solution.py:477
  129.6 2.8 %collective-permute-start.17 = (bf16[16,272,128]{2,1,0:T(8,128)(2,1)S(1)}, bf16[16,272,128]{2,1,0:T(8,128)(2,1)S(1)}, u32[]{:S(2)}, u32[]{:S(2)}) collective-permute-start(bf16[16,272,128]{2,1,0:T(8,128)(2,1)S(1)} %get-tuple-element.111), channel_id=1, source_target_pairs={{0,1},{1,0},{2,3},{3,2},{4,5},{5,4},{6,7},{7,6},{8,9},{9,8},{10,11... | collective-permute-start | bytes 3342344 | tf_op jit(solution)/shard_map/brick_sums/ppermute | solution.py:498
  132.7 9.6 %collective-permute-start.18 = (bf16[4,272,128]{2,1,0:T(8,128)(2,1)S(1)}, bf16[4,272,128]{2,1,0:T(8,128)(2,1)S(1)}, u32[]{:S(2)}, u32[]{:S(2)}) collective-permute-start(bf16[4,272,128]{2,1,0:T(8,128)(2,1)S(1)} %get-tuple-element.116), channel_id=1, source_target_pairs={{0,8},{8,0},{16,24},{24,16},{1,9},{9,1},{17,25},{25,17},{2,10},{10... | collective-permute-start | bytes 835592 | tf_op jit(solution)/shard_map/brick_sums/ppermute | solution.py:495
  134.3 14.5 %collective-permute-start.19 = (bf16[4,272,128]{2,1,0:T(8,128)(2,1)S(1)}, bf16[4,272,128]{2,1,0:T(8,128)(2,1)S(1)}, u32[]{:S(2)}, u32[]{:S(2)}) collective-permute-start(bf16[4,272,128]{2,1,0:T(8,128)(2,1)S(1)} %get-tuple-element.118), channel_id=1, source_target_pairs={{0,16},{8,24},{16,0},{24,8},{1,17},{9,25},{17,1},{25,9},{2,18},{10... | collective-permute-start | bytes 835592 | tf_op jit(solution)/shard_map/brick_sums/ppermute | solution.py:495
  135.8 13.0 %collective-permute-start.20 = (bf16[4,272,128]{2,1,0:T(8,128)(2,1)S(1)}, bf16[4,272,128]{2,1,0:T(8,128)(2,1)S(1)}, u32[]{:S(2)}, u32[]{:S(2)}) collective-permute-start(bf16[4,272,128]{2,1,0:T(8,128)(2,1)S(1)} %get-tuple-element.117), channel_id=1, source_target_pairs={{0,24},{8,16},{16,8},{24,0},{1,25},{9,17},{17,9},{25,1},{2,26},{10... | collective-permute-start | bytes 835592 | tf_op jit(solution)/shard_map/brick_sums/ppermute | solution.py:495
  149.0 4.8 %collective-permute-start.21 = (bf16[272,128]{1,0:T(8,128)(2,1)S(1)}, bf16[272,128]{1,0:T(8,128)(2,1)S(1)}, u32[]{:S(2)}, u32[]{:S(2)}) collective-permute-start(bf16[272,128]{1,0:T(8,128)(2,1)S(1)} %get-tuple-element.119), channel_id=1, source_target_pairs={{0,2},{1,3},{2,0},{3,1},{4,6},{5,7},{6,4},{7,5},{8,10},{9,11},{10,... | collective-permute-start | bytes 208904 | tf_op jit(solution)/shard_map/brick_sums/ppermute | solution.py:495
  149.8 6.9 %collective-permute-start.22 = (bf16[272,128]{1,0:T(8,128)(2,1)S(1)}, bf16[272,128]{1,0:T(8,128)(2,1)S(1)}, u32[]{:S(2)}, u32[]{:S(2)}) collective-permute-start(bf16[272,128]{1,0:T(8,128)(2,1)S(1)} %get-tuple-element.121), channel_id=1, source_target_pairs={{0,4},{1,5},{2,6},{3,7},{4,0},{5,1},{6,2},{7,3},{8,12},{9,13},{10,... | collective-permute-start | bytes 208904 | tf_op jit(solution)/shard_map/brick_sums/ppermute | solution.py:495
  151.5 6.2 %collective-permute-start.23 = (bf16[272,128]{1,0:T(8,128)(2,1)S(1)}, bf16[272,128]{1,0:T(8,128)(2,1)S(1)}, u32[]{:S(2)}, u32[]{:S(2)}) collective-permute-start(bf16[272,128]{1,0:T(8,128)(2,1)S(1)} %get-tuple-element.120), channel_id=1, source_target_pairs={{0,6},{1,7},{2,4},{3,5},{4,2},{5,3},{6,0},{7,1},{8,14},{9,15},{10,... | collective-permute-start | bytes 208904 | tf_op jit(solution)/shard_map/brick_sums/ppermute | solution.py:495
  (4 other events, 190.6 us)

commit v5 on v4

--- a/solution.py
+++ b/solution.py
@@ -456,8 +456,7 @@
             moving = [lax.ppermute(part, "ori", along) for part in moving]
             for q in range(2):
                 if distance == 1:
-                    if q == 0:
-                        moving, carry = lax.optimization_barrier((moving, carry))
+                    moving[q], carry = lax.optimization_barrier((moving[q], carry))
                 elif distance == 2 and q == 0:
                     moving[q], carry = lax.optimization_barrier((moving[q], carry))
                 else:

time: 160 us -> 153 us (0.956)
  waiting for transfers between devices: 56.4 us -> 51 us
    ppermute x6, waiting for transfers between devices: 28.4 us -> 24.6 us  [body(): moving = [lax.ppermute(part, 'ori', along) for part in moving]]
  transfers between devices with their start and end apart: 24 -> 24, of which waited for: 16 -> 14; matrix products, arithmetic and copies ran while one was open for 2% -> 2% of each run, Pallas kernels for 13% -> 13%
where the time goes in v5:
time: 153 us; the launch traced here: 152 us
  Pallas kernels  53.2 us (35%)
  waiting for transfers between devices  51 us (33%)
  starting transfers between devices  38 us (25%)
  local copies, waits for them, and re-layouts  6.29 us (4%)
  other arithmetic  2.04 us (1%)
    pallas_call x1, Pallas kernels, sum_step(): pl.pallas_call(functools.partial(sum_kernel, bricks, capacity), out_shape...  28.7 us
    ppermute x6, waiting for transfers between devices, body(): moving = [lax.ppermute(part, 'ori', along) for part in moving]  24.6 us
    ppermute x6, starting transfers between devices, body(): moving = [lax.ppermute(part, 'ori', along) for part in moving]  24.5 us
    pallas_call x6, Pallas kernels, score_step(): pl.pallas_call(functools.partial(score_kernel, chips, candidates, first),...  17.1 us
    ppermute x6, waiting for transfers between devices, add_up(): total += lax.ppermute(part, axis, perm).astype(jnp.float32)  16.8 us
    ppermute x6, starting transfers between devices, add_up(): total += lax.ppermute(part, axis, perm).astype(jnp.float32)  8.01 us
    ppermute x3, waiting for transfers between devices, body(): lax.ppermute(totals, 'ori', [(i, i ^ 2 * k) for i in range(orient_groups)])  5.58 us
    pallas_call x1, Pallas kernels, body(): pl.pallas_call(functools.partial(place_kernel, bricks, image_groups, capa...  4.74 us
  transfers between devices with their start and end apart: 24, of which 14 were waited for; matrix products, arithmetic and copies ran while one was open for 2% of the time, Pallas kernels for 13%

profile of v5, /device:TPU:0, one launch (start us, length us, event | category | flops | bytes accessed | tf_op | source)
XLA Modules:
  0.0 152.3 jit_solution(11842975327649053689)
XLA Ops:
  1.2 4.6 %collective-permute-start.1 = (bf16[256,2048]{1,0:T(8,128)(2,1)}, bf16[256,2048]{1,0:T(8,128)(2,1)S(1)}, u32[]{:S(2)}, u32[]{:S(2)}) collective-permute-start(bf16[256,2048]{1,0:T(8,128)(2,1)} %refs_0_.1), channel_id=1, source_target_pairs={{0,2},{2,4},{4,6},{3,1},{5,3},{7,5},{8,10},{10,12},{12,14},{11,9},... | collective-permute-start | bytes 3145736 | tf_op jit(solution)/shard_map/score/ppermute | solution.py:456
  5.7 3.5 %collective-permute-start.3 = (bf16[256,2048]{1,0:T(8,128)(2,1)S(1)}, bf16[256,2048]{1,0:T(8,128)(2,1)S(1)}, u32[]{:S(2)}, u32[]{:S(2)}) collective-permute-start(bf16[256,2048]{1,0:T(8,128)(2,1)S(1)} %collective-permute-done.refs_1_), channel_id=1, source_target_pairs={{0,2},{2,4},{4,6},{3,1},{5,3},{7,5},{8,10},{10,12},{12,14},{11,9},... | collective-permute-start | bytes 3145736 | tf_op jit(solution)/shard_map/score/ppermute | solution.py:456
  11.2 4.7 %place_segments.1 = (s32[64,1,256]{2,1,0:T(1,128)S(1)}, s32[4,32,256]{2,1,0:T(8,128)S(1)}) custom-call(s32[64,1,256]{2,1,0:T(1,128)S(1)} %reshape.38.dest_ref, s32[64,1,256]{2,1,0:T(1,128)S(1)} %reshape.40.rows_ref), custom_call_target="tpu_custom_call" | custom-call | flops 1000 | bytes 1000 | tf_op jit(solution)/shard_map/place_segments/place_segments/pallas_call | solution.py:422
  17.8 2.2 %copy-done.1 = bf16[1024,2048]{1,0:T(8,128)(2,1)S(1)} copy-done((bf16[1024,2048]{1,0:T(8,128)(2,1)S(1)}, bf16[1024,2048]{1,0:T(8,128)(2,1)}, u32[]{:S(2)}) %copy-start.1) | copy-done | bytes 4194328
  21.2 4.9 %score_blocks.6 = (f32[1024,128]{1,0:T(8,128)S(1)}, f32[8,1024,256]{2,1,0:T(8,128)S(1)}, bf16[2048,2048]{1,0:T(8,128)(2,1)S(1)}, f32[8,8,256]{2,1,0:T(8,128)S(1)}) custom-call(bf16[256,2048]{1,0:T(8,128)(2,1)S(1)} %copy-done.3, bf16[256,2048]{1,0:T(8,128)(2,1)S(1)} %collective-permute-done.refs_1_, bf16[1024,2048]{1,0:T(8,128)(2,1)S(1)} %copy-done.1), custom_call_target="tpu_custom_call" | custom-call | flops 1000 | bytes 1000 | tf_op jit(solution)/shard_map/score/score_blocks/pallas_call | solution.py:182
  26.2 3.5 %collective-permute-start.2 = (bf16[256,2048]{1,0:T(8,128)(2,1)S(1)}, bf16[256,2048]{1,0:T(8,128)(2,1)S(1)}, u32[]{:S(2)}, u32[]{:S(2)}) collective-permute-start(bf16[256,2048]{1,0:T(8,128)(2,1)S(1)} %collective-permute-done.1.refs_0_), channel_id=1, source_target_pairs={{0,2},{2,4},{4,6},{3,1},{5,3},{7,5},{8,10},{10,12},{12,14},{11,9},... | collective-permute-start | bytes 3145736 | tf_op jit(solution)/shard_map/score/ppermute | solution.py:456
  29.8 4.1 %collective-permute-start.5 = (bf16[256,2048]{1,0:T(8,128)(2,1)S(1)}, bf16[256,2048]{1,0:T(8,128)(2,1)S(1)}, u32[]{:S(2)}, u32[]{:S(2)}) collective-permute-start(bf16[256,2048]{1,0:T(8,128)(2,1)S(1)} %collective-permute-done.3.refs_0_), channel_id=1, source_target_pairs={{0,2},{2,4},{4,6},{3,1},{5,3},{7,5},{8,10},{10,12},{12,14},{11,9},... | collective-permute-start | bytes 3145736 | tf_op jit(solution)/shard_map/score/ppermute | solution.py:456
  33.9 8.0 %collective-permute-done.2.refs_0_ = bf16[256,2048]{1,0:T(8,128)(2,1)S(1)} collective-permute-done((bf16[256,2048]{1,0:T(8,128)(2,1)S(1)}, bf16[256,2048]{1,0:T(8,128)(2,1)S(1)}, u32[]{:S(2)}, u32[]{:S(2)}) %collective-permute-start.2) | collective-permute-done | bytes 1048608 | tf_op jit(solution)/shard_map/score/ppermute | solution.py:456
  41.9 4.4 %collective-permute-start.4 = (bf16[256,2048]{1,0:T(8,128)(2,1)S(1)}, bf16[256,2048]{1,0:T(8,128)(2,1)S(1)}, u32[]{:S(2)}, u32[]{:S(2)}) collective-permute-start(bf16[256,2048]{1,0:T(8,128)(2,1)S(1)} %collective-permute-done.2.refs_0_), channel_id=1, source_target_pairs={{0,2},{2,4},{4,6},{3,1},{5,3},{7,5},{8,10},{10,12},{12,14},{11,9},... | collective-permute-start | bytes 3145736 | tf_op jit(solution)/shard_map/score/ppermute | solution.py:456
  46.5 2.0 %score_blocks.7 = (f32[8,1024,256]{2,1,0:T(8,128)S(1)}, bf16[2048,2048]{1,0:T(8,128)(2,1)S(1)}, f32[8,8,256]{2,1,0:T(8,128)S(1)}) custom-call(bf16[256,2048]{1,0:T(8,128)(2,1)S(1)} %collective-permute-done.1.refs_0_, bf16[256,2048]{1,0:T(8,128)(2,1)S(1)} %collective-permute-done.6.refs_1_, ...), custom_call_target="tpu_custom_call", output_to_operand_aliasing={{0}: (4, {}), {1}: (5, {}), {2}: (6, {})} | custom-call | flops 1000 | bytes 1000 | tf_op jit(solution)/shard_map/score/score_blocks/pallas_call | solution.py:182
  48.5 4.7 %collective-permute-done.5.refs_0_ = bf16[256,2048]{1,0:T(8,128)(2,1)S(1)} collective-permute-done((bf16[256,2048]{1,0:T(8,128)(2,1)S(1)}, bf16[256,2048]{1,0:T(8,128)(2,1)S(1)}, u32[]{:S(2)}, u32[]{:S(2)}) %collective-permute-start.5) | collective-permute-done | bytes 1048608 | tf_op jit(solution)/shard_map/score/ppermute | solution.py:456
  53.2 4.4 %collective-permute-start.9 = (bf16[256,2048]{1,0:T(8,128)(2,1)S(1)}, bf16[256,2048]{1,0:T(8,128)(2,1)S(1)}, u32[]{:S(2)}, u32[]{:S(2)}) collective-permute-start(bf16[256,2048]{1,0:T(8,128)(2,1)S(1)} %collective-permute-done.5.refs_0_), channel_id=1, source_target_pairs={{0,2},{2,4},{4,6},{3,1},{5,3},{7,5},{8,10},{10,12},{12,14},{11,9},... | collective-permute-start | bytes 3145736 | tf_op jit(solution)/shard_map/score/ppermute | solution.py:456
  59.6 4.7 %collective-permute-done.4.refs_0_ = bf16[256,2048]{1,0:T(8,128)(2,1)S(1)} collective-permute-done((bf16[256,2048]{1,0:T(8,128)(2,1)S(1)}, bf16[256,2048]{1,0:T(8,128)(2,1)S(1)}, u32[]{:S(2)}, u32[]{:S(2)}) %collective-permute-start.4) | collective-permute-done | bytes 1048608 | tf_op jit(solution)/shard_map/score/ppermute | solution.py:456
  68.4 7.2 %collective-permute-done.9.refs_2_ = bf16[256,2048]{1,0:T(8,128)(2,1)S(1)} collective-permute-done((bf16[256,2048]{1,0:T(8,128)(2,1)S(1)}, bf16[256,2048]{1,0:T(8,128)(2,1)S(1)}, u32[]{:S(2)}, u32[]{:S(2)}) %collective-permute-start.9) | collective-permute-done | bytes 1048608 | tf_op jit(solution)/shard_map/score/ppermute | solution.py:456
  75.6 2.7 %collective-permute-done.12.refs_3_ = bf16[256,2048]{1,0:T(8,128)(2,1)S(1)} collective-permute-done((bf16[256,2048]{1,0:T(8,128)(2,1)S(1)}, bf16[256,2048]{1,0:T(8,128)(2,1)S(1)}, u32[]{:S(2)}, u32[]{:S(2)}) %collective-permute-start.12) | collective-permute-done | bytes 1048608 | tf_op jit(solution)/shard_map/score/ppermute | solution.py:448
  78.3 4.2 %score_blocks.11 = (f32[8,1024,256]{2,1,0:T(8,128)S(1)}, bf16[2048,2048]{1,0:T(8,128)(2,1)S(1)}, f32[8,8,256]{2,1,0:T(8,128)S(1)}) custom-call(bf16[256,2048]{1,0:T(8,128)(2,1)S(1)} %collective-permute-done.4.refs_0_, bf16[256,2048]{1,0:T(8,128)(2,1)S(1)} %collective-permute-done.8.refs_1_, ...), custom_call_target="tpu_custom_call", output_to_operand_aliasing={{0}: (6, {}), {1}: (7, {}), {2}: (8, {})} | custom-call | flops 1000 | bytes 1000 | tf_op jit(solution)/shard_map/score/score_blocks/pallas_call | solution.py:182
  83.9 3.8 %collective-permute-start.15 = (f32[8,8,256]{2,1,0:T(8,128)S(1)}, f32[8,8,256]{2,1,0:T(8,128)S(1)}, u32[]{:S(2)}, u32[]{:S(2)}) collective-permute-start(f32[8,8,256]{2,1,0:T(8,128)S(1)} %merge_totals.2.refs_0_), channel_id=1, source_target_pairs={{0,4},{1,5},{2,6},{3,7},{4,0},{5,1},{6,2},{7,3},{8,12},{9,13},{10,... | collective-permute-start | bytes 196616 | tf_op jit(solution)/shard_map/softmax_total/ppermute | solution.py:476
  88.3 3.5 %collective-permute-done.15.refs_2_ = f32[8,8,256]{2,1,0:T(8,128)S(1)} collective-permute-done((f32[8,8,256]{2,1,0:T(8,128)S(1)}, f32[8,8,256]{2,1,0:T(8,128)S(1)}, u32[]{:S(2)}, u32[]{:S(2)}) %collective-permute-start.15) | collective-permute-done | bytes 65568 | tf_op jit(solution)/shard_map/softmax_total/ppermute | solution.py:476
  91.7 2.1 %collective-permute-done.16.refs_3_ = f32[8,8,256]{2,1,0:T(8,128)S(1)} collective-permute-done((f32[8,8,256]{2,1,0:T(8,128)S(1)}, f32[8,8,256]{2,1,0:T(8,128)S(1)}, u32[]{:S(2)}, u32[]{:S(2)}) %collective-permute-start.16) | collective-permute-done | bytes 65568 | tf_op jit(solution)/shard_map/softmax_total/ppermute | solution.py:476
  93.9 28.7 %sum_and_grid.1 = (bf16[16,272,128]{2,1,0:T(8,128)(2,1)S(1)}, bf16[16,1024,128]{2,1,0:T(8,128)(2,1)S(1)}, f32[64,256]{1,0:T(8,128)S(1)}) custom-call(s32[16896]{0:T(1024)S(1)} %concatenate.3.slot_ref, f32[8,1024,256]{2,1,0:T(8,128)S(1)} %get-tuple-element.111.p_ref, f32[8,8,256]{2,1,0:T(8,128)S(1)} %get-tuple-element.112.refs_0_.stats_ref, ...), custom_call_target="tpu_custom_call" | custom-call | flops 8589934592 | bytes 25165824 | tf_op jit(solution)/shard_map/sum_and_grid/sum_and_grid/pallas_call | solution.py:377
  122.7 2.5 %grid_own_bricks.1 = f32[16,272,128]{2,1,0:T(8,128)S(1)} custom-call(bf16[16,1024,128]{2,1,0:T(8,128)(2,1)S(1)} %get-tuple-element.117.slots, f32[64,256]{1,0:T(8,128)S(1)} %get-tuple-element.118.volume, s32[32,1,1024]{2,1,0:T(1,128)S(1)} %reshape.42.map_ref), custom_call_target="tpu_custom_call" | custom-call | flops 1000 | bytes 1000 | tf_op jit(solution)/shard_map/brick_sums/grid_own_bricks/pallas_call | solution.py:361
  129.3 6.0 %collective-permute-done.18 = bf16[4,272,128]{2,1,0:T(8,128)(2,1)S(1)} collective-permute-done((bf16[4,272,128]{2,1,0:T(8,128)(2,1)S(1)}, bf16[4,272,128]{2,1,0:T(8,128)(2,1)S(1)}, u32[]{:S(2)}, u32[]{:S(2)}) %collective-permute-start.18) | collective-permute-done | bytes 278560 | tf_op jit(solution)/shard_map/brick_sums/ppermute | solution.py:494
  135.3 6.5 %collective-permute-done.19 = bf16[4,272,128]{2,1,0:T(8,128)(2,1)S(1)} collective-permute-done((bf16[4,272,128]{2,1,0:T(8,128)(2,1)S(1)}, bf16[4,272,128]{2,1,0:T(8,128)(2,1)S(1)}, u32[]{:S(2)}, u32[]{:S(2)}) %collective-permute-start.19) | collective-permute-done | bytes 278560 | tf_op jit(solution)/shard_map/brick_sums/ppermute | solution.py:494
  146.8 3.0 %collective-permute-done.22 = bf16[272,128]{1,0:T(8,128)(2,1)S(1)} collective-permute-done((bf16[272,128]{1,0:T(8,128)(2,1)S(1)}, bf16[272,128]{1,0:T(8,128)(2,1)S(1)}, u32[]{:S(2)}, u32[]{:S(2)}) %collective-permute-start.22) | collective-permute-done | bytes 69664 | tf_op jit(solution)/shard_map/brick_sums/ppermute | solution.py:494
  (58 shorter events, 25.5 us)
Async XLA Ops:
  0.6 5.1 %collective-permute-start = (bf16[256,2048]{1,0:T(8,128)(2,1)}, bf16[256,2048]{1,0:T(8,128)(2,1)S(1)}, u32[]{:S(2)}, u32[]{:S(2)}) collective-permute-start(bf16[256,2048]{1,0:T(8,128)(2,1)} %refs_0_.1), channel_id=1, source_target_pairs={{0,1},{1,0},{2,3},{3,2},{4,5},{5,4},{6,7},{7,6},{8,9},{9,8},{10,11... | collective-permute-start | bytes 3145736 | tf_op jit(solution)/shard_map/score/ppermute | solution.py:439
  1.2 25.0 %collective-permute-start.1 = (bf16[256,2048]{1,0:T(8,128)(2,1)}, bf16[256,2048]{1,0:T(8,128)(2,1)S(1)}, u32[]{:S(2)}, u32[]{:S(2)}) collective-permute-start(bf16[256,2048]{1,0:T(8,128)(2,1)} %refs_0_.1), channel_id=1, source_target_pairs={{0,2},{2,4},{4,6},{3,1},{5,3},{7,5},{8,10},{10,12},{12,14},{11,9},... | collective-permute-start | bytes 3145736 | tf_op jit(solution)/shard_map/score/ppermute | solution.py:456
  5.7 24.0 %collective-permute-start.3 = (bf16[256,2048]{1,0:T(8,128)(2,1)S(1)}, bf16[256,2048]{1,0:T(8,128)(2,1)S(1)}, u32[]{:S(2)}, u32[]{:S(2)}) collective-permute-start(bf16[256,2048]{1,0:T(8,128)(2,1)S(1)} %collective-permute-done.refs_1_), channel_id=1, source_target_pairs={{0,2},{2,4},{4,6},{3,1},{5,3},{7,5},{8,10},{10,12},{12,14},{11,9},... | collective-permute-start | bytes 3145736 | tf_op jit(solution)/shard_map/score/ppermute | solution.py:456
  26.2 15.7 %collective-permute-start.2 = (bf16[256,2048]{1,0:T(8,128)(2,1)S(1)}, bf16[256,2048]{1,0:T(8,128)(2,1)S(1)}, u32[]{:S(2)}, u32[]{:S(2)}) collective-permute-start(bf16[256,2048]{1,0:T(8,128)(2,1)S(1)} %collective-permute-done.1.refs_0_), channel_id=1, source_target_pairs={{0,2},{2,4},{4,6},{3,1},{5,3},{7,5},{8,10},{10,12},{12,14},{11,9},... | collective-permute-start | bytes 3145736 | tf_op jit(solution)/shard_map/score/ppermute | solution.py:456
  29.7 16.8 %collective-permute-start.6 = (bf16[256,2048]{1,0:T(8,128)(2,1)S(1)}, bf16[256,2048]{1,0:T(8,128)(2,1)S(1)}, u32[]{:S(2)}, u32[]{:S(2)}) collective-permute-start(bf16[256,2048]{1,0:T(8,128)(2,1)S(1)} %collective-permute-done.1.refs_0_), channel_id=1, source_target_pairs={{0,1},{1,0},{2,3},{3,2},{4,5},{5,4},{6,7},{7,6},{8,9},{9,8},{10,11... | collective-permute-start | bytes 3145736 | tf_op jit(solution)/shard_map/score/ppermute | solution.py:448
  29.8 23.4 %collective-permute-start.5 = (bf16[256,2048]{1,0:T(8,128)(2,1)S(1)}, bf16[256,2048]{1,0:T(8,128)(2,1)S(1)}, u32[]{:S(2)}, u32[]{:S(2)}) collective-permute-start(bf16[256,2048]{1,0:T(8,128)(2,1)S(1)} %collective-permute-done.3.refs_0_), channel_id=1, source_target_pairs={{0,2},{2,4},{4,6},{3,1},{5,3},{7,5},{8,10},{10,12},{12,14},{11,9},... | collective-permute-start | bytes 3145736 | tf_op jit(solution)/shard_map/score/ppermute | solution.py:456
  33.9 23.7 %collective-permute-start.7 = (bf16[256,2048]{1,0:T(8,128)(2,1)S(1)}, bf16[256,2048]{1,0:T(8,128)(2,1)S(1)}, u32[]{:S(2)}, u32[]{:S(2)}) collective-permute-start(bf16[256,2048]{1,0:T(8,128)(2,1)S(1)} %collective-permute-done.3.refs_0_), channel_id=1, source_target_pairs={{0,1},{1,0},{2,3},{3,2},{4,5},{5,4},{6,7},{7,6},{8,9},{9,8},{10,11... | collective-permute-start | bytes 3145736 | tf_op jit(solution)/shard_map/score/ppermute | solution.py:448
  41.9 22.5 %collective-permute-start.4 = (bf16[256,2048]{1,0:T(8,128)(2,1)S(1)}, bf16[256,2048]{1,0:T(8,128)(2,1)S(1)}, u32[]{:S(2)}, u32[]{:S(2)}) collective-permute-start(bf16[256,2048]{1,0:T(8,128)(2,1)S(1)} %collective-permute-done.2.refs_0_), channel_id=1, source_target_pairs={{0,2},{2,4},{4,6},{3,1},{5,3},{7,5},{8,10},{10,12},{12,14},{11,9},... | collective-permute-start | bytes 3145736 | tf_op jit(solution)/shard_map/score/ppermute | solution.py:456
  46.4 18.0 %collective-permute-start.11 = (bf16[256,2048]{1,0:T(8,128)(2,1)S(1)}, bf16[256,2048]{1,0:T(8,128)(2,1)S(1)}, u32[]{:S(2)}, u32[]{:S(2)}) collective-permute-start(bf16[256,2048]{1,0:T(8,128)(2,1)S(1)} %collective-permute-done.2.refs_0_), channel_id=1, source_target_pairs={{0,1},{1,0},{2,3},{3,2},{4,5},{5,4},{6,7},{7,6},{8,9},{9,8},{10,11... | collective-permute-start | bytes 3145736 | tf_op jit(solution)/shard_map/score/ppermute | solution.py:448
  53.2 13.2 %collective-permute-start.10 = (bf16[256,2048]{1,0:T(8,128)(2,1)S(1)}, bf16[256,2048]{1,0:T(8,128)(2,1)S(1)}, u32[]{:S(2)}, u32[]{:S(2)}) collective-permute-start(bf16[256,2048]{1,0:T(8,128)(2,1)S(1)} %collective-permute-done.5.refs_0_), channel_id=1, source_target_pairs={{0,1},{1,0},{2,3},{3,2},{4,5},{5,4},{6,7},{7,6},{8,9},{9,8},{10,11... | collective-permute-start | bytes 3145736 | tf_op jit(solution)/shard_map/score/ppermute | solution.py:448
  53.2 22.5 %collective-permute-start.9 = (bf16[256,2048]{1,0:T(8,128)(2,1)S(1)}, bf16[256,2048]{1,0:T(8,128)(2,1)S(1)}, u32[]{:S(2)}, u32[]{:S(2)}) collective-permute-start(bf16[256,2048]{1,0:T(8,128)(2,1)S(1)} %collective-permute-done.5.refs_0_), channel_id=1, source_target_pairs={{0,2},{2,4},{4,6},{3,1},{5,3},{7,5},{8,10},{10,12},{12,14},{11,9},... | collective-permute-start | bytes 3145736 | tf_op jit(solution)/shard_map/score/ppermute | solution.py:456
  64.4 11.2 %collective-permute-start.8 = (bf16[256,2048]{1,0:T(8,128)(2,1)S(1)}, bf16[256,2048]{1,0:T(8,128)(2,1)S(1)}, u32[]{:S(2)}, u32[]{:S(2)}) collective-permute-start(bf16[256,2048]{1,0:T(8,128)(2,1)S(1)} %collective-permute-done.4.refs_0_), channel_id=1, source_target_pairs={{0,1},{1,0},{2,3},{3,2},{4,5},{5,4},{6,7},{7,6},{8,9},{9,8},{10,11... | collective-permute-start | bytes 3145736 | tf_op jit(solution)/shard_map/score/ppermute | solution.py:448
  75.6 2.7 %collective-permute-start.12 = (bf16[256,2048]{1,0:T(8,128)(2,1)S(1)}, bf16[256,2048]{1,0:T(8,128)(2,1)S(1)}, u32[]{:S(2)}, u32[]{:S(2)}) collective-permute-start(bf16[256,2048]{1,0:T(8,128)(2,1)S(1)} %collective-permute-done.9.refs_2_), channel_id=1, source_target_pairs={{0,1},{1,0},{2,3},{3,2},{4,5},{5,4},{6,7},{7,6},{8,9},{9,8},{10,11... | collective-permute-start | bytes 3145736 | tf_op jit(solution)/shard_map/score/ppermute | solution.py:448
  82.4 1.3 collective-permute-start.13
  83.8 4.5 %collective-permute-start.14 = (f32[8,8,256]{2,1,0:T(8,128)S(1)}, f32[8,8,256]{2,1,0:T(8,128)S(1)}, u32[]{:S(2)}, u32[]{:S(2)}) collective-permute-start(f32[8,8,256]{2,1,0:T(8,128)S(1)} %merge_totals.2.refs_0_), channel_id=1, source_target_pairs={{0,2},{1,3},{2,0},{3,1},{4,6},{5,7},{6,4},{7,5},{8,10},{9,11},{10,... | collective-permute-start | bytes 196616 | tf_op jit(solution)/shard_map/softmax_total/ppermute | solution.py:476
  83.9 7.8 %collective-permute-start.15 = (f32[8,8,256]{2,1,0:T(8,128)S(1)}, f32[8,8,256]{2,1,0:T(8,128)S(1)}, u32[]{:S(2)}, u32[]{:S(2)}) collective-permute-start(f32[8,8,256]{2,1,0:T(8,128)S(1)} %merge_totals.2.refs_0_), channel_id=1, source_target_pairs={{0,4},{1,5},{2,6},{3,7},{4,0},{5,1},{6,2},{7,3},{8,12},{9,13},{10,... | collective-permute-start | bytes 196616 | tf_op jit(solution)/shard_map/softmax_total/ppermute | solution.py:476
  87.7 6.2 %collective-permute-start.16 = (f32[8,8,256]{2,1,0:T(8,128)S(1)}, f32[8,8,256]{2,1,0:T(8,128)S(1)}, u32[]{:S(2)}, u32[]{:S(2)}) collective-permute-start(f32[8,8,256]{2,1,0:T(8,128)S(1)} %merge_totals.2.refs_0_), channel_id=1, source_target_pairs={{0,6},{1,7},{2,4},{3,5},{4,2},{5,3},{6,0},{7,1},{8,14},{9,15},{10,... | collective-permute-start | bytes 196616 | tf_op jit(solution)/shard_map/softmax_total/ppermute | solution.py:476
  122.6 2.8 %collective-permute-start.17 = (bf16[16,272,128]{2,1,0:T(8,128)(2,1)S(1)}, bf16[16,272,128]{2,1,0:T(8,128)(2,1)S(1)}, u32[]{:S(2)}, u32[]{:S(2)}) collective-permute-start(bf16[16,272,128]{2,1,0:T(8,128)(2,1)S(1)} %get-tuple-element.119), channel_id=1, source_target_pairs={{0,1},{1,0},{2,3},{3,2},{4,5},{5,4},{6,7},{7,6},{8,9},{9,8},{10,11... | collective-permute-start | bytes 3342344 | tf_op jit(solution)/shard_map/brick_sums/ppermute | solution.py:497
  125.8 9.6 %collective-permute-start.18 = (bf16[4,272,128]{2,1,0:T(8,128)(2,1)S(1)}, bf16[4,272,128]{2,1,0:T(8,128)(2,1)S(1)}, u32[]{:S(2)}, u32[]{:S(2)}) collective-permute-start(bf16[4,272,128]{2,1,0:T(8,128)(2,1)S(1)} %get-tuple-element.124), channel_id=1, source_target_pairs={{0,8},{8,0},{16,24},{24,16},{1,9},{9,1},{17,25},{25,17},{2,10},{10... | collective-permute-start | bytes 835592 | tf_op jit(solution)/shard_map/brick_sums/ppermute | solution.py:494
  127.3 14.5 %collective-permute-start.19 = (bf16[4,272,128]{2,1,0:T(8,128)(2,1)S(1)}, bf16[4,272,128]{2,1,0:T(8,128)(2,1)S(1)}, u32[]{:S(2)}, u32[]{:S(2)}) collective-permute-start(bf16[4,272,128]{2,1,0:T(8,128)(2,1)S(1)} %get-tuple-element.126), channel_id=1, source_target_pairs={{0,16},{8,24},{16,0},{24,8},{1,17},{9,25},{17,1},{25,9},{2,18},{10... | collective-permute-start | bytes 835592 | tf_op jit(solution)/shard_map/brick_sums/ppermute | solution.py:494
  128.9 13.0 %collective-permute-start.20 = (bf16[4,272,128]{2,1,0:T(8,128)(2,1)S(1)}, bf16[4,272,128]{2,1,0:T(8,128)(2,1)S(1)}, u32[]{:S(2)}, u32[]{:S(2)}) collective-permute-start(bf16[4,272,128]{2,1,0:T(8,128)(2,1)S(1)} %get-tuple-element.125), channel_id=1, source_target_pairs={{0,24},{8,16},{16,8},{24,0},{1,25},{9,17},{17,9},{25,1},{2,26},{10... | collective-permute-start | bytes 835592 | tf_op jit(solution)/shard_map/brick_sums/ppermute | solution.py:494
  142.1 4.8 %collective-permute-start.21 = (bf16[272,128]{1,0:T(8,128)(2,1)S(1)}, bf16[272,128]{1,0:T(8,128)(2,1)S(1)}, u32[]{:S(2)}, u32[]{:S(2)}) collective-permute-start(bf16[272,128]{1,0:T(8,128)(2,1)S(1)} %get-tuple-element.127), channel_id=1, source_target_pairs={{0,2},{1,3},{2,0},{3,1},{4,6},{5,7},{6,4},{7,5},{8,10},{9,11},{10,... | collective-permute-start | bytes 208904 | tf_op jit(solution)/shard_map/brick_sums/ppermute | solution.py:494
  142.9 6.9 %collective-permute-start.22 = (bf16[272,128]{1,0:T(8,128)(2,1)S(1)}, bf16[272,128]{1,0:T(8,128)(2,1)S(1)}, u32[]{:S(2)}, u32[]{:S(2)}) collective-permute-start(bf16[272,128]{1,0:T(8,128)(2,1)S(1)} %get-tuple-element.129), channel_id=1, source_target_pairs={{0,4},{1,5},{2,6},{3,7},{4,0},{5,1},{6,2},{7,3},{8,12},{9,13},{10,... | collective-permute-start | bytes 208904 | tf_op jit(solution)/shard_map/brick_sums/ppermute | solution.py:494
  144.6 6.2 %collective-permute-start.23 = (bf16[272,128]{1,0:T(8,128)(2,1)S(1)}, bf16[272,128]{1,0:T(8,128)(2,1)S(1)}, u32[]{:S(2)}, u32[]{:S(2)}) collective-permute-start(bf16[272,128]{1,0:T(8,128)(2,1)S(1)} %get-tuple-element.128), channel_id=1, source_target_pairs={{0,6},{1,7},{2,4},{3,5},{4,2},{5,3},{6,0},{7,1},{8,14},{9,15},{10,... | collective-permute-start | bytes 208904 | tf_op jit(solution)/shard_map/brick_sums/ppermute | solution.py:494
  (4 other events, 179.4 us)

commit v6 on v5

--- a/solution.py
+++ b/solution.py
@@ -10,6 +10,7 @@
 BRICK_ROWS = 256
 EXTRA_ROWS = 16
 TILE = 256
+JOINED = 2
 temper_scale = 4.0
 
 ANY = pl.BlockSpec(memory_space=pl.ANY)
@@ -69,14 +70,11 @@
     n = len(candidates)
     images, refs = refs[:n], refs[n:]
     proj_ref, refs = refs[0], refs[1:]
-    if not first:
-        norm_in, refs = refs[0], refs[4:]
     if first:
-        norm_ref, refs = refs[0], refs[1:]
+        norm_ref, p_ref, x_ref, stat_ref, sem = refs
     else:
-        norm_ref = norm_in
-    p_hbm, x_hbm, stat_hbm, held, p_buf, stat_buf, sem_in, sem_p, sem_x, sem_s = refs
-    block = held.shape[1]
+        norm_ref, _, _, _, p_ref, x_ref, stat_ref, sem = refs
+    block = images[0].shape[0]
     orients = proj_ref.shape[0]
     chunk = min(512, orients)
     me = lax.axis_index("ori")
@@ -88,21 +86,15 @@
         valid = jnp.logical_and(source >= 0, source < chips)
         plan.append((valid, jnp.clip(source, 0, chips - 1) * 2 + (core if own else 1 - core)))
 
-    def copies(i):
-        slot = plan[i][1]
-        rows = pl.ds(pl.multiple_of(slot * block, block), block)
-        return (
-            lambda: pltpu.make_async_copy(images[i], held.at[i], sem_in.at[i]),
-            lambda: pltpu.make_async_copy(held.at[i], x_hbm.at[rows], sem_x.at[i]),
-            lambda: pltpu.make_async_copy(p_buf.at[i], p_hbm.at[slot], sem_p.at[i]),
-            lambda: pltpu.make_async_copy(stat_buf.at[i], stat_hbm.at[slot], sem_s.at[i]),
-        )
+    def keep(i):
+        rows = pl.ds(pl.multiple_of(plan[i][1] * block, block), block)
+        return pltpu.make_async_copy(images[i], x_ref.at[rows], sem.at[i])
 
     for i in range(n):
 
         @pl.when(plan[i][0])
         def _(i=i):
-            copies(i)[0]().start()
+            keep(i).start()
 
     if first:
 
@@ -119,42 +111,27 @@
 
         @pl.when(plan[i][0])
         def _(i=i):
-            fetch, keep, out, stats = copies(i)
-            fetch().wait()
-            keep().start()
-
-            def score(r, largest):
-                rows = pl.ds(pl.multiple_of(r * chunk, chunk), chunk)
-                found = dot(proj_ref[rows, :], held[i], NT)
-                norm = norm_ref[rows, 0:1]
-                found = temper_scale * (found - 0.5 * norm)
-                p_buf[i, rows, :] = found
-                return jnp.maximum(largest, jnp.max(found, axis=0, keepdims=True))
-
-            largest = lax.fori_loop(
-                0, orients // chunk, score, jnp.full((1, block), -jnp.inf, jnp.float32)
-            )
-
-            def exponential(r, total):
-                rows = pl.ds(pl.multiple_of(r * chunk, chunk), chunk)
-                value = jnp.exp(p_buf[i, rows, :] - largest)
-                p_buf[i, rows, :] = value
-                return total + jnp.sum(value, axis=0, keepdims=True)
-
-            total = lax.fori_loop(
-                0, orients // chunk, exponential, jnp.zeros((1, block), jnp.float32)
-            )
-            out().start()
+            slot = plan[i][1]
+            chunks = [slice(r, r + chunk) for r in range(0, orients, chunk)]
+            largest = jnp.full((1, block), -jnp.inf, jnp.float32)
+            for rows in chunks:
+                found = dot(proj_ref[rows, :], images[i][...], NT)
+                found = temper_scale * (found - 0.5 * norm_ref[rows, 0:1])
+                p_ref[slot, rows, :] = found
+                largest = jnp.maximum(largest, jnp.max(found, axis=0, keepdims=True))
+            total = jnp.zeros((1, block), jnp.float32)
+            for rows in chunks:
+                value = jnp.exp(p_ref[slot, rows, :] - largest)
+                p_ref[slot, rows, :] = value
+                total += jnp.sum(value, axis=0, keepdims=True)
             pick = lax.broadcasted_iota(jnp.int32, (8, block), 0) == 0
-            stat_buf[i] = jnp.where(pick, largest, total)
-            stats().start()
+            stat_ref[slot] = jnp.where(pick, largest, total)
 
     for i in range(n):
 
         @pl.when(plan[i][0])
         def _(i=i):
-            for copy in copies(i)[1:]:
-                copy().wait()
+            keep(i).wait()
 
 
 def score_step(chips, candidates, images, projections, carry):
@@ -168,33 +145,24 @@
         jax.ShapeDtypeStruct((blocks * block, width), jnp.bfloat16),
         jax.ShapeDtypeStruct((blocks, 8, block), jnp.float32),
     ]
-    in_specs = [ANY] * n + [VMEM]
+    in_specs = [VMEM] * (n + 1)
     args = list(images) + [projections]
     if first:
         out_shape = [jax.ShapeDtypeStruct((orients, 128), jnp.float32)] + shapes
-        out_specs = [VMEM] + [ANY] * 3
         aliases = {}
     else:
-        in_specs += [VMEM] + [ANY] * 3
+        in_specs += [VMEM] * 4
         args += list(carry)
-        out_shape, out_specs = shapes, [ANY] * 3
+        out_shape = shapes
         aliases = {n + 2 + k: k for k in range(3)}
     out = pl.pallas_call(
         functools.partial(score_kernel, chips, candidates, first),
         out_shape=out_shape,
         in_specs=in_specs,
-        out_specs=out_specs,
-        scratch_shapes=[
-            pltpu.VMEM((n, block, width), jnp.bfloat16),
-            pltpu.VMEM((n, orients, block), jnp.float32),
-            pltpu.VMEM((n, 8, block), jnp.float32),
-            pltpu.SemaphoreType.DMA((n,)),
-            pltpu.SemaphoreType.DMA((n,)),
-            pltpu.SemaphoreType.DMA((n,)),
-            pltpu.SemaphoreType.DMA((n,)),
-        ],
+        out_specs=[VMEM] * len(out_shape),
+        scratch_shapes=[pltpu.SemaphoreType.DMA((n,))],
         input_output_aliases=aliases,
-        compiler_params=pltpu.CompilerParams(vmem_limit_bytes=14 << 20),
+        compiler_params=pltpu.CompilerParams(vmem_limit_bytes=10 << 20),
         cost_estimate=pl.CostEstimate(flops=1000, bytes_accessed=1000, transcendentals=0),
         name="score_blocks",
     )(*args)
@@ -244,6 +212,8 @@
 ):
     blocks, orients, block = p_ref.shape
     owned = dest_ref.shape[2]
+    taken = weights.shape[0]
+    joined = taken // owned
     groups = orients // owned
     segments = dest_ref.shape[0] // groups
     per_tile = TILE // 128
@@ -260,10 +230,10 @@
 
     def scatter(held, base):
         for s in range(per_tile):
-            for r in range(owned // 8):
+            for r in range(taken // 8):
                 values = held[r * 8 : r * 8 + 8, s * 128 : (s + 1) * 128]
                 for k in range(8):
-                    slot = slot_ref[base + s * owned + r * 8 + k]
+                    slot = slot_ref[base + s * taken + r * 8 + k]
                     slots[pl.ds(slot, 1), :] = values[k : k + 1, :]
 
     def product(t):
@@ -271,7 +241,7 @@
         return dot(weights[...], x_ref[:, columns])
 
     def group(g, ignored):
-        rows = pl.ds(pl.multiple_of(g * owned, owned), owned)
+        rows = pl.ds(pl.multiple_of(g * taken, taken), taken)
         for k in range(blocks):
             scale = jnp.exp(stats_ref[k, 0:1] - totals_ref[k, 0:1]) / totals_ref[k, 1:2]
             weights[:, k * block : (k + 1) * block] = (p_ref[k, rows, :] * scale).astype(
@@ -282,28 +252,34 @@
         high = sums.astype(jnp.bfloat16).astype(jnp.float32)
         low = sums - high
 
-        def weigh(s):
-            dest = dest_ref[g * segments + s]
-            member = lax.broadcasted_iota(jnp.int32, (bricks, owned), 0) == dest
-            parts = [jnp.where(member, part, 0.0).astype(jnp.bfloat16) for part in (high, low)]
-            landed = one_hot_rows(BRICK_ROWS, rows_ref[g * segments + s])
+        def weigh(s, h):
+            lanes = slice(h * owned, (h + 1) * owned)
+            at = (g * joined + h) * segments + s
+            member = lax.broadcasted_iota(jnp.int32, (bricks, owned), 0) == dest_ref[at]
+            parts = [
+                jnp.where(member, part[:, lanes], 0.0).astype(jnp.bfloat16)
+                for part in (high, low)
+            ]
+            landed = one_hot_rows(BRICK_ROWS, rows_ref[at])
             return jnp.concatenate(parts, axis=0), landed
 
         def pair(j, ignored):
-            both = [weigh(2 * j * per_tile + k) for k in range(2 * per_tile)]
+            both = [
+                weigh(2 * j * per_tile + k, h) for k in range(2 * per_tile) for h in range(joined)
+            ]
             carried = jnp.concatenate([first for first, _ in both], axis=1)
             landed = jnp.concatenate([second for _, second in both], axis=1)
             volume[...] += dot(carried, landed, NT)
-            base = (g * segments + 2 * j * per_tile) * owned
+            base = (g * segments + 2 * j * per_tile) * taken
             even[...] = product(2 * j)
             scatter(odd, base)
             odd[...] = product(2 * j + 1)
-            scatter(even, base + per_tile * owned)
+            scatter(even, base + per_tile * taken)
             return ignored
 
         return lax.fori_loop(0, tiles // 2, pair, ignored)
 
-    lax.fori_loop(0, groups, group, 0)
+    lax.fori_loop(0, groups // joined, group, 0)
     scatter(odd, groups * segments * owned)
     span = map_ref.shape[2]
 
@@ -373,6 +349,7 @@
     blocks, orients, block = p.shape
     width = x.shape[1]
     owned = orients // groups
+    joined = JOINED
     shape = (bricks // 2, BRICK_ROWS + EXTRA_ROWS, 128)
     return pl.pallas_call(
         functools.partial(sum_kernel, bricks, capacity),
@@ -384,12 +361,12 @@
         in_specs=[SMEM] + [VMEM] * 7,
         out_specs=[VMEM] * 3,
         scratch_shapes=[
-            pltpu.VMEM((owned, blocks * block), jnp.bfloat16),
-            pltpu.VMEM((owned, TILE), jnp.float32),
-            pltpu.VMEM((owned, TILE), jnp.float32),
+            pltpu.VMEM((joined * owned, blocks * block), jnp.bfloat16),
+            pltpu.VMEM((joined * owned, TILE), jnp.float32),
+            pltpu.VMEM((joined * owned, TILE), jnp.float32),
             pltpu.VMEM((bricks * groups * capacity + 512, 128), jnp.float32),
         ],
-        compiler_params=pltpu.CompilerParams(vmem_limit_bytes=19 << 20),
+        compiler_params=pltpu.CompilerParams(vmem_limit_bytes=21 << 20),
         cost_estimate=pl.CostEstimate(
             flops=2 * blocks * block * orients * width, bytes_accessed=24 << 20, transcendentals=0
         ),
@@ -432,7 +409,10 @@
             name="place_segments",
         )(dest, rows)
         row_map = row_map[:, :, :capacity].transpose(1, 0, 2).reshape(bricks, 1, image_groups * capacity)
-        unused = jnp.full(((TILE // 128) * owned,), bricks * image_groups * capacity, jnp.int32)
+        slot = slot.reshape(image_groups // JOINED, JOINED, segments, owned).transpose(0, 2, 1, 3)
+        unused = jnp.full(
+            ((TILE // 128) * JOINED * owned,), bricks * image_groups * capacity, jnp.int32
+        )
         placed = (jnp.concatenate([unused, slot.reshape(-1)]), row_map, dest, rows)
 
     with jax.named_scope("score"):

time: 153 us -> 149 us (0.974)
  Pallas kernels: 53.2 us -> 46.5 us
  waiting for transfers between devices: 51 us -> 52.7 us
    pallas_call x1, Pallas kernels: 28.7 us -> 25.3 us  [sum_step(): pl.pallas_call(functools.partial(sum_kernel, bricks, capacity), out_shape...]
    pallas_call x6, Pallas kernels: 17.1 us -> 13.9 us  [score_step(): pl.pallas_call(functools.partial(score_kernel, chips, candidates, first),...]
    unnamed x8 -> x10, local copies, waits for them, and re-layouts: 3.42 us -> 3.46 us
  transfers between devices with their start and end apart: 24 -> 24, of which waited for: 14 -> 15; matrix products, arithmetic and copies ran while one was open for 2% -> 3% of each run, Pallas kernels for 13% -> 12%
where the time goes in v6:
time: 149 us; the launch traced here: 148 us
  waiting for transfers between devices  52.7 us (35%)
  Pallas kernels  46.5 us (31%)
  starting transfers between devices  38.7 us (26%)
  local copies, waits for them, and re-layouts  6.39 us (4%)
  other arithmetic  2.04 us (1%)
    ppermute x6, waiting for transfers between devices, body(): moving = [lax.ppermute(part, 'ori', along) for part in moving]  25.7 us
    pallas_call x1, Pallas kernels, sum_step(): pl.pallas_call(functools.partial(sum_kernel, bricks, capacity), out_shape...  25.3 us
    ppermute x6, starting transfers between devices, body(): moving = [lax.ppermute(part, 'ori', along) for part in moving]  24.9 us
    ppermute x6, waiting for transfers between devices, add_up(): total += lax.ppermute(part, axis, perm).astype(jnp.float32)  16.8 us
    pallas_call x6, Pallas kernels, score_step(): pl.pallas_call(functools.partial(score_kernel, chips, candidates, first),...  13.9 us
    ppermute x6, starting transfers between devices, add_up(): total += lax.ppermute(part, axis, perm).astype(jnp.float32)  8.01 us
    ppermute x3, waiting for transfers between devices, body(): lax.ppermute(totals, 'ori', [(i, i ^ 2 * k) for i in range(orient_groups)])  6.16 us
    ppermute x3, starting transfers between devices, body(): lax.ppermute(totals, 'ori', [(i, i ^ 2 * k) for i in range(orient_groups)])  4.81 us
  transfers between devices with their start and end apart: 24, of which 15 were waited for; matrix products, arithmetic and copies ran while one was open for 3% of the time, Pallas kernels for 12%

profile of v6, /device:TPU:0, one launch (start us, length us, event | category | flops | bytes accessed | tf_op | source)
XLA Modules:
  0.0 148.1 jit_solution(10042898112956015194)
XLA Ops:
  1.2 4.6 %collective-permute-start.1 = (bf16[256,2048]{1,0:T(8,128)(2,1)}, bf16[256,2048]{1,0:T(8,128)(2,1)S(1)}, u32[]{:S(2)}, u32[]{:S(2)}) collective-permute-start(bf16[256,2048]{1,0:T(8,128)(2,1)} %refs_0_.1), channel_id=1, source_target_pairs={{0,2},{2,4},{4,6},{3,1},{5,3},{7,5},{8,10},{10,12},{12,14},{11,9},... | collective-permute-start | bytes 3145736 | tf_op jit(solution)/shard_map/score/ppermute | solution.py:436
  5.7 3.5 %collective-permute-start.3 = (bf16[256,2048]{1,0:T(8,128)(2,1)S(1)}, bf16[256,2048]{1,0:T(8,128)(2,1)S(1)}, u32[]{:S(2)}, u32[]{:S(2)}) collective-permute-start(bf16[256,2048]{1,0:T(8,128)(2,1)S(1)} %collective-permute-done.refs_1_), channel_id=1, source_target_pairs={{0,2},{2,4},{4,6},{3,1},{5,3},{7,5},{8,10},{10,12},{12,14},{11,9},... | collective-permute-start | bytes 3145736 | tf_op jit(solution)/shard_map/score/ppermute | solution.py:436
  11.2 4.7 %place_segments.1 = (s32[64,1,256]{2,1,0:T(1,128)S(1)}, s32[4,32,256]{2,1,0:T(8,128)S(1)}) custom-call(s32[64,1,256]{2,1,0:T(1,128)S(1)} %reshape.41.dest_ref, s32[64,1,256]{2,1,0:T(1,128)S(1)} %reshape.43.rows_ref), custom_call_target="tpu_custom_call" | custom-call | flops 1000 | bytes 1000 | tf_op jit(solution)/shard_map/place_segments/place_segments/pallas_call | solution.py:399
  17.9 2.2 %copy-done.1 = bf16[1024,2048]{1,0:T(8,128)(2,1)S(1)} copy-done((bf16[1024,2048]{1,0:T(8,128)(2,1)S(1)}, bf16[1024,2048]{1,0:T(8,128)(2,1)}, u32[]{:S(2)}) %copy-start.1) | copy-done | bytes 4194328
  21.3 3.9 %score_blocks.6 = (f32[1024,128]{1,0:T(8,128)S(1)}, f32[8,1024,256]{2,1,0:T(8,128)S(1)}, bf16[2048,2048]{1,0:T(8,128)(2,1)S(1)}, f32[8,8,256]{2,1,0:T(8,128)S(1)}) custom-call(bf16[256,2048]{1,0:T(8,128)(2,1)S(1)} %copy-done.3, bf16[256,2048]{1,0:T(8,128)(2,1)S(1)} %collective-permute-done.refs_1_, bf16[1024,2048]{1,0:T(8,128)(2,1)S(1)} %copy-done.1), custom_call_target="tpu_custom_call" | custom-call | flops 1000 | bytes 1000 | tf_op jit(solution)/shard_map/score/score_blocks/pallas_call | solution.py:158
  25.2 3.5 %collective-permute-start.2 = (bf16[256,2048]{1,0:T(8,128)(2,1)S(1)}, bf16[256,2048]{1,0:T(8,128)(2,1)S(1)}, u32[]{:S(2)}, u32[]{:S(2)}) collective-permute-start(bf16[256,2048]{1,0:T(8,128)(2,1)S(1)} %collective-permute-done.1.refs_0_), channel_id=1, source_target_pairs={{0,2},{2,4},{4,6},{3,1},{5,3},{7,5},{8,10},{10,12},{12,14},{11,9},... | collective-permute-start | bytes 3145736 | tf_op jit(solution)/shard_map/score/ppermute | solution.py:436
  29.4 4.4 %collective-permute-start.5 = (bf16[256,2048]{1,0:T(8,128)(2,1)S(1)}, bf16[256,2048]{1,0:T(8,128)(2,1)S(1)}, u32[]{:S(2)}, u32[]{:S(2)}) collective-permute-start(bf16[256,2048]{1,0:T(8,128)(2,1)S(1)} %collective-permute-done.3.refs_0_), channel_id=1, source_target_pairs={{0,2},{2,4},{4,6},{3,1},{5,3},{7,5},{8,10},{10,12},{12,14},{11,9},... | collective-permute-start | bytes 3145736 | tf_op jit(solution)/shard_map/score/ppermute | solution.py:436
  33.9 7.0 %collective-permute-done.2.refs_0_ = bf16[256,2048]{1,0:T(8,128)(2,1)S(1)} collective-permute-done((bf16[256,2048]{1,0:T(8,128)(2,1)S(1)}, bf16[256,2048]{1,0:T(8,128)(2,1)S(1)}, u32[]{:S(2)}, u32[]{:S(2)}) %collective-permute-start.2) | collective-permute-done | bytes 1048608 | tf_op jit(solution)/shard_map/score/ppermute | solution.py:436
  41.0 4.4 %collective-permute-start.4 = (bf16[256,2048]{1,0:T(8,128)(2,1)S(1)}, bf16[256,2048]{1,0:T(8,128)(2,1)S(1)}, u32[]{:S(2)}, u32[]{:S(2)}) collective-permute-start(bf16[256,2048]{1,0:T(8,128)(2,1)S(1)} %collective-permute-done.2.refs_0_), channel_id=1, source_target_pairs={{0,2},{2,4},{4,6},{3,1},{5,3},{7,5},{8,10},{10,12},{12,14},{11,9},... | collective-permute-start | bytes 3145736 | tf_op jit(solution)/shard_map/score/ppermute | solution.py:436
  47.1 5.1 %collective-permute-done.5.refs_0_ = bf16[256,2048]{1,0:T(8,128)(2,1)S(1)} collective-permute-done((bf16[256,2048]{1,0:T(8,128)(2,1)S(1)}, bf16[256,2048]{1,0:T(8,128)(2,1)S(1)}, u32[]{:S(2)}, u32[]{:S(2)}) %collective-permute-start.5) | collective-permute-done | bytes 1048608 | tf_op jit(solution)/shard_map/score/ppermute | solution.py:436
  52.2 4.4 %collective-permute-start.9 = (bf16[256,2048]{1,0:T(8,128)(2,1)S(1)}, bf16[256,2048]{1,0:T(8,128)(2,1)S(1)}, u32[]{:S(2)}, u32[]{:S(2)}) collective-permute-start(bf16[256,2048]{1,0:T(8,128)(2,1)S(1)} %collective-permute-done.5.refs_0_), channel_id=1, source_target_pairs={{0,2},{2,4},{4,6},{3,1},{5,3},{7,5},{8,10},{10,12},{12,14},{11,9},... | collective-permute-start | bytes 3145736 | tf_op jit(solution)/shard_map/score/ppermute | solution.py:436
  58.3 5.2 %collective-permute-done.4.refs_0_ = bf16[256,2048]{1,0:T(8,128)(2,1)S(1)} collective-permute-done((bf16[256,2048]{1,0:T(8,128)(2,1)S(1)}, bf16[256,2048]{1,0:T(8,128)(2,1)S(1)}, u32[]{:S(2)}, u32[]{:S(2)}) %collective-permute-start.4) | collective-permute-done | bytes 1048608 | tf_op jit(solution)/shard_map/score/ppermute | solution.py:436
  66.8 7.8 %collective-permute-done.9.refs_2_ = bf16[256,2048]{1,0:T(8,128)(2,1)S(1)} collective-permute-done((bf16[256,2048]{1,0:T(8,128)(2,1)S(1)}, bf16[256,2048]{1,0:T(8,128)(2,1)S(1)}, u32[]{:S(2)}, u32[]{:S(2)}) %collective-permute-start.9) | collective-permute-done | bytes 1048608 | tf_op jit(solution)/shard_map/score/ppermute | solution.py:436
  74.7 2.7 %collective-permute-done.12.refs_3_ = bf16[256,2048]{1,0:T(8,128)(2,1)S(1)} collective-permute-done((bf16[256,2048]{1,0:T(8,128)(2,1)S(1)}, bf16[256,2048]{1,0:T(8,128)(2,1)S(1)}, u32[]{:S(2)}, u32[]{:S(2)}) %collective-permute-start.12) | collective-permute-done | bytes 1048608 | tf_op jit(solution)/shard_map/score/ppermute | solution.py:428
  77.3 3.4 %score_blocks.11 = (f32[8,1024,256]{2,1,0:T(8,128)S(1)}, bf16[2048,2048]{1,0:T(8,128)(2,1)S(1)}, f32[8,8,256]{2,1,0:T(8,128)S(1)}) custom-call(bf16[256,2048]{1,0:T(8,128)(2,1)S(1)} %collective-permute-done.4.refs_0_, bf16[256,2048]{1,0:T(8,128)(2,1)S(1)} %collective-permute-done.8.refs_1_, ...), custom_call_target="tpu_custom_call", output_to_operand_aliasing={{0}: (6, {}), {1}: (7, {}), {2}: (8, {})} | custom-call | flops 1000 | bytes 1000 | tf_op jit(solution)/shard_map/score/score_blocks/pallas_call | solution.py:158
  82.2 4.7 %collective-permute-start.15 = (f32[8,8,256]{2,1,0:T(8,128)S(1)}, f32[8,8,256]{2,1,0:T(8,128)S(1)}, u32[]{:S(2)}, u32[]{:S(2)}) collective-permute-start(f32[8,8,256]{2,1,0:T(8,128)S(1)} %merge_totals.2.refs_0_), channel_id=1, source_target_pairs={{0,4},{1,5},{2,6},{3,7},{4,0},{5,1},{6,2},{7,3},{8,12},{9,13},{10,... | collective-permute-start | bytes 196616 | tf_op jit(solution)/shard_map/softmax_total/ppermute | solution.py:456
  86.9 4.0 %collective-permute-done.15.refs_2_ = f32[8,8,256]{2,1,0:T(8,128)S(1)} collective-permute-done((f32[8,8,256]{2,1,0:T(8,128)S(1)}, f32[8,8,256]{2,1,0:T(8,128)S(1)}, u32[]{:S(2)}, u32[]{:S(2)}) %collective-permute-start.15) | collective-permute-done | bytes 65568 | tf_op jit(solution)/shard_map/softmax_total/ppermute | solution.py:456
  91.0 2.1 %collective-permute-done.16.refs_3_ = f32[8,8,256]{2,1,0:T(8,128)S(1)} collective-permute-done((f32[8,8,256]{2,1,0:T(8,128)S(1)}, f32[8,8,256]{2,1,0:T(8,128)S(1)}, u32[]{:S(2)}, u32[]{:S(2)}) %collective-permute-start.16) | collective-permute-done | bytes 65568 | tf_op jit(solution)/shard_map/softmax_total/ppermute | solution.py:456
  93.1 25.3 %sum_and_grid.1 = (bf16[16,272,128]{2,1,0:T(8,128)(2,1)S(1)}, bf16[16,1024,128]{2,1,0:T(8,128)(2,1)S(1)}, f32[64,256]{1,0:T(8,128)S(1)}) custom-call(s32[17408]{0:T(1024)S(1)} %concatenate.3.slot_ref, f32[8,1024,256]{2,1,0:T(8,128)S(1)} %get-tuple-element.111.p_ref, f32[8,8,256]{2,1,0:T(8,128)S(1)} %get-tuple-element.112.refs_0_.stats_ref, ...), custom_call_target="tpu_custom_call" | custom-call | flops 8589934592 | bytes 25165824 | tf_op jit(solution)/shard_map/sum_and_grid/sum_and_grid/pallas_call | solution.py:354
  118.5 2.5 %grid_own_bricks.1 = f32[16,272,128]{2,1,0:T(8,128)S(1)} custom-call(bf16[16,1024,128]{2,1,0:T(8,128)(2,1)S(1)} %get-tuple-element.117.slots, f32[64,256]{1,0:T(8,128)S(1)} %get-tuple-element.118.volume, s32[32,1,1024]{2,1,0:T(1,128)S(1)} %reshape.46.map_ref), custom_call_target="tpu_custom_call" | custom-call | flops 1000 | bytes 1000 | tf_op jit(solution)/shard_map/brick_sums/grid_own_bricks/pallas_call | solution.py:337
  125.2 6.0 %collective-permute-done.18 = bf16[4,272,128]{2,1,0:T(8,128)(2,1)S(1)} collective-permute-done((bf16[4,272,128]{2,1,0:T(8,128)(2,1)S(1)}, bf16[4,272,128]{2,1,0:T(8,128)(2,1)S(1)}, u32[]{:S(2)}, u32[]{:S(2)}) %collective-permute-start.18) | collective-permute-done | bytes 278560 | tf_op jit(solution)/shard_map/brick_sums/ppermute | solution.py:474
  131.2 6.5 %collective-permute-done.19 = bf16[4,272,128]{2,1,0:T(8,128)(2,1)S(1)} collective-permute-done((bf16[4,272,128]{2,1,0:T(8,128)(2,1)S(1)}, bf16[4,272,128]{2,1,0:T(8,128)(2,1)S(1)}, u32[]{:S(2)}, u32[]{:S(2)}) %collective-permute-start.19) | collective-permute-done | bytes 278560 | tf_op jit(solution)/shard_map/brick_sums/ppermute | solution.py:474
  140.4 1.9 %collective-permute-start.23 = (bf16[272,128]{1,0:T(8,128)(2,1)S(1)}, bf16[272,128]{1,0:T(8,128)(2,1)S(1)}, u32[]{:S(2)}, u32[]{:S(2)}) collective-permute-start(bf16[272,128]{1,0:T(8,128)(2,1)S(1)} %get-tuple-element.128), channel_id=1, source_target_pairs={{0,6},{1,7},{2,4},{3,5},{4,2},{5,3},{6,0},{7,1},{8,14},{9,15},{10,... | collective-permute-start | bytes 208904 | tf_op jit(solution)/shard_map/brick_sums/ppermute | solution.py:474
  142.7 3.0 %collective-permute-done.22 = bf16[272,128]{1,0:T(8,128)(2,1)S(1)} collective-permute-done((bf16[272,128]{1,0:T(8,128)(2,1)S(1)}, bf16[272,128]{1,0:T(8,128)(2,1)S(1)}, u32[]{:S(2)}, u32[]{:S(2)}) %collective-permute-start.22) | collective-permute-done | bytes 69664 | tf_op jit(solution)/shard_map/brick_sums/ppermute | solution.py:474
  (61 shorter events, 24.3 us)
Async XLA Ops:
  0.6 5.1 %collective-permute-start = (bf16[256,2048]{1,0:T(8,128)(2,1)}, bf16[256,2048]{1,0:T(8,128)(2,1)S(1)}, u32[]{:S(2)}, u32[]{:S(2)}) collective-permute-start(bf16[256,2048]{1,0:T(8,128)(2,1)} %refs_0_.1), channel_id=1, source_target_pairs={{0,1},{1,0},{2,3},{3,2},{4,5},{5,4},{6,7},{7,6},{8,9},{9,8},{10,11... | collective-permute-start | bytes 3145736 | tf_op jit(solution)/shard_map/score/ppermute | solution.py:419
  1.2 24.1 %collective-permute-start.1 = (bf16[256,2048]{1,0:T(8,128)(2,1)}, bf16[256,2048]{1,0:T(8,128)(2,1)S(1)}, u32[]{:S(2)}, u32[]{:S(2)}) collective-permute-start(bf16[256,2048]{1,0:T(8,128)(2,1)} %refs_0_.1), channel_id=1, source_target_pairs={{0,2},{2,4},{4,6},{3,1},{5,3},{7,5},{8,10},{10,12},{12,14},{11,9},... | collective-permute-start | bytes 3145736 | tf_op jit(solution)/shard_map/score/ppermute | solution.py:436
  5.7 23.7 %collective-permute-start.3 = (bf16[256,2048]{1,0:T(8,128)(2,1)S(1)}, bf16[256,2048]{1,0:T(8,128)(2,1)S(1)}, u32[]{:S(2)}, u32[]{:S(2)}) collective-permute-start(bf16[256,2048]{1,0:T(8,128)(2,1)S(1)} %collective-permute-done.refs_1_), channel_id=1, source_target_pairs={{0,2},{2,4},{4,6},{3,1},{5,3},{7,5},{8,10},{10,12},{12,14},{11,9},... | collective-permute-start | bytes 3145736 | tf_op jit(solution)/shard_map/score/ppermute | solution.py:436
  25.2 15.7 %collective-permute-start.2 = (bf16[256,2048]{1,0:T(8,128)(2,1)S(1)}, bf16[256,2048]{1,0:T(8,128)(2,1)S(1)}, u32[]{:S(2)}, u32[]{:S(2)}) collective-permute-start(bf16[256,2048]{1,0:T(8,128)(2,1)S(1)} %collective-permute-done.1.refs_0_), channel_id=1, source_target_pairs={{0,2},{2,4},{4,6},{3,1},{5,3},{7,5},{8,10},{10,12},{12,14},{11,9},... | collective-permute-start | bytes 3145736 | tf_op jit(solution)/shard_map/score/ppermute | solution.py:436
  28.7 16.8 %collective-permute-start.6 = (bf16[256,2048]{1,0:T(8,128)(2,1)S(1)}, bf16[256,2048]{1,0:T(8,128)(2,1)S(1)}, u32[]{:S(2)}, u32[]{:S(2)}) collective-permute-start(bf16[256,2048]{1,0:T(8,128)(2,1)S(1)} %collective-permute-done.1.refs_0_), channel_id=1, source_target_pairs={{0,1},{1,0},{2,3},{3,2},{4,5},{5,4},{6,7},{7,6},{8,9},{9,8},{10,11... | collective-permute-start | bytes 3145736 | tf_op jit(solution)/shard_map/score/ppermute | solution.py:428
  29.4 22.8 %collective-permute-start.5 = (bf16[256,2048]{1,0:T(8,128)(2,1)S(1)}, bf16[256,2048]{1,0:T(8,128)(2,1)S(1)}, u32[]{:S(2)}, u32[]{:S(2)}) collective-permute-start(bf16[256,2048]{1,0:T(8,128)(2,1)S(1)} %collective-permute-done.3.refs_0_), channel_id=1, source_target_pairs={{0,2},{2,4},{4,6},{3,1},{5,3},{7,5},{8,10},{10,12},{12,14},{11,9},... | collective-permute-start | bytes 3145736 | tf_op jit(solution)/shard_map/score/ppermute | solution.py:436
  33.9 22.8 %collective-permute-start.7 = (bf16[256,2048]{1,0:T(8,128)(2,1)S(1)}, bf16[256,2048]{1,0:T(8,128)(2,1)S(1)}, u32[]{:S(2)}, u32[]{:S(2)}) collective-permute-start(bf16[256,2048]{1,0:T(8,128)(2,1)S(1)} %collective-permute-done.3.refs_0_), channel_id=1, source_target_pairs={{0,1},{1,0},{2,3},{3,2},{4,5},{5,4},{6,7},{7,6},{8,9},{9,8},{10,11... | collective-permute-start | bytes 3145736 | tf_op jit(solution)/shard_map/score/ppermute | solution.py:428
  41.0 22.5 %collective-permute-start.4 = (bf16[256,2048]{1,0:T(8,128)(2,1)S(1)}, bf16[256,2048]{1,0:T(8,128)(2,1)S(1)}, u32[]{:S(2)}, u32[]{:S(2)}) collective-permute-start(bf16[256,2048]{1,0:T(8,128)(2,1)S(1)} %collective-permute-done.2.refs_0_), channel_id=1, source_target_pairs={{0,2},{2,4},{4,6},{3,1},{5,3},{7,5},{8,10},{10,12},{12,14},{11,9},... | collective-permute-start | bytes 3145736 | tf_op jit(solution)/shard_map/score/ppermute | solution.py:436
  45.4 18.0 %collective-permute-start.11 = (bf16[256,2048]{1,0:T(8,128)(2,1)S(1)}, bf16[256,2048]{1,0:T(8,128)(2,1)S(1)}, u32[]{:S(2)}, u32[]{:S(2)}) collective-permute-start(bf16[256,2048]{1,0:T(8,128)(2,1)S(1)} %collective-permute-done.2.refs_0_), channel_id=1, source_target_pairs={{0,1},{1,0},{2,3},{3,2},{4,5},{5,4},{6,7},{7,6},{8,9},{9,8},{10,11... | collective-permute-start | bytes 3145736 | tf_op jit(solution)/shard_map/score/ppermute | solution.py:428
  52.2 13.0 %collective-permute-start.10 = (bf16[256,2048]{1,0:T(8,128)(2,1)S(1)}, bf16[256,2048]{1,0:T(8,128)(2,1)S(1)}, u32[]{:S(2)}, u32[]{:S(2)}) collective-permute-start(bf16[256,2048]{1,0:T(8,128)(2,1)S(1)} %collective-permute-done.5.refs_0_), channel_id=1, source_target_pairs={{0,1},{1,0},{2,3},{3,2},{4,5},{5,4},{6,7},{7,6},{8,9},{9,8},{10,11... | collective-permute-start | bytes 3145736 | tf_op jit(solution)/shard_map/score/ppermute | solution.py:428
  52.2 22.5 %collective-permute-start.9 = (bf16[256,2048]{1,0:T(8,128)(2,1)S(1)}, bf16[256,2048]{1,0:T(8,128)(2,1)S(1)}, u32[]{:S(2)}, u32[]{:S(2)}) collective-permute-start(bf16[256,2048]{1,0:T(8,128)(2,1)S(1)} %collective-permute-done.5.refs_0_), channel_id=1, source_target_pairs={{0,2},{2,4},{4,6},{3,1},{5,3},{7,5},{8,10},{10,12},{12,14},{11,9},... | collective-permute-start | bytes 3145736 | tf_op jit(solution)/shard_map/score/ppermute | solution.py:436
  63.4 11.2 %collective-permute-start.8 = (bf16[256,2048]{1,0:T(8,128)(2,1)S(1)}, bf16[256,2048]{1,0:T(8,128)(2,1)S(1)}, u32[]{:S(2)}, u32[]{:S(2)}) collective-permute-start(bf16[256,2048]{1,0:T(8,128)(2,1)S(1)} %collective-permute-done.4.refs_0_), channel_id=1, source_target_pairs={{0,1},{1,0},{2,3},{3,2},{4,5},{5,4},{6,7},{7,6},{8,9},{9,8},{10,11... | collective-permute-start | bytes 3145736 | tf_op jit(solution)/shard_map/score/ppermute | solution.py:428
  74.7 2.7 %collective-permute-start.12 = (bf16[256,2048]{1,0:T(8,128)(2,1)S(1)}, bf16[256,2048]{1,0:T(8,128)(2,1)S(1)}, u32[]{:S(2)}, u32[]{:S(2)}) collective-permute-start(bf16[256,2048]{1,0:T(8,128)(2,1)S(1)} %collective-permute-done.9.refs_2_), channel_id=1, source_target_pairs={{0,1},{1,0},{2,3},{3,2},{4,5},{5,4},{6,7},{7,6},{8,9},{9,8},{10,11... | collective-permute-start | bytes 3145736 | tf_op jit(solution)/shard_map/score/ppermute | solution.py:428
  80.7 1.3 collective-permute-start.13
  82.1 4.8 %collective-permute-start.14 = (f32[8,8,256]{2,1,0:T(8,128)S(1)}, f32[8,8,256]{2,1,0:T(8,128)S(1)}, u32[]{:S(2)}, u32[]{:S(2)}) collective-permute-start(f32[8,8,256]{2,1,0:T(8,128)S(1)} %merge_totals.2.refs_0_), channel_id=1, source_target_pairs={{0,2},{1,3},{2,0},{3,1},{4,6},{5,7},{6,4},{7,5},{8,10},{9,11},{10,... | collective-permute-start | bytes 196616 | tf_op jit(solution)/shard_map/softmax_total/ppermute | solution.py:456
  82.2 8.8 %collective-permute-start.15 = (f32[8,8,256]{2,1,0:T(8,128)S(1)}, f32[8,8,256]{2,1,0:T(8,128)S(1)}, u32[]{:S(2)}, u32[]{:S(2)}) collective-permute-start(f32[8,8,256]{2,1,0:T(8,128)S(1)} %merge_totals.2.refs_0_), channel_id=1, source_target_pairs={{0,4},{1,5},{2,6},{3,7},{4,0},{5,1},{6,2},{7,3},{8,12},{9,13},{10,... | collective-permute-start | bytes 196616 | tf_op jit(solution)/shard_map/softmax_total/ppermute | solution.py:456
  86.9 6.2 %collective-permute-start.16 = (f32[8,8,256]{2,1,0:T(8,128)S(1)}, f32[8,8,256]{2,1,0:T(8,128)S(1)}, u32[]{:S(2)}, u32[]{:S(2)}) collective-permute-start(f32[8,8,256]{2,1,0:T(8,128)S(1)} %merge_totals.2.refs_0_), channel_id=1, source_target_pairs={{0,6},{1,7},{2,4},{3,5},{4,2},{5,3},{6,0},{7,1},{8,14},{9,15},{10,... | collective-permute-start | bytes 196616 | tf_op jit(solution)/shard_map/softmax_total/ppermute | solution.py:456
  118.4 2.8 %collective-permute-start.17 = (bf16[16,272,128]{2,1,0:T(8,128)(2,1)S(1)}, bf16[16,272,128]{2,1,0:T(8,128)(2,1)S(1)}, u32[]{:S(2)}, u32[]{:S(2)}) collective-permute-start(bf16[16,272,128]{2,1,0:T(8,128)(2,1)S(1)} %get-tuple-element.119), channel_id=1, source_target_pairs={{0,1},{1,0},{2,3},{3,2},{4,5},{5,4},{6,7},{7,6},{8,9},{9,8},{10,11... | collective-permute-start | bytes 3342344 | tf_op jit(solution)/shard_map/brick_sums/ppermute | solution.py:477
  121.6 9.6 %collective-permute-start.18 = (bf16[4,272,128]{2,1,0:T(8,128)(2,1)S(1)}, bf16[4,272,128]{2,1,0:T(8,128)(2,1)S(1)}, u32[]{:S(2)}, u32[]{:S(2)}) collective-permute-start(bf16[4,272,128]{2,1,0:T(8,128)(2,1)S(1)} %get-tuple-element.124), channel_id=1, source_target_pairs={{0,8},{8,0},{16,24},{24,16},{1,9},{9,1},{17,25},{25,17},{2,10},{10... | collective-permute-start | bytes 835592 | tf_op jit(solution)/shard_map/brick_sums/ppermute | solution.py:474
  123.2 14.5 %collective-permute-start.19 = (bf16[4,272,128]{2,1,0:T(8,128)(2,1)S(1)}, bf16[4,272,128]{2,1,0:T(8,128)(2,1)S(1)}, u32[]{:S(2)}, u32[]{:S(2)}) collective-permute-start(bf16[4,272,128]{2,1,0:T(8,128)(2,1)S(1)} %get-tuple-element.126), channel_id=1, source_target_pairs={{0,16},{8,24},{16,0},{24,8},{1,17},{9,25},{17,1},{25,9},{2,18},{10... | collective-permute-start | bytes 835592 | tf_op jit(solution)/shard_map/brick_sums/ppermute | solution.py:474
  124.7 13.0 %collective-permute-start.20 = (bf16[4,272,128]{2,1,0:T(8,128)(2,1)S(1)}, bf16[4,272,128]{2,1,0:T(8,128)(2,1)S(1)}, u32[]{:S(2)}, u32[]{:S(2)}) collective-permute-start(bf16[4,272,128]{2,1,0:T(8,128)(2,1)S(1)} %get-tuple-element.125), channel_id=1, source_target_pairs={{0,24},{8,16},{16,8},{24,0},{1,25},{9,17},{17,9},{25,1},{2,26},{10... | collective-permute-start | bytes 835592 | tf_op jit(solution)/shard_map/brick_sums/ppermute | solution.py:474
  137.9 4.8 %collective-permute-start.21 = (bf16[272,128]{1,0:T(8,128)(2,1)S(1)}, bf16[272,128]{1,0:T(8,128)(2,1)S(1)}, u32[]{:S(2)}, u32[]{:S(2)}) collective-permute-start(bf16[272,128]{1,0:T(8,128)(2,1)S(1)} %get-tuple-element.127), channel_id=1, source_target_pairs={{0,2},{1,3},{2,0},{3,1},{4,6},{5,7},{6,4},{7,5},{8,10},{9,11},{10,... | collective-permute-start | bytes 208904 | tf_op jit(solution)/shard_map/brick_sums/ppermute | solution.py:474
  138.7 6.9 %collective-permute-start.22 = (bf16[272,128]{1,0:T(8,128)(2,1)S(1)}, bf16[272,128]{1,0:T(8,128)(2,1)S(1)}, u32[]{:S(2)}, u32[]{:S(2)}) collective-permute-start(bf16[272,128]{1,0:T(8,128)(2,1)S(1)} %get-tuple-element.129), channel_id=1, source_target_pairs={{0,4},{1,5},{2,6},{3,7},{4,0},{5,1},{6,2},{7,3},{8,12},{9,13},{10,... | collective-permute-start | bytes 208904 | tf_op jit(solution)/shard_map/brick_sums/ppermute | solution.py:474
  140.4 6.2 %collective-permute-start.23 = (bf16[272,128]{1,0:T(8,128)(2,1)S(1)}, bf16[272,128]{1,0:T(8,128)(2,1)S(1)}, u32[]{:S(2)}, u32[]{:S(2)}) collective-permute-start(bf16[272,128]{1,0:T(8,128)(2,1)S(1)} %get-tuple-element.128), channel_id=1, source_target_pairs={{0,6},{1,7},{2,4},{3,5},{4,2},{5,3},{6,0},{7,1},{8,14},{9,15},{10,... | collective-permute-start | bytes 208904 | tf_op jit(solution)/shard_map/brick_sums/ppermute | solution.py:474
  (4 other events, 174.2 us)

commit v7 on v6

--- a/solution.py
+++ b/solution.py
@@ -124,7 +124,7 @@
                 value = jnp.exp(p_ref[slot, rows, :] - largest)
                 p_ref[slot, rows, :] = value
                 total += jnp.sum(value, axis=0, keepdims=True)
-            pick = lax.broadcasted_iota(jnp.int32, (8, block), 0) == 0
+            pick = lax.broadcasted_iota(jnp.int32, (2, block), 0) == 0
             stat_ref[slot] = jnp.where(pick, largest, total)
 
     for i in range(n):
@@ -143,7 +143,7 @@
     shapes = [
         jax.ShapeDtypeStruct((blocks, orients, block), jnp.float32),
         jax.ShapeDtypeStruct((blocks * block, width), jnp.bfloat16),
-        jax.ShapeDtypeStruct((blocks, 8, block), jnp.float32),
+        jax.ShapeDtypeStruct((blocks, 2, block), jnp.float32),
     ]
     in_specs = [VMEM] * (n + 1)
     args = list(images) + [projections]
@@ -304,7 +304,7 @@
 
 def grid_bricks(parity, slots_of, volume, map_ref, out_ref):
     bricks = map_ref.shape[0]
-    unroll = 8
+    unroll = min(16, bricks // 2)
     sub = lax.broadcasted_iota(jnp.int32, (EXTRA_ROWS, 128), 0)
 
     def grid_brick(i):

time: 149 us -> 147 us (0.987)
  waiting for transfers between devices: 52.7 us -> 51.2 us
  transfers between devices with their start and end apart: 24 -> 24, of which waited for: 15 -> 13; matrix products, arithmetic and copies ran while one was open for 3% -> 3% of each run, Pallas kernels for 12% -> 12%
where the time goes in v7:
time: 147 us; the launch traced here: 146 us
  waiting for transfers between devices  51.2 us (35%)
  Pallas kernels  46.2 us (31%)
  starting transfers between devices  38.7 us (26%)
  local copies, waits for them, and re-layouts  6.39 us (4%)
  other arithmetic  2.04 us (1%)
    ppermute x6, waiting for transfers between devices, body(): moving = [lax.ppermute(part, 'ori', along) for part in moving]  25.7 us
    pallas_call x1, Pallas kernels, sum_step(): pl.pallas_call(functools.partial(sum_kernel, bricks, capacity), out_shape...  25.1 us
    ppermute x6, starting transfers between devices, body(): moving = [lax.ppermute(part, 'ori', along) for part in moving]  24.9 us
    ppermute x6, waiting for transfers between devices, add_up(): total += lax.ppermute(part, axis, perm).astype(jnp.float32)  15.9 us
    pallas_call x6, Pallas kernels, score_step(): pl.pallas_call(functools.partial(score_kernel, chips, candidates, first),...  13.9 us
    ppermute x6, starting transfers between devices, add_up(): total += lax.ppermute(part, axis, perm).astype(jnp.float32)  8 us
    ppermute x3, waiting for transfers between devices, body(): lax.ppermute(totals, 'ori', [(i, i ^ 2 * k) for i in range(orient_groups)])  5.53 us
    ppermute x3, starting transfers between devices, body(): lax.ppermute(totals, 'ori', [(i, i ^ 2 * k) for i in range(orient_groups)])  4.8 us
  transfers between devices with their start and end apart: 24, of which 13 were waited for; matrix products, arithmetic and copies ran while one was open for 3% of the time, Pallas kernels for 12%

profile of v7, /device:TPU:0, one launch (start us, length us, event | category | flops | bytes accessed | tf_op | source)
XLA Modules:
  0.0 146.3 jit_solution(12694234445092985922)
XLA Ops:
  1.2 4.6 %collective-permute-start.1 = (bf16[256,2048]{1,0:T(8,128)(2,1)}, bf16[256,2048]{1,0:T(8,128)(2,1)S(1)}, u32[]{:S(2)}, u32[]{:S(2)}) collective-permute-start(bf16[256,2048]{1,0:T(8,128)(2,1)} %refs_0_.1), channel_id=1, source_target_pairs={{0,2},{2,4},{4,6},{3,1},{5,3},{7,5},{8,10},{10,12},{12,14},{11,9},... | collective-permute-start | bytes 3145736 | tf_op jit(solution)/shard_map/score/ppermute | solution.py:436
  5.7 3.5 %collective-permute-start.3 = (bf16[256,2048]{1,0:T(8,128)(2,1)S(1)}, bf16[256,2048]{1,0:T(8,128)(2,1)S(1)}, u32[]{:S(2)}, u32[]{:S(2)}) collective-permute-start(bf16[256,2048]{1,0:T(8,128)(2,1)S(1)} %collective-permute-done.refs_1_), channel_id=1, source_target_pairs={{0,2},{2,4},{4,6},{3,1},{5,3},{7,5},{8,10},{10,12},{12,14},{11,9},... | collective-permute-start | bytes 3145736 | tf_op jit(solution)/shard_map/score/ppermute | solution.py:436
  11.2 4.7 %place_segments.1 = (s32[64,1,256]{2,1,0:T(1,128)S(1)}, s32[4,32,256]{2,1,0:T(8,128)S(1)}) custom-call(s32[64,1,256]{2,1,0:T(1,128)S(1)} %reshape.41.dest_ref, s32[64,1,256]{2,1,0:T(1,128)S(1)} %reshape.43.rows_ref), custom_call_target="tpu_custom_call" | custom-call | flops 1000 | bytes 1000 | tf_op jit(solution)/shard_map/place_segments/place_segments/pallas_call | solution.py:399
  17.9 2.2 %copy-done.1 = bf16[1024,2048]{1,0:T(8,128)(2,1)S(1)} copy-done((bf16[1024,2048]{1,0:T(8,128)(2,1)S(1)}, bf16[1024,2048]{1,0:T(8,128)(2,1)}, u32[]{:S(2)}) %copy-start.1) | copy-done | bytes 4194328
  21.3 3.9 %score_blocks.6 = (f32[1024,128]{1,0:T(8,128)S(1)}, f32[8,1024,256]{2,1,0:T(8,128)S(1)}, bf16[2048,2048]{1,0:T(8,128)(2,1)S(1)}, f32[8,2,256]{2,1,0:T(2,128)S(1)}) custom-call(bf16[256,2048]{1,0:T(8,128)(2,1)S(1)} %copy-done.3, bf16[256,2048]{1,0:T(8,128)(2,1)S(1)} %collective-permute-done.refs_1_, bf16[1024,2048]{1,0:T(8,128)(2,1)S(1)} %copy-done.1), custom_call_target="tpu_custom_call" | custom-call | flops 1000 | bytes 1000 | tf_op jit(solution)/shard_map/score/score_blocks/pallas_call | solution.py:158
  25.2 3.5 %collective-permute-start.2 = (bf16[256,2048]{1,0:T(8,128)(2,1)S(1)}, bf16[256,2048]{1,0:T(8,128)(2,1)S(1)}, u32[]{:S(2)}, u32[]{:S(2)}) collective-permute-start(bf16[256,2048]{1,0:T(8,128)(2,1)S(1)} %collective-permute-done.1.refs_0_), channel_id=1, source_target_pairs={{0,2},{2,4},{4,6},{3,1},{5,3},{7,5},{8,10},{10,12},{12,14},{11,9},... | collective-permute-start | bytes 3145736 | tf_op jit(solution)/shard_map/score/ppermute | solution.py:436
  29.4 4.4 %collective-permute-start.5 = (bf16[256,2048]{1,0:T(8,128)(2,1)S(1)}, bf16[256,2048]{1,0:T(8,128)(2,1)S(1)}, u32[]{:S(2)}, u32[]{:S(2)}) collective-permute-start(bf16[256,2048]{1,0:T(8,128)(2,1)S(1)} %collective-permute-done.3.refs_0_), channel_id=1, source_target_pairs={{0,2},{2,4},{4,6},{3,1},{5,3},{7,5},{8,10},{10,12},{12,14},{11,9},... | collective-permute-start | bytes 3145736 | tf_op jit(solution)/shard_map/score/ppermute | solution.py:436
  33.9 7.0 %collective-permute-done.2.refs_0_ = bf16[256,2048]{1,0:T(8,128)(2,1)S(1)} collective-permute-done((bf16[256,2048]{1,0:T(8,128)(2,1)S(1)}, bf16[256,2048]{1,0:T(8,128)(2,1)S(1)}, u32[]{:S(2)}, u32[]{:S(2)}) %collective-permute-start.2) | collective-permute-done | bytes 1048608 | tf_op jit(solution)/shard_map/score/ppermute | solution.py:436
  41.0 4.4 %collective-permute-start.4 = (bf16[256,2048]{1,0:T(8,128)(2,1)S(1)}, bf16[256,2048]{1,0:T(8,128)(2,1)S(1)}, u32[]{:S(2)}, u32[]{:S(2)}) collective-permute-start(bf16[256,2048]{1,0:T(8,128)(2,1)S(1)} %collective-permute-done.2.refs_0_), channel_id=1, source_target_pairs={{0,2},{2,4},{4,6},{3,1},{5,3},{7,5},{8,10},{10,12},{12,14},{11,9},... | collective-permute-start | bytes 3145736 | tf_op jit(solution)/shard_map/score/ppermute | solution.py:436
  47.1 5.1 %collective-permute-done.5.refs_0_ = bf16[256,2048]{1,0:T(8,128)(2,1)S(1)} collective-permute-done((bf16[256,2048]{1,0:T(8,128)(2,1)S(1)}, bf16[256,2048]{1,0:T(8,128)(2,1)S(1)}, u32[]{:S(2)}, u32[]{:S(2)}) %collective-permute-start.5) | collective-permute-done | bytes 1048608 | tf_op jit(solution)/shard_map/score/ppermute | solution.py:436
  52.2 4.4 %collective-permute-start.9 = (bf16[256,2048]{1,0:T(8,128)(2,1)S(1)}, bf16[256,2048]{1,0:T(8,128)(2,1)S(1)}, u32[]{:S(2)}, u32[]{:S(2)}) collective-permute-start(bf16[256,2048]{1,0:T(8,128)(2,1)S(1)} %collective-permute-done.5.refs_0_), channel_id=1, source_target_pairs={{0,2},{2,4},{4,6},{3,1},{5,3},{7,5},{8,10},{10,12},{12,14},{11,9},... | collective-permute-start | bytes 3145736 | tf_op jit(solution)/shard_map/score/ppermute | solution.py:436
  58.3 5.2 %collective-permute-done.4.refs_0_ = bf16[256,2048]{1,0:T(8,128)(2,1)S(1)} collective-permute-done((bf16[256,2048]{1,0:T(8,128)(2,1)S(1)}, bf16[256,2048]{1,0:T(8,128)(2,1)S(1)}, u32[]{:S(2)}, u32[]{:S(2)}) %collective-permute-start.4) | collective-permute-done | bytes 1048608 | tf_op jit(solution)/shard_map/score/ppermute | solution.py:436
  63.5 1.8 %score_blocks.9 = (f32[8,1024,256]{2,1,0:T(8,128)S(1)}, bf16[2048,2048]{1,0:T(8,128)(2,1)S(1)}, f32[8,2,256]{2,1,0:T(2,128)S(1)}) custom-call(bf16[256,2048]{1,0:T(8,128)(2,1)S(1)} %collective-permute-done.2.refs_0_, bf16[256,2048]{1,0:T(8,128)(2,1)S(1)} %collective-permute-done.11.refs_1_, ...), custom_call_target="tpu_custom_call", output_to_operand_aliasing={{0}: (4, {}), {1}: (5, {}), {2}: (6, {})} | custom-call | flops 1000 | bytes 1000 | tf_op jit(solution)/shard_map/score/score_blocks/pallas_call | solution.py:158
  66.9 7.8 %collective-permute-done.9.refs_2_ = bf16[256,2048]{1,0:T(8,128)(2,1)S(1)} collective-permute-done((bf16[256,2048]{1,0:T(8,128)(2,1)S(1)}, bf16[256,2048]{1,0:T(8,128)(2,1)S(1)}, u32[]{:S(2)}, u32[]{:S(2)}) %collective-permute-start.9) | collective-permute-done | bytes 1048608 | tf_op jit(solution)/shard_map/score/ppermute | solution.py:436
  74.7 2.7 %collective-permute-done.12.refs_3_ = bf16[256,2048]{1,0:T(8,128)(2,1)S(1)} collective-permute-done((bf16[256,2048]{1,0:T(8,128)(2,1)S(1)}, bf16[256,2048]{1,0:T(8,128)(2,1)S(1)}, u32[]{:S(2)}, u32[]{:S(2)}) %collective-permute-start.12) | collective-permute-done | bytes 1048608 | tf_op jit(solution)/shard_map/score/ppermute | solution.py:428
  77.3 3.4 %score_blocks.11 = (f32[8,1024,256]{2,1,0:T(8,128)S(1)}, bf16[2048,2048]{1,0:T(8,128)(2,1)S(1)}, f32[8,2,256]{2,1,0:T(2,128)S(1)}) custom-call(bf16[256,2048]{1,0:T(8,128)(2,1)S(1)} %collective-permute-done.4.refs_0_, bf16[256,2048]{1,0:T(8,128)(2,1)S(1)} %collective-permute-done.8.refs_1_, ...), custom_call_target="tpu_custom_call", output_to_operand_aliasing={{0}: (6, {}), {1}: (7, {}), {2}: (8, {})} | custom-call | flops 1000 | bytes 1000 | tf_op jit(solution)/shard_map/score/score_blocks/pallas_call | solution.py:158
  82.1 4.7 %collective-permute-start.15 = (f32[8,2,256]{2,1,0:T(2,128)S(1)}, f32[8,2,256]{2,1,0:T(2,128)S(1)}, u32[]{:S(2)}, u32[]{:S(2)}) collective-permute-start(f32[8,2,256]{2,1,0:T(2,128)S(1)} %merge_totals.2.refs_0_), channel_id=1, source_target_pairs={{0,4},{1,5},{2,6},{3,7},{4,0},{5,1},{6,2},{7,3},{8,12},{9,13},{10,... | collective-permute-start | bytes 49160 | tf_op jit(solution)/shard_map/softmax_total/ppermute | solution.py:456
  88.5 3.8 %collective-permute-done.16.refs_3_ = f32[8,2,256]{2,1,0:T(2,128)S(1)} collective-permute-done((f32[8,2,256]{2,1,0:T(2,128)S(1)}, f32[8,2,256]{2,1,0:T(2,128)S(1)}, u32[]{:S(2)}, u32[]{:S(2)}) %collective-permute-start.16) | collective-permute-done | bytes 16416 | tf_op jit(solution)/shard_map/softmax_total/ppermute | solution.py:456
  92.4 25.1 %sum_and_grid.1 = (bf16[16,272,128]{2,1,0:T(8,128)(2,1)S(1)}, bf16[16,1024,128]{2,1,0:T(8,128)(2,1)S(1)}, f32[64,256]{1,0:T(8,128)S(1)}) custom-call(s32[17408]{0:T(1024)S(1)} %concatenate.3.slot_ref, f32[8,1024,256]{2,1,0:T(8,128)S(1)} %get-tuple-element.111.p_ref, f32[8,2,256]{2,1,0:T(2,128)S(1)} %get-tuple-element.112.refs_0_.stats_ref, ...), custom_call_target="tpu_custom_call" | custom-call | flops 8589934592 | bytes 25165824 | tf_op jit(solution)/shard_map/sum_and_grid/sum_and_grid/pallas_call | solution.py:354
  117.6 2.3 %grid_own_bricks.1 = f32[16,272,128]{2,1,0:T(8,128)S(1)} custom-call(bf16[16,1024,128]{2,1,0:T(8,128)(2,1)S(1)} %get-tuple-element.117.slots, f32[64,256]{1,0:T(8,128)S(1)} %get-tuple-element.118.volume, s32[32,1,1024]{2,1,0:T(1,128)S(1)} %reshape.46.map_ref), custom_call_target="tpu_custom_call" | custom-call | flops 1000 | bytes 1000 | tf_op jit(solution)/shard_map/brick_sums/grid_own_bricks/pallas_call | solution.py:337
  124.3 6.0 %collective-permute-done.18 = bf16[4,272,128]{2,1,0:T(8,128)(2,1)S(1)} collective-permute-done((bf16[4,272,128]{2,1,0:T(8,128)(2,1)S(1)}, bf16[4,272,128]{2,1,0:T(8,128)(2,1)S(1)}, u32[]{:S(2)}, u32[]{:S(2)}) %collective-permute-start.18) | collective-permute-done | bytes 278560 | tf_op jit(solution)/shard_map/brick_sums/ppermute | solution.py:474
  130.3 6.4 %collective-permute-done.19 = bf16[4,272,128]{2,1,0:T(8,128)(2,1)S(1)} collective-permute-done((bf16[4,272,128]{2,1,0:T(8,128)(2,1)S(1)}, bf16[4,272,128]{2,1,0:T(8,128)(2,1)S(1)}, u32[]{:S(2)}, u32[]{:S(2)}) %collective-permute-start.19) | collective-permute-done | bytes 278560 | tf_op jit(solution)/shard_map/brick_sums/ppermute | solution.py:474
  137.7 3.7 %collective-permute-start.23 = (bf16[272,128]{1,0:T(8,128)(2,1)S(1)}, bf16[272,128]{1,0:T(8,128)(2,1)S(1)}, u32[]{:S(2)}, u32[]{:S(2)}) collective-permute-start(bf16[272,128]{1,0:T(8,128)(2,1)S(1)} %get-tuple-element.128), channel_id=1, source_target_pairs={{0,6},{1,7},{2,4},{3,5},{4,2},{5,3},{6,0},{7,1},{8,14},{9,15},{10,... | collective-permute-start | bytes 208904 | tf_op jit(solution)/shard_map/brick_sums/ppermute | solution.py:474
  141.3 3.5 %collective-permute-done.22 = bf16[272,128]{1,0:T(8,128)(2,1)S(1)} collective-permute-done((bf16[272,128]{1,0:T(8,128)(2,1)S(1)}, bf16[272,128]{1,0:T(8,128)(2,1)S(1)}, u32[]{:S(2)}, u32[]{:S(2)}) %collective-permute-start.22) | collective-permute-done | bytes 69664 | tf_op jit(solution)/shard_map/brick_sums/ppermute | solution.py:474
  (61 shorter events, 21.2 us)
Async XLA Ops:
  0.6 5.1 %collective-permute-start = (bf16[256,2048]{1,0:T(8,128)(2,1)}, bf16[256,2048]{1,0:T(8,128)(2,1)S(1)}, u32[]{:S(2)}, u32[]{:S(2)}) collective-permute-start(bf16[256,2048]{1,0:T(8,128)(2,1)} %refs_0_.1), channel_id=1, source_target_pairs={{0,1},{1,0},{2,3},{3,2},{4,5},{5,4},{6,7},{7,6},{8,9},{9,8},{10,11... | collective-permute-start | bytes 3145736 | tf_op jit(solution)/shard_map/score/ppermute | solution.py:419
  1.2 24.1 %collective-permute-start.1 = (bf16[256,2048]{1,0:T(8,128)(2,1)}, bf16[256,2048]{1,0:T(8,128)(2,1)S(1)}, u32[]{:S(2)}, u32[]{:S(2)}) collective-permute-start(bf16[256,2048]{1,0:T(8,128)(2,1)} %refs_0_.1), channel_id=1, source_target_pairs={{0,2},{2,4},{4,6},{3,1},{5,3},{7,5},{8,10},{10,12},{12,14},{11,9},... | collective-permute-start | bytes 3145736 | tf_op jit(solution)/shard_map/score/ppermute | solution.py:436
  5.7 23.7 %collective-permute-start.3 = (bf16[256,2048]{1,0:T(8,128)(2,1)S(1)}, bf16[256,2048]{1,0:T(8,128)(2,1)S(1)}, u32[]{:S(2)}, u32[]{:S(2)}) collective-permute-start(bf16[256,2048]{1,0:T(8,128)(2,1)S(1)} %collective-permute-done.refs_1_), channel_id=1, source_target_pairs={{0,2},{2,4},{4,6},{3,1},{5,3},{7,5},{8,10},{10,12},{12,14},{11,9},... | collective-permute-start | bytes 3145736 | tf_op jit(solution)/shard_map/score/ppermute | solution.py:436
  25.2 15.7 %collective-permute-start.2 = (bf16[256,2048]{1,0:T(8,128)(2,1)S(1)}, bf16[256,2048]{1,0:T(8,128)(2,1)S(1)}, u32[]{:S(2)}, u32[]{:S(2)}) collective-permute-start(bf16[256,2048]{1,0:T(8,128)(2,1)S(1)} %collective-permute-done.1.refs_0_), channel_id=1, source_target_pairs={{0,2},{2,4},{4,6},{3,1},{5,3},{7,5},{8,10},{10,12},{12,14},{11,9},... | collective-permute-start | bytes 3145736 | tf_op jit(solution)/shard_map/score/ppermute | solution.py:436
  28.7 16.8 %collective-permute-start.6 = (bf16[256,2048]{1,0:T(8,128)(2,1)S(1)}, bf16[256,2048]{1,0:T(8,128)(2,1)S(1)}, u32[]{:S(2)}, u32[]{:S(2)}) collective-permute-start(bf16[256,2048]{1,0:T(8,128)(2,1)S(1)} %collective-permute-done.1.refs_0_), channel_id=1, source_target_pairs={{0,1},{1,0},{2,3},{3,2},{4,5},{5,4},{6,7},{7,6},{8,9},{9,8},{10,11... | collective-permute-start | bytes 3145736 | tf_op jit(solution)/shard_map/score/ppermute | solution.py:428
  29.4 22.8 %collective-permute-start.5 = (bf16[256,2048]{1,0:T(8,128)(2,1)S(1)}, bf16[256,2048]{1,0:T(8,128)(2,1)S(1)}, u32[]{:S(2)}, u32[]{:S(2)}) collective-permute-start(bf16[256,2048]{1,0:T(8,128)(2,1)S(1)} %collective-permute-done.3.refs_0_), channel_id=1, source_target_pairs={{0,2},{2,4},{4,6},{3,1},{5,3},{7,5},{8,10},{10,12},{12,14},{11,9},... | collective-permute-start | bytes 3145736 | tf_op jit(solution)/shard_map/score/ppermute | solution.py:436
  33.9 22.8 %collective-permute-start.7 = (bf16[256,2048]{1,0:T(8,128)(2,1)S(1)}, bf16[256,2048]{1,0:T(8,128)(2,1)S(1)}, u32[]{:S(2)}, u32[]{:S(2)}) collective-permute-start(bf16[256,2048]{1,0:T(8,128)(2,1)S(1)} %collective-permute-done.3.refs_0_), channel_id=1, source_target_pairs={{0,1},{1,0},{2,3},{3,2},{4,5},{5,4},{6,7},{7,6},{8,9},{9,8},{10,11... | collective-permute-start | bytes 3145736 | tf_op jit(solution)/shard_map/score/ppermute | solution.py:428
  41.0 22.5 %collective-permute-start.4 = (bf16[256,2048]{1,0:T(8,128)(2,1)S(1)}, bf16[256,2048]{1,0:T(8,128)(2,1)S(1)}, u32[]{:S(2)}, u32[]{:S(2)}) collective-permute-start(bf16[256,2048]{1,0:T(8,128)(2,1)S(1)} %collective-permute-done.2.refs_0_), channel_id=1, source_target_pairs={{0,2},{2,4},{4,6},{3,1},{5,3},{7,5},{8,10},{10,12},{12,14},{11,9},... | collective-permute-start | bytes 3145736 | tf_op jit(solution)/shard_map/score/ppermute | solution.py:436
  45.4 18.0 %collective-permute-start.11 = (bf16[256,2048]{1,0:T(8,128)(2,1)S(1)}, bf16[256,2048]{1,0:T(8,128)(2,1)S(1)}, u32[]{:S(2)}, u32[]{:S(2)}) collective-permute-start(bf16[256,2048]{1,0:T(8,128)(2,1)S(1)} %collective-permute-done.2.refs_0_), channel_id=1, source_target_pairs={{0,1},{1,0},{2,3},{3,2},{4,5},{5,4},{6,7},{7,6},{8,9},{9,8},{10,11... | collective-permute-start | bytes 3145736 | tf_op jit(solution)/shard_map/score/ppermute | solution.py:428
  52.2 13.0 %collective-permute-start.10 = (bf16[256,2048]{1,0:T(8,128)(2,1)S(1)}, bf16[256,2048]{1,0:T(8,128)(2,1)S(1)}, u32[]{:S(2)}, u32[]{:S(2)}) collective-permute-start(bf16[256,2048]{1,0:T(8,128)(2,1)S(1)} %collective-permute-done.5.refs_0_), channel_id=1, source_target_pairs={{0,1},{1,0},{2,3},{3,2},{4,5},{5,4},{6,7},{7,6},{8,9},{9,8},{10,11... | collective-permute-start | bytes 3145736 | tf_op jit(solution)/shard_map/score/ppermute | solution.py:428
  52.2 22.5 %collective-permute-start.9 = (bf16[256,2048]{1,0:T(8,128)(2,1)S(1)}, bf16[256,2048]{1,0:T(8,128)(2,1)S(1)}, u32[]{:S(2)}, u32[]{:S(2)}) collective-permute-start(bf16[256,2048]{1,0:T(8,128)(2,1)S(1)} %collective-permute-done.5.refs_0_), channel_id=1, source_target_pairs={{0,2},{2,4},{4,6},{3,1},{5,3},{7,5},{8,10},{10,12},{12,14},{11,9},... | collective-permute-start | bytes 3145736 | tf_op jit(solution)/shard_map/score/ppermute | solution.py:436
  63.4 11.2 %collective-permute-start.8 = (bf16[256,2048]{1,0:T(8,128)(2,1)S(1)}, bf16[256,2048]{1,0:T(8,128)(2,1)S(1)}, u32[]{:S(2)}, u32[]{:S(2)}) collective-permute-start(bf16[256,2048]{1,0:T(8,128)(2,1)S(1)} %collective-permute-done.4.refs_0_), channel_id=1, source_target_pairs={{0,1},{1,0},{2,3},{3,2},{4,5},{5,4},{6,7},{7,6},{8,9},{9,8},{10,11... | collective-permute-start | bytes 3145736 | tf_op jit(solution)/shard_map/score/ppermute | solution.py:428
  74.7 2.7 %collective-permute-start.12 = (bf16[256,2048]{1,0:T(8,128)(2,1)S(1)}, bf16[256,2048]{1,0:T(8,128)(2,1)S(1)}, u32[]{:S(2)}, u32[]{:S(2)}) collective-permute-start(bf16[256,2048]{1,0:T(8,128)(2,1)S(1)} %collective-permute-done.9.refs_2_), channel_id=1, source_target_pairs={{0,1},{1,0},{2,3},{3,2},{4,5},{5,4},{6,7},{7,6},{8,9},{9,8},{10,11... | collective-permute-start | bytes 3145736 | tf_op jit(solution)/shard_map/score/ppermute | solution.py:428
  80.7 1.2 collective-permute-start.13
  82.0 4.8 %collective-permute-start.14 = (f32[8,2,256]{2,1,0:T(2,128)S(1)}, f32[8,2,256]{2,1,0:T(2,128)S(1)}, u32[]{:S(2)}, u32[]{:S(2)}) collective-permute-start(f32[8,2,256]{2,1,0:T(2,128)S(1)} %merge_totals.2.refs_0_), channel_id=1, source_target_pairs={{0,2},{1,3},{2,0},{3,1},{4,6},{5,7},{6,4},{7,5},{8,10},{9,11},{10,... | collective-permute-start | bytes 49160 | tf_op jit(solution)/shard_map/softmax_total/ppermute | solution.py:456
  82.1 6.4 %collective-permute-start.15 = (f32[8,2,256]{2,1,0:T(2,128)S(1)}, f32[8,2,256]{2,1,0:T(2,128)S(1)}, u32[]{:S(2)}, u32[]{:S(2)}) collective-permute-start(f32[8,2,256]{2,1,0:T(2,128)S(1)} %merge_totals.2.refs_0_), channel_id=1, source_target_pairs={{0,4},{1,5},{2,6},{3,7},{4,0},{5,1},{6,2},{7,3},{8,12},{9,13},{10,... | collective-permute-start | bytes 49160 | tf_op jit(solution)/shard_map/softmax_total/ppermute | solution.py:456
  86.8 5.5 %collective-permute-start.16 = (f32[8,2,256]{2,1,0:T(2,128)S(1)}, f32[8,2,256]{2,1,0:T(2,128)S(1)}, u32[]{:S(2)}, u32[]{:S(2)}) collective-permute-start(f32[8,2,256]{2,1,0:T(2,128)S(1)} %merge_totals.2.refs_0_), channel_id=1, source_target_pairs={{0,6},{1,7},{2,4},{3,5},{4,2},{5,3},{6,0},{7,1},{8,14},{9,15},{10,... | collective-permute-start | bytes 49160 | tf_op jit(solution)/shard_map/softmax_total/ppermute | solution.py:456
  117.6 2.8 %collective-permute-start.17 = (bf16[16,272,128]{2,1,0:T(8,128)(2,1)S(1)}, bf16[16,272,128]{2,1,0:T(8,128)(2,1)S(1)}, u32[]{:S(2)}, u32[]{:S(2)}) collective-permute-start(bf16[16,272,128]{2,1,0:T(8,128)(2,1)S(1)} %get-tuple-element.119), channel_id=1, source_target_pairs={{0,1},{1,0},{2,3},{3,2},{4,5},{5,4},{6,7},{7,6},{8,9},{9,8},{10,11... | collective-permute-start | bytes 3342344 | tf_op jit(solution)/shard_map/brick_sums/ppermute | solution.py:477
  120.7 9.6 %collective-permute-start.18 = (bf16[4,272,128]{2,1,0:T(8,128)(2,1)S(1)}, bf16[4,272,128]{2,1,0:T(8,128)(2,1)S(1)}, u32[]{:S(2)}, u32[]{:S(2)}) collective-permute-start(bf16[4,272,128]{2,1,0:T(8,128)(2,1)S(1)} %get-tuple-element.124), channel_id=1, source_target_pairs={{0,8},{8,0},{16,24},{24,16},{1,9},{9,1},{17,25},{25,17},{2,10},{10... | collective-permute-start | bytes 835592 | tf_op jit(solution)/shard_map/brick_sums/ppermute | solution.py:474
  122.3 14.4 %collective-permute-start.19 = (bf16[4,272,128]{2,1,0:T(8,128)(2,1)S(1)}, bf16[4,272,128]{2,1,0:T(8,128)(2,1)S(1)}, u32[]{:S(2)}, u32[]{:S(2)}) collective-permute-start(bf16[4,272,128]{2,1,0:T(8,128)(2,1)S(1)} %get-tuple-element.126), channel_id=1, source_target_pairs={{0,16},{8,24},{16,0},{24,8},{1,17},{9,25},{17,1},{25,9},{2,18},{10... | collective-permute-start | bytes 835592 | tf_op jit(solution)/shard_map/brick_sums/ppermute | solution.py:474
  123.8 12.9 %collective-permute-start.20 = (bf16[4,272,128]{2,1,0:T(8,128)(2,1)S(1)}, bf16[4,272,128]{2,1,0:T(8,128)(2,1)S(1)}, u32[]{:S(2)}, u32[]{:S(2)}) collective-permute-start(bf16[4,272,128]{2,1,0:T(8,128)(2,1)S(1)} %get-tuple-element.125), channel_id=1, source_target_pairs={{0,24},{8,16},{16,8},{24,0},{1,25},{9,17},{17,9},{25,1},{2,26},{10... | collective-permute-start | bytes 835592 | tf_op jit(solution)/shard_map/brick_sums/ppermute | solution.py:474
  136.9 4.5 %collective-permute-start.21 = (bf16[272,128]{1,0:T(8,128)(2,1)S(1)}, bf16[272,128]{1,0:T(8,128)(2,1)S(1)}, u32[]{:S(2)}, u32[]{:S(2)}) collective-permute-start(bf16[272,128]{1,0:T(8,128)(2,1)S(1)} %get-tuple-element.127), channel_id=1, source_target_pairs={{0,2},{1,3},{2,0},{3,1},{4,6},{5,7},{6,4},{7,5},{8,10},{9,11},{10,... | collective-permute-start | bytes 208904 | tf_op jit(solution)/shard_map/brick_sums/ppermute | solution.py:474
  136.9 7.9 %collective-permute-start.22 = (bf16[272,128]{1,0:T(8,128)(2,1)S(1)}, bf16[272,128]{1,0:T(8,128)(2,1)S(1)}, u32[]{:S(2)}, u32[]{:S(2)}) collective-permute-start(bf16[272,128]{1,0:T(8,128)(2,1)S(1)} %get-tuple-element.129), channel_id=1, source_target_pairs={{0,4},{1,5},{2,6},{3,7},{4,0},{5,1},{6,2},{7,3},{8,12},{9,13},{10,... | collective-permute-start | bytes 208904 | tf_op jit(solution)/shard_map/brick_sums/ppermute | solution.py:474
  137.7 7.2 %collective-permute-start.23 = (bf16[272,128]{1,0:T(8,128)(2,1)S(1)}, bf16[272,128]{1,0:T(8,128)(2,1)S(1)}, u32[]{:S(2)}, u32[]{:S(2)}) collective-permute-start(bf16[272,128]{1,0:T(8,128)(2,1)S(1)} %get-tuple-element.128), channel_id=1, source_target_pairs={{0,6},{1,7},{2,4},{3,5},{4,2},{5,3},{6,0},{7,1},{8,14},{9,15},{10,... | collective-permute-start | bytes 208904 | tf_op jit(solution)/shard_map/brick_sums/ppermute | solution.py:474
  (4 other events, 172.4 us)

commit v8 on v7

--- a/solution.py
+++ b/solution.py
@@ -9,7 +9,7 @@
 
 BRICK_ROWS = 256
 EXTRA_ROWS = 16
-TILE = 256
+TILE = 512
 JOINED = 2
 temper_scale = 4.0
 
@@ -366,7 +366,7 @@
             pltpu.VMEM((joined * owned, TILE), jnp.float32),
             pltpu.VMEM((bricks * groups * capacity + 512, 128), jnp.float32),
         ],
-        compiler_params=pltpu.CompilerParams(vmem_limit_bytes=21 << 20),
+        compiler_params=pltpu.CompilerParams(vmem_limit_bytes=23 << 20),
         cost_estimate=pl.CostEstimate(
             flops=2 * blocks * block * orients * width, bytes_accessed=24 << 20, transcendentals=0
         ),

time: 147 us -> 146 us (level)
  no operation moved by 1% of the time
where the time goes in v8:
time: 146 us
  waiting for transfers between devices  51.2 us (35%)
  Pallas kernels  45.5 us (31%)
  starting transfers between devices  38.7 us (27%)
  local copies, waits for them, and re-layouts  6.39 us (4%)
  other arithmetic  2.04 us (1%)
    ppermute x6, waiting for transfers between devices, body(): moving = [lax.ppermute(part, 'ori', along) for part in moving]  25.7 us
    ppermute x6, starting transfers between devices, body(): moving = [lax.ppermute(part, 'ori', along) for part in moving]  24.9 us
    pallas_call x1, Pallas kernels, sum_step(): pl.pallas_call(functools.partial(sum_kernel, bricks, capacity), out_shape...  24.6 us
    ppermute x6, waiting for transfers between devices, add_up(): total += lax.ppermute(part, axis, perm).astype(jnp.float32)  15.9 us
    pallas_call x6, Pallas kernels, score_step(): pl.pallas_call(functools.partial(score_kernel, chips, candidates, first),...  13.6 us
    ppermute x6, starting transfers between devices, add_up(): total += lax.ppermute(part, axis, perm).astype(jnp.float32)  8 us
    ppermute x3, waiting for transfers between devices, body(): lax.ppermute(totals, 'ori', [(i, i ^ 2 * k) for i in range(orient_groups)])  5.53 us
    ppermute x3, starting transfers between devices, body(): lax.ppermute(totals, 'ori', [(i, i ^ 2 * k) for i in range(orient_groups)])  4.8 us
  transfers between devices with their start and end apart: 24, of which 13 were waited for; matrix products, arithmetic and copies ran while one was open for 3% of the time, Pallas kernels for 12%

profile of v8, /device:TPU:0, one launch (start us, length us, event | category | flops | bytes accessed | tf_op | source)
XLA Modules:
  0.0 145.6 jit_solution(3581241890390102825)
XLA Ops:
  1.2 4.6 %collective-permute-start.1 = (bf16[256,2048]{1,0:T(8,128)(2,1)}, bf16[256,2048]{1,0:T(8,128)(2,1)S(1)}, u32[]{:S(2)}, u32[]{:S(2)}) collective-permute-start(bf16[256,2048]{1,0:T(8,128)(2,1)} %refs_0_.1), channel_id=1, source_target_pairs={{0,2},{2,4},{4,6},{3,1},{5,3},{7,5},{8,10},{10,12},{12,14},{11,9},... | collective-permute-start | bytes 3145736 | tf_op jit(solution)/shard_map/score/ppermute | solution.py:436
  5.7 3.5 %collective-permute-start.3 = (bf16[256,2048]{1,0:T(8,128)(2,1)S(1)}, bf16[256,2048]{1,0:T(8,128)(2,1)S(1)}, u32[]{:S(2)}, u32[]{:S(2)}) collective-permute-start(bf16[256,2048]{1,0:T(8,128)(2,1)S(1)} %collective-permute-done.refs_1_), channel_id=1, source_target_pairs={{0,2},{2,4},{4,6},{3,1},{5,3},{7,5},{8,10},{10,12},{12,14},{11,9},... | collective-permute-start | bytes 3145736 | tf_op jit(solution)/shard_map/score/ppermute | solution.py:436
  11.2 4.7 %place_segments.1 = (s32[64,1,256]{2,1,0:T(1,128)S(1)}, s32[4,32,256]{2,1,0:T(8,128)S(1)}) custom-call(s32[64,1,256]{2,1,0:T(1,128)S(1)} %reshape.41.dest_ref, s32[64,1,256]{2,1,0:T(1,128)S(1)} %reshape.43.rows_ref), custom_call_target="tpu_custom_call" | custom-call | flops 1000 | bytes 1000 | tf_op jit(solution)/shard_map/place_segments/place_segments/pallas_call | solution.py:399
  17.9 2.2 %copy-done.1 = bf16[1024,2048]{1,0:T(8,128)(2,1)S(1)} copy-done((bf16[1024,2048]{1,0:T(8,128)(2,1)S(1)}, bf16[1024,2048]{1,0:T(8,128)(2,1)}, u32[]{:S(2)}) %copy-start.1) | copy-done | bytes 4194328
  21.3 3.9 %score_blocks.6 = (f32[1024,128]{1,0:T(8,128)S(1)}, f32[8,1024,256]{2,1,0:T(8,128)S(1)}, bf16[2048,2048]{1,0:T(8,128)(2,1)S(1)}, f32[8,2,256]{2,1,0:T(2,128)S(1)}) custom-call(bf16[256,2048]{1,0:T(8,128)(2,1)S(1)} %copy-done.3, bf16[256,2048]{1,0:T(8,128)(2,1)S(1)} %collective-permute-done.refs_1_, bf16[1024,2048]{1,0:T(8,128)(2,1)S(1)} %copy-done.1), custom_call_target="tpu_custom_call" | custom-call | flops 1000 | bytes 1000 | tf_op jit(solution)/shard_map/score/score_blocks/pallas_call | solution.py:158
  25.2 3.5 %collective-permute-start.2 = (bf16[256,2048]{1,0:T(8,128)(2,1)S(1)}, bf16[256,2048]{1,0:T(8,128)(2,1)S(1)}, u32[]{:S(2)}, u32[]{:S(2)}) collective-permute-start(bf16[256,2048]{1,0:T(8,128)(2,1)S(1)} %collective-permute-done.1.refs_0_), channel_id=1, source_target_pairs={{0,2},{2,4},{4,6},{3,1},{5,3},{7,5},{8,10},{10,12},{12,14},{11,9},... | collective-permute-start | bytes 3145736 | tf_op jit(solution)/shard_map/score/ppermute | solution.py:436
  29.4 4.4 %collective-permute-start.5 = (bf16[256,2048]{1,0:T(8,128)(2,1)S(1)}, bf16[256,2048]{1,0:T(8,128)(2,1)S(1)}, u32[]{:S(2)}, u32[]{:S(2)}) collective-permute-start(bf16[256,2048]{1,0:T(8,128)(2,1)S(1)} %collective-permute-done.3.refs_0_), channel_id=1, source_target_pairs={{0,2},{2,4},{4,6},{3,1},{5,3},{7,5},{8,10},{10,12},{12,14},{11,9},... | collective-permute-start | bytes 3145736 | tf_op jit(solution)/shard_map/score/ppermute | solution.py:436
  33.9 7.0 %collective-permute-done.2.refs_0_ = bf16[256,2048]{1,0:T(8,128)(2,1)S(1)} collective-permute-done((bf16[256,2048]{1,0:T(8,128)(2,1)S(1)}, bf16[256,2048]{1,0:T(8,128)(2,1)S(1)}, u32[]{:S(2)}, u32[]{:S(2)}) %collective-permute-start.2) | collective-permute-done | bytes 1048608 | tf_op jit(solution)/shard_map/score/ppermute | solution.py:436
  41.0 4.4 %collective-permute-start.4 = (bf16[256,2048]{1,0:T(8,128)(2,1)S(1)}, bf16[256,2048]{1,0:T(8,128)(2,1)S(1)}, u32[]{:S(2)}, u32[]{:S(2)}) collective-permute-start(bf16[256,2048]{1,0:T(8,128)(2,1)S(1)} %collective-permute-done.2.refs_0_), channel_id=1, source_target_pairs={{0,2},{2,4},{4,6},{3,1},{5,3},{7,5},{8,10},{10,12},{12,14},{11,9},... | collective-permute-start | bytes 3145736 | tf_op jit(solution)/shard_map/score/ppermute | solution.py:436
  47.1 5.1 %collective-permute-done.5.refs_0_ = bf16[256,2048]{1,0:T(8,128)(2,1)S(1)} collective-permute-done((bf16[256,2048]{1,0:T(8,128)(2,1)S(1)}, bf16[256,2048]{1,0:T(8,128)(2,1)S(1)}, u32[]{:S(2)}, u32[]{:S(2)}) %collective-permute-start.5) | collective-permute-done | bytes 1048608 | tf_op jit(solution)/shard_map/score/ppermute | solution.py:436
  52.2 4.4 %collective-permute-start.9 = (bf16[256,2048]{1,0:T(8,128)(2,1)S(1)}, bf16[256,2048]{1,0:T(8,128)(2,1)S(1)}, u32[]{:S(2)}, u32[]{:S(2)}) collective-permute-start(bf16[256,2048]{1,0:T(8,128)(2,1)S(1)} %collective-permute-done.5.refs_0_), channel_id=1, source_target_pairs={{0,2},{2,4},{4,6},{3,1},{5,3},{7,5},{8,10},{10,12},{12,14},{11,9},... | collective-permute-start | bytes 3145736 | tf_op jit(solution)/shard_map/score/ppermute | solution.py:436
  58.3 5.2 %collective-permute-done.4.refs_0_ = bf16[256,2048]{1,0:T(8,128)(2,1)S(1)} collective-permute-done((bf16[256,2048]{1,0:T(8,128)(2,1)S(1)}, bf16[256,2048]{1,0:T(8,128)(2,1)S(1)}, u32[]{:S(2)}, u32[]{:S(2)}) %collective-permute-start.4) | collective-permute-done | bytes 1048608 | tf_op jit(solution)/shard_map/score/ppermute | solution.py:436
  63.5 1.8 %score_blocks.9 = (f32[8,1024,256]{2,1,0:T(8,128)S(1)}, bf16[2048,2048]{1,0:T(8,128)(2,1)S(1)}, f32[8,2,256]{2,1,0:T(2,128)S(1)}) custom-call(bf16[256,2048]{1,0:T(8,128)(2,1)S(1)} %collective-permute-done.2.refs_0_, bf16[256,2048]{1,0:T(8,128)(2,1)S(1)} %collective-permute-done.11.refs_1_, ...), custom_call_target="tpu_custom_call", output_to_operand_aliasing={{0}: (4, {}), {1}: (5, {}), {2}: (6, {})} | custom-call | flops 1000 | bytes 1000 | tf_op jit(solution)/shard_map/score/score_blocks/pallas_call | solution.py:158
  66.9 7.8 %collective-permute-done.9.refs_2_ = bf16[256,2048]{1,0:T(8,128)(2,1)S(1)} collective-permute-done((bf16[256,2048]{1,0:T(8,128)(2,1)S(1)}, bf16[256,2048]{1,0:T(8,128)(2,1)S(1)}, u32[]{:S(2)}, u32[]{:S(2)}) %collective-permute-start.9) | collective-permute-done | bytes 1048608 | tf_op jit(solution)/shard_map/score/ppermute | solution.py:436
  74.7 2.7 %collective-permute-done.12.refs_3_ = bf16[256,2048]{1,0:T(8,128)(2,1)S(1)} collective-permute-done((bf16[256,2048]{1,0:T(8,128)(2,1)S(1)}, bf16[256,2048]{1,0:T(8,128)(2,1)S(1)}, u32[]{:S(2)}, u32[]{:S(2)}) %collective-permute-start.12) | collective-permute-done | bytes 1048608 | tf_op jit(solution)/shard_map/score/ppermute | solution.py:428
  77.3 3.2 %score_blocks.11 = (f32[8,1024,256]{2,1,0:T(8,128)S(1)}, bf16[2048,2048]{1,0:T(8,128)(2,1)S(1)}, f32[8,2,256]{2,1,0:T(2,128)S(1)}) custom-call(bf16[256,2048]{1,0:T(8,128)(2,1)S(1)} %collective-permute-done.4.refs_0_, bf16[256,2048]{1,0:T(8,128)(2,1)S(1)} %collective-permute-done.8.refs_1_, ...), custom_call_target="tpu_custom_call", output_to_operand_aliasing={{0}: (6, {}), {1}: (7, {}), {2}: (8, {})} | custom-call | flops 1000 | bytes 1000 | tf_op jit(solution)/shard_map/score/score_blocks/pallas_call | solution.py:158
  81.9 4.7 %collective-permute-start.15 = (f32[8,2,256]{2,1,0:T(2,128)S(1)}, f32[8,2,256]{2,1,0:T(2,128)S(1)}, u32[]{:S(2)}, u32[]{:S(2)}) collective-permute-start(f32[8,2,256]{2,1,0:T(2,128)S(1)} %merge_totals.2.refs_0_), channel_id=1, source_target_pairs={{0,4},{1,5},{2,6},{3,7},{4,0},{5,1},{6,2},{7,3},{8,12},{9,13},{10,... | collective-permute-start | bytes 49160 | tf_op jit(solution)/shard_map/softmax_total/ppermute | solution.py:456
  88.3 3.8 %collective-permute-done.16.refs_3_ = f32[8,2,256]{2,1,0:T(2,128)S(1)} collective-permute-done((f32[8,2,256]{2,1,0:T(2,128)S(1)}, f32[8,2,256]{2,1,0:T(2,128)S(1)}, u32[]{:S(2)}, u32[]{:S(2)}) %collective-permute-start.16) | collective-permute-done | bytes 16416 | tf_op jit(solution)/shard_map/softmax_total/ppermute | solution.py:456
  92.2 24.6 %sum_and_grid.1 = (bf16[16,272,128]{2,1,0:T(8,128)(2,1)S(1)}, bf16[16,1024,128]{2,1,0:T(8,128)(2,1)S(1)}, f32[64,256]{1,0:T(8,128)S(1)}) custom-call(s32[18432]{0:T(1024)S(1)} %concatenate.3.slot_ref, f32[8,1024,256]{2,1,0:T(8,128)S(1)} %get-tuple-element.111.p_ref, f32[8,2,256]{2,1,0:T(2,128)S(1)} %get-tuple-element.112.refs_0_.stats_ref, ...), custom_call_target="tpu_custom_call" | custom-call | flops 8589934592 | bytes 25165824 | tf_op jit(solution)/shard_map/sum_and_grid/sum_and_grid/pallas_call | solution.py:354
  116.9 2.3 %grid_own_bricks.1 = f32[16,272,128]{2,1,0:T(8,128)S(1)} custom-call(bf16[16,1024,128]{2,1,0:T(8,128)(2,1)S(1)} %get-tuple-element.117.slots, f32[64,256]{1,0:T(8,128)S(1)} %get-tuple-element.118.volume, s32[32,1,1024]{2,1,0:T(1,128)S(1)} %reshape.46.map_ref), custom_call_target="tpu_custom_call" | custom-call | flops 1000 | bytes 1000 | tf_op jit(solution)/shard_map/brick_sums/grid_own_bricks/pallas_call | solution.py:337
  123.6 6.0 %collective-permute-done.18 = bf16[4,272,128]{2,1,0:T(8,128)(2,1)S(1)} collective-permute-done((bf16[4,272,128]{2,1,0:T(8,128)(2,1)S(1)}, bf16[4,272,128]{2,1,0:T(8,128)(2,1)S(1)}, u32[]{:S(2)}, u32[]{:S(2)}) %collective-permute-start.18) | collective-permute-done | bytes 278560 | tf_op jit(solution)/shard_map/brick_sums/ppermute | solution.py:474
  129.6 6.4 %collective-permute-done.19 = bf16[4,272,128]{2,1,0:T(8,128)(2,1)S(1)} collective-permute-done((bf16[4,272,128]{2,1,0:T(8,128)(2,1)S(1)}, bf16[4,272,128]{2,1,0:T(8,128)(2,1)S(1)}, u32[]{:S(2)}, u32[]{:S(2)}) %collective-permute-start.19) | collective-permute-done | bytes 278560 | tf_op jit(solution)/shard_map/brick_sums/ppermute | solution.py:474
  137.0 3.6 %collective-permute-start.23 = (bf16[272,128]{1,0:T(8,128)(2,1)S(1)}, bf16[272,128]{1,0:T(8,128)(2,1)S(1)}, u32[]{:S(2)}, u32[]{:S(2)}) collective-permute-start(bf16[272,128]{1,0:T(8,128)(2,1)S(1)} %get-tuple-element.128), channel_id=1, source_target_pairs={{0,6},{1,7},{2,4},{3,5},{4,2},{5,3},{6,0},{7,1},{8,14},{9,15},{10,... | collective-permute-start | bytes 208904 | tf_op jit(solution)/shard_map/brick_sums/ppermute | solution.py:474
  140.6 3.5 %collective-permute-done.22 = bf16[272,128]{1,0:T(8,128)(2,1)S(1)} collective-permute-done((bf16[272,128]{1,0:T(8,128)(2,1)S(1)}, bf16[272,128]{1,0:T(8,128)(2,1)S(1)}, u32[]{:S(2)}, u32[]{:S(2)}) %collective-permute-start.22) | collective-permute-done | bytes 69664 | tf_op jit(solution)/shard_map/brick_sums/ppermute | solution.py:474
  (61 shorter events, 21.2 us)
Async XLA Ops:
  0.6 5.1 %collective-permute-start = (bf16[256,2048]{1,0:T(8,128)(2,1)}, bf16[256,2048]{1,0:T(8,128)(2,1)S(1)}, u32[]{:S(2)}, u32[]{:S(2)}) collective-permute-start(bf16[256,2048]{1,0:T(8,128)(2,1)} %refs_0_.1), channel_id=1, source_target_pairs={{0,1},{1,0},{2,3},{3,2},{4,5},{5,4},{6,7},{7,6},{8,9},{9,8},{10,11... | collective-permute-start | bytes 3145736 | tf_op jit(solution)/shard_map/score/ppermute | solution.py:419
  1.2 24.1 %collective-permute-start.1 = (bf16[256,2048]{1,0:T(8,128)(2,1)}, bf16[256,2048]{1,0:T(8,128)(2,1)S(1)}, u32[]{:S(2)}, u32[]{:S(2)}) collective-permute-start(bf16[256,2048]{1,0:T(8,128)(2,1)} %refs_0_.1), channel_id=1, source_target_pairs={{0,2},{2,4},{4,6},{3,1},{5,3},{7,5},{8,10},{10,12},{12,14},{11,9},... | collective-permute-start | bytes 3145736 | tf_op jit(solution)/shard_map/score/ppermute | solution.py:436
  5.7 23.7 %collective-permute-start.3 = (bf16[256,2048]{1,0:T(8,128)(2,1)S(1)}, bf16[256,2048]{1,0:T(8,128)(2,1)S(1)}, u32[]{:S(2)}, u32[]{:S(2)}) collective-permute-start(bf16[256,2048]{1,0:T(8,128)(2,1)S(1)} %collective-permute-done.refs_1_), channel_id=1, source_target_pairs={{0,2},{2,4},{4,6},{3,1},{5,3},{7,5},{8,10},{10,12},{12,14},{11,9},... | collective-permute-start | bytes 3145736 | tf_op jit(solution)/shard_map/score/ppermute | solution.py:436
  25.2 15.7 %collective-permute-start.2 = (bf16[256,2048]{1,0:T(8,128)(2,1)S(1)}, bf16[256,2048]{1,0:T(8,128)(2,1)S(1)}, u32[]{:S(2)}, u32[]{:S(2)}) collective-permute-start(bf16[256,2048]{1,0:T(8,128)(2,1)S(1)} %collective-permute-done.1.refs_0_), channel_id=1, source_target_pairs={{0,2},{2,4},{4,6},{3,1},{5,3},{7,5},{8,10},{10,12},{12,14},{11,9},... | collective-permute-start | bytes 3145736 | tf_op jit(solution)/shard_map/score/ppermute | solution.py:436
  28.7 16.8 %collective-permute-start.6 = (bf16[256,2048]{1,0:T(8,128)(2,1)S(1)}, bf16[256,2048]{1,0:T(8,128)(2,1)S(1)}, u32[]{:S(2)}, u32[]{:S(2)}) collective-permute-start(bf16[256,2048]{1,0:T(8,128)(2,1)S(1)} %collective-permute-done.1.refs_0_), channel_id=1, source_target_pairs={{0,1},{1,0},{2,3},{3,2},{4,5},{5,4},{6,7},{7,6},{8,9},{9,8},{10,11... | collective-permute-start | bytes 3145736 | tf_op jit(solution)/shard_map/score/ppermute | solution.py:428
  29.4 22.8 %collective-permute-start.5 = (bf16[256,2048]{1,0:T(8,128)(2,1)S(1)}, bf16[256,2048]{1,0:T(8,128)(2,1)S(1)}, u32[]{:S(2)}, u32[]{:S(2)}) collective-permute-start(bf16[256,2048]{1,0:T(8,128)(2,1)S(1)} %collective-permute-done.3.refs_0_), channel_id=1, source_target_pairs={{0,2},{2,4},{4,6},{3,1},{5,3},{7,5},{8,10},{10,12},{12,14},{11,9},... | collective-permute-start | bytes 3145736 | tf_op jit(solution)/shard_map/score/ppermute | solution.py:436
  33.9 22.8 %collective-permute-start.7 = (bf16[256,2048]{1,0:T(8,128)(2,1)S(1)}, bf16[256,2048]{1,0:T(8,128)(2,1)S(1)}, u32[]{:S(2)}, u32[]{:S(2)}) collective-permute-start(bf16[256,2048]{1,0:T(8,128)(2,1)S(1)} %collective-permute-done.3.refs_0_), channel_id=1, source_target_pairs={{0,1},{1,0},{2,3},{3,2},{4,5},{5,4},{6,7},{7,6},{8,9},{9,8},{10,11... | collective-permute-start | bytes 3145736 | tf_op jit(solution)/shard_map/score/ppermute | solution.py:428
  41.0 22.5 %collective-permute-start.4 = (bf16[256,2048]{1,0:T(8,128)(2,1)S(1)}, bf16[256,2048]{1,0:T(8,128)(2,1)S(1)}, u32[]{:S(2)}, u32[]{:S(2)}) collective-permute-start(bf16[256,2048]{1,0:T(8,128)(2,1)S(1)} %collective-permute-done.2.refs_0_), channel_id=1, source_target_pairs={{0,2},{2,4},{4,6},{3,1},{5,3},{7,5},{8,10},{10,12},{12,14},{11,9},... | collective-permute-start | bytes 3145736 | tf_op jit(solution)/shard_map/score/ppermute | solution.py:436
  45.4 18.0 %collective-permute-start.11 = (bf16[256,2048]{1,0:T(8,128)(2,1)S(1)}, bf16[256,2048]{1,0:T(8,128)(2,1)S(1)}, u32[]{:S(2)}, u32[]{:S(2)}) collective-permute-start(bf16[256,2048]{1,0:T(8,128)(2,1)S(1)} %collective-permute-done.2.refs_0_), channel_id=1, source_target_pairs={{0,1},{1,0},{2,3},{3,2},{4,5},{5,4},{6,7},{7,6},{8,9},{9,8},{10,11... | collective-permute-start | bytes 3145736 | tf_op jit(solution)/shard_map/score/ppermute | solution.py:428
  52.2 13.0 %collective-permute-start.10 = (bf16[256,2048]{1,0:T(8,128)(2,1)S(1)}, bf16[256,2048]{1,0:T(8,128)(2,1)S(1)}, u32[]{:S(2)}, u32[]{:S(2)}) collective-permute-start(bf16[256,2048]{1,0:T(8,128)(2,1)S(1)} %collective-permute-done.5.refs_0_), channel_id=1, source_target_pairs={{0,1},{1,0},{2,3},{3,2},{4,5},{5,4},{6,7},{7,6},{8,9},{9,8},{10,11... | collective-permute-start | bytes 3145736 | tf_op jit(solution)/shard_map/score/ppermute | solution.py:428
  52.2 22.5 %collective-permute-start.9 = (bf16[256,2048]{1,0:T(8,128)(2,1)S(1)}, bf16[256,2048]{1,0:T(8,128)(2,1)S(1)}, u32[]{:S(2)}, u32[]{:S(2)}) collective-permute-start(bf16[256,2048]{1,0:T(8,128)(2,1)S(1)} %collective-permute-done.5.refs_0_), channel_id=1, source_target_pairs={{0,2},{2,4},{4,6},{3,1},{5,3},{7,5},{8,10},{10,12},{12,14},{11,9},... | collective-permute-start | bytes 3145736 | tf_op jit(solution)/shard_map/score/ppermute | solution.py:436
  63.4 11.2 %collective-permute-start.8 = (bf16[256,2048]{1,0:T(8,128)(2,1)S(1)}, bf16[256,2048]{1,0:T(8,128)(2,1)S(1)}, u32[]{:S(2)}, u32[]{:S(2)}) collective-permute-start(bf16[256,2048]{1,0:T(8,128)(2,1)S(1)} %collective-permute-done.4.refs_0_), channel_id=1, source_target_pairs={{0,1},{1,0},{2,3},{3,2},{4,5},{5,4},{6,7},{7,6},{8,9},{9,8},{10,11... | collective-permute-start | bytes 3145736 | tf_op jit(solution)/shard_map/score/ppermute | solution.py:428
  74.7 2.7 %collective-permute-start.12 = (bf16[256,2048]{1,0:T(8,128)(2,1)S(1)}, bf16[256,2048]{1,0:T(8,128)(2,1)S(1)}, u32[]{:S(2)}, u32[]{:S(2)}) collective-permute-start(bf16[256,2048]{1,0:T(8,128)(2,1)S(1)} %collective-permute-done.9.refs_2_), channel_id=1, source_target_pairs={{0,1},{1,0},{2,3},{3,2},{4,5},{5,4},{6,7},{7,6},{8,9},{9,8},{10,11... | collective-permute-start | bytes 3145736 | tf_op jit(solution)/shard_map/score/ppermute | solution.py:428
  80.5 1.2 collective-permute-start.13
  81.8 4.8 %collective-permute-start.14 = (f32[8,2,256]{2,1,0:T(2,128)S(1)}, f32[8,2,256]{2,1,0:T(2,128)S(1)}, u32[]{:S(2)}, u32[]{:S(2)}) collective-permute-start(f32[8,2,256]{2,1,0:T(2,128)S(1)} %merge_totals.2.refs_0_), channel_id=1, source_target_pairs={{0,2},{1,3},{2,0},{3,1},{4,6},{5,7},{6,4},{7,5},{8,10},{9,11},{10,... | collective-permute-start | bytes 49160 | tf_op jit(solution)/shard_map/softmax_total/ppermute | solution.py:456
  81.9 6.4 %collective-permute-start.15 = (f32[8,2,256]{2,1,0:T(2,128)S(1)}, f32[8,2,256]{2,1,0:T(2,128)S(1)}, u32[]{:S(2)}, u32[]{:S(2)}) collective-permute-start(f32[8,2,256]{2,1,0:T(2,128)S(1)} %merge_totals.2.refs_0_), channel_id=1, source_target_pairs={{0,4},{1,5},{2,6},{3,7},{4,0},{5,1},{6,2},{7,3},{8,12},{9,13},{10,... | collective-permute-start | bytes 49160 | tf_op jit(solution)/shard_map/softmax_total/ppermute | solution.py:456
  86.6 5.5 %collective-permute-start.16 = (f32[8,2,256]{2,1,0:T(2,128)S(1)}, f32[8,2,256]{2,1,0:T(2,128)S(1)}, u32[]{:S(2)}, u32[]{:S(2)}) collective-permute-start(f32[8,2,256]{2,1,0:T(2,128)S(1)} %merge_totals.2.refs_0_), channel_id=1, source_target_pairs={{0,6},{1,7},{2,4},{3,5},{4,2},{5,3},{6,0},{7,1},{8,14},{9,15},{10,... | collective-permute-start | bytes 49160 | tf_op jit(solution)/shard_map/softmax_total/ppermute | solution.py:456
  116.9 2.8 %collective-permute-start.17 = (bf16[16,272,128]{2,1,0:T(8,128)(2,1)S(1)}, bf16[16,272,128]{2,1,0:T(8,128)(2,1)S(1)}, u32[]{:S(2)}, u32[]{:S(2)}) collective-permute-start(bf16[16,272,128]{2,1,0:T(8,128)(2,1)S(1)} %get-tuple-element.119), channel_id=1, source_target_pairs={{0,1},{1,0},{2,3},{3,2},{4,5},{5,4},{6,7},{7,6},{8,9},{9,8},{10,11... | collective-permute-start | bytes 3342344 | tf_op jit(solution)/shard_map/brick_sums/ppermute | solution.py:477
  120.0 9.6 %collective-permute-start.18 = (bf16[4,272,128]{2,1,0:T(8,128)(2,1)S(1)}, bf16[4,272,128]{2,1,0:T(8,128)(2,1)S(1)}, u32[]{:S(2)}, u32[]{:S(2)}) collective-permute-start(bf16[4,272,128]{2,1,0:T(8,128)(2,1)S(1)} %get-tuple-element.124), channel_id=1, source_target_pairs={{0,8},{8,0},{16,24},{24,16},{1,9},{9,1},{17,25},{25,17},{2,10},{10... | collective-permute-start | bytes 835592 | tf_op jit(solution)/shard_map/brick_sums/ppermute | solution.py:474
  121.6 14.4 %collective-permute-start.19 = (bf16[4,272,128]{2,1,0:T(8,128)(2,1)S(1)}, bf16[4,272,128]{2,1,0:T(8,128)(2,1)S(1)}, u32[]{:S(2)}, u32[]{:S(2)}) collective-permute-start(bf16[4,272,128]{2,1,0:T(8,128)(2,1)S(1)} %get-tuple-element.126), channel_id=1, source_target_pairs={{0,16},{8,24},{16,0},{24,8},{1,17},{9,25},{17,1},{25,9},{2,18},{10... | collective-permute-start | bytes 835592 | tf_op jit(solution)/shard_map/brick_sums/ppermute | solution.py:474
  123.1 12.9 %collective-permute-start.20 = (bf16[4,272,128]{2,1,0:T(8,128)(2,1)S(1)}, bf16[4,272,128]{2,1,0:T(8,128)(2,1)S(1)}, u32[]{:S(2)}, u32[]{:S(2)}) collective-permute-start(bf16[4,272,128]{2,1,0:T(8,128)(2,1)S(1)} %get-tuple-element.125), channel_id=1, source_target_pairs={{0,24},{8,16},{16,8},{24,0},{1,25},{9,17},{17,9},{25,1},{2,26},{10... | collective-permute-start | bytes 835592 | tf_op jit(solution)/shard_map/brick_sums/ppermute | solution.py:474
  136.2 4.5 %collective-permute-start.21 = (bf16[272,128]{1,0:T(8,128)(2,1)S(1)}, bf16[272,128]{1,0:T(8,128)(2,1)S(1)}, u32[]{:S(2)}, u32[]{:S(2)}) collective-permute-start(bf16[272,128]{1,0:T(8,128)(2,1)S(1)} %get-tuple-element.127), channel_id=1, source_target_pairs={{0,2},{1,3},{2,0},{3,1},{4,6},{5,7},{6,4},{7,5},{8,10},{9,11},{10,... | collective-permute-start | bytes 208904 | tf_op jit(solution)/shard_map/brick_sums/ppermute | solution.py:474
  136.2 7.9 %collective-permute-start.22 = (bf16[272,128]{1,0:T(8,128)(2,1)S(1)}, bf16[272,128]{1,0:T(8,128)(2,1)S(1)}, u32[]{:S(2)}, u32[]{:S(2)}) collective-permute-start(bf16[272,128]{1,0:T(8,128)(2,1)S(1)} %get-tuple-element.129), channel_id=1, source_target_pairs={{0,4},{1,5},{2,6},{3,7},{4,0},{5,1},{6,2},{7,3},{8,12},{9,13},{10,... | collective-permute-start | bytes 208904 | tf_op jit(solution)/shard_map/brick_sums/ppermute | solution.py:474
  137.0 7.1 %collective-permute-start.23 = (bf16[272,128]{1,0:T(8,128)(2,1)S(1)}, bf16[272,128]{1,0:T(8,128)(2,1)S(1)}, u32[]{:S(2)}, u32[]{:S(2)}) collective-permute-start(bf16[272,128]{1,0:T(8,128)(2,1)S(1)} %get-tuple-element.128), channel_id=1, source_target_pairs={{0,6},{1,7},{2,4},{3,5},{4,2},{5,3},{6,0},{7,1},{8,14},{9,15},{10,... | collective-permute-start | bytes 208904 | tf_op jit(solution)/shard_map/brick_sums/ppermute | solution.py:474
  (4 other events, 171.7 us)
